TPU v7x, 256 devices: a whole 4x4x8 slice. The times are simulated.
256 devices in a mesh: tm: 64 (over z, x, core), tp: 4 (over y).
Axes of the slice: x: 4, y: 4, z: 8, core: 2. Of those that a mesh axis runs over, the one named last changes fastest.
Arguments:
- tokens: bfloat16 [24576, 1536], P('tm', 'tp')
- ln_gain: float32 [1536], replicated, may hold values from 0.1 to 1.9
- w_qkv: bfloat16 [1536, 3, 1536], P(None, None, 'tp')
- w_out: bfloat16 [1536, 1536], P(None, 'tp'), may hold values from -0.15625 to 0.15625
- frame_mask: int32 [24576], P('tm'), may hold values from 0 to 1, as said below
- out_grad: bfloat16 [24576, 1536], P('tm', 'tp')
Outputs:
- layer_out: bfloat16 [24576, 1536], P('tm', 'tp')
- tokens_grad: bfloat16 [24576, 1536], P('tm', 'tp')
- gain_grad: float32 [1536], replicated
- qkv_grad: float32 [1536, 3, 1536], P('tm', None, 'tp')
- out_weight_grad: float32 [1536, 1536], P('tm', 'tp')
Inputs may be any that keep to these rules, and one draw needn't show every extreme that they name: `frame_mask`: each frame is 0 with probability one quarter, independently, and every frame from the recording's valid length on is 0; the valid length lies between 24320 and 24575.
All inputs are finite; a program needn't handle non-finite values.
Results may differ from a plain program's by a relative error of at most 0.014.
Values may be sent and summed in bfloat16 or wider, within the bound.
No kernel may reach another device: no remote copies, remote signals or barrier semaphores. Data moves between devices by JAX's collectives and lax.ppermute only.
A program may use at most 128 MiB of HBM per device.

v0:
```python
import jax
import jax.numpy as jnp
from jax import lax
from jax.experimental import pallas as pl
from jax.experimental.pallas import tpu as pltpu
from jax.sharding import Mesh, PartitionSpec as P

HEAD = 64
WINDOW = 128
EPSILON = 1e-05
LANES = 128
TM = ("z", "x", "core")
F32 = jnp.float32
BF16 = jnp.bfloat16


def shifted(value, axis, by):
    size = lax.axis_size(axis)
    return lax.ppermute(value, axis, [(i, (i + by) % size) for i in range(size)])


def swapped(value, axis, bit):
    size = lax.axis_size(axis)
    return lax.ppermute(value, axis, [(i, i ^ bit) for i in range(size)])


def to_next(value):
    size = lax.axis_size(TM)
    return lax.ppermute(value, TM, [(i, i + 1) for i in range(size - 1)])


def to_previous(value):
    size = lax.axis_size(TM)
    return lax.ppermute(value, TM, [(i + 1, i) for i in range(size - 1)])


def dot_nn(a, b):
    return lax.dot_general(a, b, (((1,), (0,)), ((), ())), preferred_element_type=F32)


def dot_nt(a, b):
    return lax.dot_general(a, b, (((1,), (1,)), ((), ())), preferred_element_type=F32)


def dot_tn(a, b):
    return lax.dot_general(a, b, (((0,), (0,)), ((), ())), preferred_element_type=F32)


def call(body, outs, args, smem=(), scratch=(), flops=0, moved=0, vmem=24):
    in_specs = [
        pl.BlockSpec(memory_space=pltpu.SMEM if k in smem else pltpu.VMEM) for k in range(len(args))
    ]
    return pl.pallas_call(
        body,
        out_shape=[jax.ShapeDtypeStruct(s, d) for s, d in outs],
        in_specs=in_specs,
        out_specs=[pl.BlockSpec(memory_space=pltpu.VMEM)] * len(outs),
        scratch_shapes=list(scratch),
        cost_estimate=pl.CostEstimate(flops=flops, bytes_accessed=moved, transcendentals=0),
        compiler_params=pltpu.CompilerParams(vmem_limit_bytes=vmem * 2**20),
    )(*args)


def block_of(place, step):
    return lax.rem(place[3] + step, 4)


def project_kernel(
    place, t0, t1, t2, t3, gain, weights, mask, normed, q_out, k_out, v_out, kv_low, kv_high, stats
):
    parts = (t0, t1, t2, t3)
    width = 4 * t0.shape[1]
    wide = [t[...].astype(F32) for t in parts]
    average = sum(jnp.sum(t, axis=1, keepdims=True) for t in wide) / width
    centered = [t - average for t in wide]
    variance = sum(jnp.sum(t * t, axis=1, keepdims=True) for t in centered) / width
    inverse_std = lax.rsqrt(variance + EPSILON)
    lane = lax.broadcasted_iota(jnp.int32, stats.shape, 1)
    stats[...] = jnp.where(lane == 0, average, inverse_std)
    for step in range(4):
        block = block_of(place, step)
        normed[block] = (centered[step] * inverse_std * gain[block]).astype(BF16)
    rows = t0.shape[1]
    for kind, out in enumerate((q_out, k_out, v_out)):
        total = None
        for block in range(4):
            term = dot_nn(normed[block], weights[kind, rows * block : rows * (block + 1), :])
            total = term if total is None else total + term
        out[...] = total.astype(BF16)
        if kind > 0:
            columns = slice((kind - 1) * rows, kind * rows)
            kv_low[:WINDOW, columns] = out[:WINDOW, :]
            kv_high[:WINDOW, columns] = out[out.shape[0] - WINDOW :, :]
    frames = t0.shape[0]
    for out, start in ((kv_low, 0), (kv_high, frames - WINDOW)):
        row = mask[:, start : start + WINDOW].astype(F32)
        out[WINDOW:, :LANES] = jnp.broadcast_to(row, (16, LANES)).astype(BF16)


def attention_kernel(
    place, mask, q_in, k_in, v_in, kv_prev, kv_next, g0, g1, g2, g3, w_out,
    attended, q_grad, kv_grad, kv_low, kv_high, gated,
    k_ext, v_ext, k_cross, v_cross, upstream, cap, dk_ext, dv_ext,
):
    frames, width = q_in.shape
    span = 3 * WINDOW
    blocks = frames // WINDOW
    turned = []
    for block in range(blocks + 2):
        if block == 0:
            row = kv_prev[WINDOW:, :LANES].astype(F32)[:1]
        elif block > blocks:
            row = kv_next[WINDOW:, :LANES].astype(F32)[:1]
        else:
            row = mask[:, (block - 1) * WINDOW : block * WINDOW].astype(F32)
        turned.append(jnp.transpose(jnp.broadcast_to(row, (WINDOW, WINDOW))))
    key_at = lax.broadcasted_iota(jnp.int32, (WINDOW, WINDOW), 0)
    query_at = lax.broadcasted_iota(jnp.int32, (WINDOW, WINDOW), 1)
    high, low = 3.0e38, -1e30
    for block in range(blocks):
        before = (key_at >= query_at) & (turned[block] > 0)
        inside = (key_at == query_at) | (turned[block + 1] > 0)
        after = (key_at <= query_at) & (turned[block + 2] > 0)
        for part, allowed in enumerate((before, inside, after)):
            cap[block, part * WINDOW : (part + 1) * WINDOW, :] = jnp.where(allowed, high, low)

    total = None
    for step, ref in enumerate((g0, g1, g2, g3)):
        block = block_of(place, step)
        for part in range(blocks):
            rows = slice(part * WINDOW, (part + 1) * WINDOW)
            keep = turned[part + 1]
            keep = jnp.concatenate([keep] * (width // WINDOW), axis=1)
            gated[block, rows, :] = (ref[rows, :].astype(F32) * keep).astype(BF16)
    for block in range(4):
        term = dot_nn(gated[block], w_out[width * block : width * (block + 1), :])
        total = term if total is None else total + term
    upstream[...] = total.astype(BF16)

    for ext, own, at in ((k_ext, k_in, 0), (v_ext, v_in, width)):
        ext[:WINDOW, :] = kv_prev[:WINDOW, at : at + width]
        ext[WINDOW : WINDOW + frames, :] = own[...]
        ext[WINDOW + frames :, :] = kv_next[:WINDOW, at : at + width]
    dk_ext[...] = jnp.zeros_like(dk_ext)
    dv_ext[...] = jnp.zeros_like(dv_ext)
    scaling = HEAD ** (-0.5)
    first = lax.broadcasted_iota(jnp.int32, (WINDOW, LANES), 1) < HEAD
    for pair in range(width // LANES):
        lanes = slice(pair * LANES, (pair + 1) * LANES)
        k_cross[...] = jnp.transpose(k_ext[:, lanes].astype(F32) * scaling).astype(BF16)
        v_cross[...] = jnp.transpose(v_ext[:, lanes].astype(F32)).astype(BF16)
        for block in range(blocks):
            rows = slice(block * WINDOW, (block + 1) * WINDOW)
            keys = slice(block * WINDOW, block * WINDOW + span)
            query = q_in[rows, lanes] * jnp.asarray(scaling, BF16)
            zero = jnp.zeros_like(query)
            query = jnp.concatenate(
                [jnp.where(first, query, zero), jnp.where(first, zero, query)], axis=0
            )
            grad = upstream[rows, lanes]
            grad = jnp.concatenate(
                [jnp.where(first, grad, zero), jnp.where(first, zero, grad)], axis=0
            )
            bound = cap[block]
            bound = jnp.concatenate([bound, bound], axis=1)
            scores = jnp.minimum(dot_nt(k_ext[keys, lanes], query), bound)
            largest = jnp.max(scores, axis=0, keepdims=True)
            exponent = jnp.exp(scores - largest)
            probability = exponent * (1.0 / jnp.sum(exponent, axis=0, keepdims=True))
            probability_low = probability.astype(BF16)
            probability_grad = dot_nt(v_ext[keys, lanes], grad)
            row_dots = jnp.sum(probability * probability_grad, axis=0, keepdims=True)
            score_grad = (probability * (probability_grad - row_dots)).astype(BF16)
            dv_ext[keys, lanes] += dot_nn(probability_low, grad)
            dk_ext[keys, lanes] += dot_nn(score_grad, query)
            for cross, factor, out in (
                (v_cross, probability_low, attended),
                (k_cross, score_grad, q_grad),
            ):
                both = dot_nn(cross[:, keys], factor)
                both = jnp.concatenate([both[:HEAD, :WINDOW], both[HEAD:, WINDOW:]], axis=0)
                out[rows, lanes] = jnp.transpose(both).astype(BF16)
    for ext, at in ((dk_ext, 0), (dv_ext, width)):
        columns = slice(at, at + width)
        kv_low[:, columns] = ext[:WINDOW, :].astype(BF16)
        kv_grad[:, columns] = ext[WINDOW : WINDOW + frames, :]
        kv_high[:, columns] = ext[WINDOW + frames :, :].astype(BF16)


def split_rows(place, block, held, send, keep):
    core = place[2]
    for group in range(8):
        at = group % 4 * 8 + 2 * block + group // 4
        for out, whose in ((send, 1 - core), (keep, core)):
            start = pl.multiple_of(48 * group + 24 * whose, 8)
            both = jnp.concatenate([held[0, pl.ds(start, 24), :], held[1, pl.ds(start, 24), :]], 0)
            out[at] = both.astype(BF16)


def folded(value):
    return value[:, :LANES] + value[:, LANES : 2 * LANES] + value[:, 2 * LANES :]


def in_two(value):
    head = value.astype(BF16).astype(F32)
    return jnp.concatenate([head, value - head], axis=0).astype(BF16)


def from_two(value):
    wide = value.astype(F32)
    return wide[:8] + wide[8:16]


def first_weights_kernel(
    place, gated, attended, q_grad, normed, weights, send, keep, gain_sums, held
):
    width = attended.shape[1]
    for block in range(4):
        rows = slice(width * block, width * (block + 1))
        held[0] = dot_tn(gated[block], attended[...])
        held[1] = dot_tn(normed[block], q_grad[...])
        gain_sums[block] = folded(held[1] * weights[0, rows, :].astype(F32))
        split_rows(place, block, held, send, keep)


def second_weights_kernel(
    place, kv_grad, from_prev, from_next, normed, weights, gain_sums, gain,
    send, keep, k_grad, v_grad, gain_part, held,
):
    frames, width = k_grad.shape
    for out, at in ((k_grad, 0), (v_grad, width)):
        columns = slice(at, at + width)
        out[:WINDOW, :] = (
            kv_grad[:WINDOW, columns] + from_prev[:, columns].astype(F32)
        ).astype(BF16)
        out[WINDOW : frames - WINDOW, :] = kv_grad[WINDOW : frames - WINDOW, columns].astype(BF16)
        out[frames - WINDOW :, :] = (
            kv_grad[frames - WINDOW :, columns] + from_next[:, columns].astype(F32)
        ).astype(BF16)
    gain_part[...] = jnp.zeros_like(gain_part)
    for block in range(4):
        rows = slice(width * block, width * (block + 1))
        held[0] = dot_tn(normed[block], k_grad[...])
        held[1] = dot_tn(normed[block], v_grad[...])
        sums = gain_sums[block] + folded(
            held[0] * weights[1, rows, :].astype(F32) + held[1] * weights[2, rows, :].astype(F32)
        )
        for part in range(width // LANES):
            lanes = slice(part * LANES, (part + 1) * LANES)
            turned = jnp.transpose(sums[lanes, :])
            row = jnp.sum(turned, axis=0, keepdims=True)
            gain_part[block : block + 1, lanes] = row / gain[block][:, lanes]
        split_rows(place, block, held, send, keep)
    send[32, :16, :] = in_two(gain_part[...])


def norm_kernel(after, attended, w_out, q_grad, k_grad, v_grad, weights, normed, gain, parts):
    del after
    frames, width = q_grad.shape
    first_sum = second_sum = None
    for block in range(4):
        rows = slice(width * block, width * (block + 1))
        total = None
        for kind, part in enumerate((q_grad, k_grad, v_grad)):
            term = dot_nt(part[...], weights[kind, rows, :])
            total = term if total is None else total + term
        parts[block, :frames, :] = total.astype(BF16)
        branch = dot_nt(attended[...], w_out[rows, :])
        parts[block, frames + 16 :, :] = branch.astype(BF16)
        first = jnp.sum(total * gain[block], axis=1, keepdims=True)
        second = jnp.sum(total * normed[block].astype(F32), axis=1, keepdims=True)
        first_sum = first if first_sum is None else first_sum + first
        second_sum = second if second_sum is None else second_sum + second
    lane = lax.broadcasted_iota(jnp.int32, (frames, LANES), 1)
    sums = jnp.transpose(jnp.where(lane == 0, first_sum, jnp.where(lane == 1, second_sum, 0.0)))
    tail = in_two(sums[:8, :])
    for block in range(4):
        parts[block, frames : frames + 16, :] = tail


def tokens_kernel(place, gain, tokens, out_grad, stats, parts, out):
    frames = tokens.shape[0]
    width = 4 * tokens.shape[1]
    average, inverse_std = stats[:, 0:1], stats[:, 1:2]
    total, rows = None, None
    for block in range(4):
        part = parts[block, :frames, :].astype(F32)
        tail = from_two(parts[block, frames : frames + 16, :])
        total = part if total is None else total + part
        rows = tail if rows is None else rows + tail
    rows = jnp.concatenate([rows, jnp.zeros((LANES - 8, frames), F32)], axis=0) / width
    turned = jnp.transpose(rows)
    first_mean, second_mean = turned[:, 0:1], turned[:, 1:2]
    whitened = (tokens[...].astype(F32) - average) * inverse_std
    unit = total * gain[place[3]]
    moved = (unit - first_mean - whitened * second_mean) * inverse_std
    out[...] = (out_grad[...].astype(F32) + moved).astype(BF16)


def layer_kernel(tokens, mask, parts, out):
    total = None
    for block in range(4):
        term = parts[block, tokens.shape[0] + 16 :, :].astype(F32)
        total = term if total is None else total + term
    for part in range(tokens.shape[0] // WINDOW):
        rows = slice(part * WINDOW, (part + 1) * WINDOW)
        row = mask[:, rows].astype(F32)
        keep = jnp.transpose(jnp.broadcast_to(row, (WINDOW, WINDOW)))
        keep = jnp.concatenate([keep] * (tokens.shape[1] // WINDOW), axis=1)
        out[rows, :] = (tokens[rows, :].astype(F32) + keep * total[rows, :]).astype(BF16)


def core_sum(place, keep, received, outs):
    for step, out in enumerate(outs):
        for z in range(8):
            which = lax.rem(place[1] + step, 4) * 8 + z
            out[z] = (keep[which].astype(F32) + received[which].astype(F32)).astype(out.dtype)


def first_core_kernel(place, keep, received, own, p1, p2, p3):
    core_sum(place, keep, received, (own, p1, p2, p3))


def second_core_kernel(place, keep, received, gain_part, own, p1, p2, p3, gain_sum):
    core_sum(place, keep, received, (own, p1, p2, p3))
    gain_sum[...] = from_two(in_two(gain_part[...])) + from_two(received[32, :16, :])
    for out in (p1, p2, p3):
        out[8, :16, :] = in_two(gain_sum[...])


def x_sum_kernel(
    place, own1, a1, a2, a3, own2, b1, b2, b3, gain_part, send, keep, gain_sum
):
    parity = lax.rem(place[0], 2)
    for out, whose in ((send, 1 - parity), (keep, parity)):
        for far in range(4):
            for at, (own, r1, r2, r3) in enumerate(((own1, a1, a2, a3), (own2, b1, b2, b3))):
                which = 2 * far + whose
                total = own[which] + r2[which].astype(F32)
                total = total + (r1[which].astype(F32) + r3[which].astype(F32))
                start = 96 * far + 48 * at
                out[start : start + 48, :] = total.astype(out.dtype)
    near = from_two(in_two(gain_part[...])) + from_two(b2[8, :16, :])
    gain_sum[...] = near + (from_two(b1[8, :16, :]) + from_two(b3[8, :16, :]))
    send[384:, :] = in_two(gain_sum[...])


def near_sum_kernel(place, keep, received, gain_part, own, p1, p2, p3, gain_sum):
    far = lax.div(place[0], 2)
    gain_sum[...] = from_two(in_two(gain_part[...])) + from_two(received[384:, :])
    for step, out in enumerate((own, p1, p2, p3)):
        rows = pl.ds(pl.multiple_of(96 * lax.rem(far + step, 4), 32), 96)
        total = keep[rows, :] + received[rows, :].astype(F32)
        out[:96, :] = total.astype(out.dtype)
        if step:
            out[96:, :] = in_two(gain_sum[...])


def far_sum_kernel(own, r1, r2, r3, gain_part, out_weight, qkv_weight, gain_sum):
    total = own[...] + r2[:96, :].astype(F32)
    total = total + (r1[:96, :].astype(F32) + r3[:96, :].astype(F32))
    out_weight[...] = total[:24]
    for kind in range(3):
        qkv_weight[kind] = total[24 * (kind + 1) : 24 * (kind + 2)]
    near = from_two(in_two(gain_part[...])) + from_two(r2[96:, :])
    gain_sum[...] = (near + (from_two(r1[96:, :]) + from_two(r3[96:, :])))[:4]


def per_device(tokens, ln_gain, w_qkv, w_out, frame_mask, out_grad):
    frames, width = tokens.shape
    place = jnp.stack([lax.axis_index(a) for a in ("z", "x", "core", "tp")]).astype(jnp.int32)
    token_parts = [tokens] + [shifted(tokens, "tp", -step) for step in (1, 2, 3)]
    late, token_parts[1:] = lax.optimization_barrier((out_grad, token_parts[1:]))
    grad_parts = [out_grad] + [shifted(late, "tp", -step) for step in (1, 2, 3)]
    mask_row = frame_mask[None, :]
    gain = ln_gain.reshape(4, 1, width)
    weights = jnp.transpose(w_qkv, (1, 0, 2))

    sheet, wide_sheet = ((frames, width), BF16), ((4, frames, width), BF16)
    edge, halo = ((WINDOW, 2 * width), BF16), ((WINDOW + 16, 2 * width), BF16)
    square = frames * width * width * 2
    normed, q_own, k_own, v_own, kv_low, kv_high, stats = call(
        project_kernel,
        [wide_sheet, sheet, sheet, sheet, halo, halo, ((frames, LANES), F32)],
        (place, *token_parts, gain, weights, mask_row),
        smem=(0,),
        flops=12 * square,
        moved=8 * 2**20,
    )
    kv_prev, kv_next = to_next(kv_high), to_previous(kv_low)
    span = frames + 2 * WINDOW
    attended, q_grad, kv_grad, edge_low, edge_high, gated = call(
        attention_kernel,
        [sheet, sheet, ((frames, 2 * width), F32), edge, edge, wide_sheet],
        (place, mask_row, q_own, k_own, v_own, kv_prev, kv_next, *grad_parts, w_out),
        smem=(0,),
        scratch=[
            pltpu.VMEM((span, width), BF16),
            pltpu.VMEM((span, width), BF16),
            pltpu.VMEM((LANES, span), BF16),
            pltpu.VMEM((LANES, span), BF16),
            pltpu.VMEM((frames, width), BF16),
            pltpu.VMEM((frames // WINDOW, 3 * WINDOW, WINDOW), F32),
            pltpu.VMEM((span, width), F32),
            pltpu.VMEM((span, width), F32),
        ],
        flops=40 * square,
        moved=8 * 2**20,
    )
    from_next, from_prev = to_previous(edge_low), to_next(edge_high)
    held = pltpu.VMEM((2, frames, width), F32)

    def pieces(count, dtype=BF16):
        return ((count, 48, width), dtype)

    small = ((8, width), F32)
    send, keep, gain_sums = call(
        first_weights_kernel,
        [pieces(32), pieces(32), ((4, frames, LANES), F32)],
        (place, gated, attended, q_grad, normed, weights),
        smem=(0,),
        scratch=[held],
        flops=12 * square,
        moved=9 * 2**20,
    )
    received = swapped(send, "core", 1)
    send2, keep2, k_grad, v_grad, gain_part = call(
        second_weights_kernel,
        [pieces(33), pieces(32), sheet, sheet, small],
        (place, kv_grad, from_prev, from_next, normed, weights, gain_sums, gain),
        smem=(0,),
        scratch=[held],
        flops=12 * square,
        moved=9 * 2**20,
    )
    received2 = swapped(send2, "core", 1)
    own1, *parts = call(
        first_core_kernel,
        [pieces(8, F32)] + [pieces(8)] * 3,
        (place, keep, received),
        smem=(0,),
        moved=6 * 2**20,
        vmem=16,
    )
    received1 = [shifted(part, "x", by + 1) for by, part in enumerate(parts)]
    own2, *parts, gain_part = call(
        second_core_kernel,
        [pieces(8, F32)] + [pieces(9)] * 3 + [small],
        (place, keep2, received2, gain_part),
        smem=(0,),
        moved=6 * 2**20,
        vmem=16,
    )
    received2 = [shifted(part, "x", by + 1) for by, part in enumerate(parts)]
    (exchanged,) = call(
        norm_kernel,
        [((4, 2 * frames + 16, width), BF16)],
        (gain_part, attended, w_out, q_grad, k_grad, v_grad, weights, normed, gain),
        flops=16 * square,
        moved=9 * 2**20,
    )
    exchanged = lax.all_to_all(exchanged, "tp", 0, 0, tiled=True)
    send, keep, gain_part = call(
        x_sum_kernel,
        [((400, width), BF16), ((384, width), F32), small],
        (place, own1, *received1, own2, *received2, gain_part),
        smem=(0,),
        moved=6 * 2**20,
        vmem=16,
    )
    received = swapped(send, "z", 1)
    (layer_out,) = call(
        layer_kernel, [sheet], (tokens, mask_row, exchanged), moved=2 * 2**20, vmem=16
    )
    (tokens_grad,) = call(
        tokens_kernel,
        [sheet],
        (place, gain, tokens, out_grad, stats, exchanged),
        smem=(0,),
        moved=4 * 2**20,
        vmem=16,
    )
    own, *parts, gain_part = call(
        near_sum_kernel,
        [((96, width), F32)] + [((112, width), BF16)] * 3 + [small],
        (place, keep, received, gain_part),
        smem=(0,),
        moved=2**20,
        vmem=16,
    )
    received = [shifted(part, "z", 2 * (by + 1)) for by, part in enumerate(parts)]
    out_weight_grad, qkv_grad, gain_part = call(
        far_sum_kernel,
        [((24, width), F32), ((3, 24, width), F32), ((4, width), F32)],
        (own, *received, gain_part),
        moved=2**20,
        vmem=16,
    )
    around = [shifted(gain_part, "tp", by) for by in (1, 2, 3)]
    gain_grad = (gain_part + around[1]) + (around[0] + around[2])
    return (
        layer_out,
        tokens_grad,
        gain_grad.reshape(-1),
        jnp.transpose(qkv_grad, (1, 0, 2)),
        out_weight_grad,
    )


def solution(mesh):
    split = Mesh(mesh.devices.reshape(8, 4, 2, 4), ("z", "x", "core", "tp"))
    return jax.shard_map(
        per_device,
        mesh=split,
        in_specs=(P(TM, "tp"), P(), P(None, None, "tp"), P(None, "tp"), P(TM), P(TM, "tp")),
        out_specs=(P(TM, "tp"), P(TM, "tp"), P(), P(TM, None, "tp"), P(TM, "tp")),
        check_vma=False,
    )
```

profile of v0, /device:TPU:6, one launch (start us, length us, event | category | flops | bytes accessed | tf_op | source)
XLA Modules:
  0.0 151.8 jit_solution(4776587425269848449)
XLA Ops:
  0.6 3.1 %collective-permute-start = (bf16[384,384]{1,0:T(8,128)(2,1)}, bf16[384,384]{1,0:T(8,128)(2,1)S(1)}, u32[]{:S(2)}, u32[]{:S(2)}) collective-permute-start(bf16[384,384]{1,0:T(8,128)(2,1)} %tokens.3), channel_id=1, source_target_pairs={{0,3},{1,0},{2,1},{3,2},{4,7},{5,4},{6,5},{7,6},{8,11},{9,8},{10,9... | collective-permute-start | bytes 884744 | tf_op jit(solution)/shard_map/ppermute | solution.py:19
  6.8 9.8 %collective-permute-done.t1 = bf16[384,384]{1,0:T(8,128)(2,1)S(1)} collective-permute-done((bf16[384,384]{1,0:T(8,128)(2,1)}, bf16[384,384]{1,0:T(8,128)(2,1)S(1)}, u32[]{:S(2)}, u32[]{:S(2)}) %collective-permute-start) | collective-permute-done | bytes 294944 | tf_op jit(solution)/shard_map/ppermute | solution.py:19
  16.6 3.6 %collective-permute-done.2.t3 = bf16[384,384]{1,0:T(8,128)(2,1)S(1)} collective-permute-done((bf16[384,384]{1,0:T(8,128)(2,1)}, bf16[384,384]{1,0:T(8,128)(2,1)S(1)}, u32[]{:S(2)}, u32[]{:S(2)}) %collective-permute-start.2) | collective-permute-done | bytes 294944 | tf_op jit(solution)/shard_map/ppermute | solution.py:19
  25.2 3.6 %shard_map.101 = (bf16[4,384,384]{2,1,0:T(8,128)(2,1)S(1)}, bf16[384,384]{1,0:T(8,128)(2,1)S(1)}, bf16[384,384]{1,0:T(8,128)(2,1)S(1)}, bf16[384,384]{1,0:T(8,12...) custom-call(s32[4]{0:T(128)S(1)} %pad_add_fusion.place, ...), custom_call_target="tpu_custom_call" | custom-call | flops 1358954496 | bytes 8388608 | tf_op jit(solution)/shard_map/pallas_call | solution.py:53
  30.8 3.8 %collective-permute-start.4 = (bf16[144,768]{1,0:T(8,128)(2,1)S(1)}, bf16[144,768]{1,0:T(8,128)(2,1)S(1)}, u32[]{:S(2)}, u32[]{:S(2)}) collective-permute-start(bf16[144,768]{1,0:T(8,128)(2,1)S(1)} %get-tuple-element.57), channel_id=1, source_target_pairs={{4,0},{8,4},{12,8},{16,12},{20,16},{24,20},{28,24},{32,28},{36,32}... | collective-permute-start | bytes 663560 | tf_op jit(solution)/shard_map/ppermute | solution.py:34
  37.9 6.4 %shard_map.102 = (bf16[384,384]{1,0:T(8,128)(2,1)S(1)}, bf16[384,384]{1,0:T(8,128)(2,1)S(1)}, f32[384,768]{1,0:T(8,128)S(1)}, bf16[128,768]{1,0:T(8,128)(2,1)S(1...) custom-call(s32[4]{0:T(128)S(1)} %pad_add_fusion.place, s32[1,384]{1,0:T(1,128)S(1)} %broadcast_in_dim.3.mask, ...), custom_call_target="tpu_custom_call" | custom-call | flops 4529848320 | bytes 8388608 | tf_op jit(solution)/shard_map/pallas_call | solution.py:53
  44.3 6.1 %collective-permute-start.8 = (bf16[128,768]{1,0:T(8,128)(2,1)S(1)}, bf16[128,768]{1,0:T(8,128)(2,1)S(1)}, u32[]{:S(2)}, u32[]{:S(2)}) collective-permute-start(bf16[128,768]{1,0:T(8,128)(2,1)S(1)} %get-tuple-element.60), channel_id=1, source_target_pairs={{0,4},{4,8},{8,12},{12,16},{16,20},{20,24},{24,28},{28,32},{32,36}... | collective-permute-start | bytes 589832 | tf_op jit(solution)/shard_map/ppermute | solution.py:29
  52.4 3.4 %shard_map.103 = (bf16[32,48,384]{2,1,0:T(8,128)(2,1)}, bf16[32,48,384]{2,1,0:T(8,128)(2,1)S(1)}, f32[4,384,128]{2,1,0:T(8,128)S(1)}) custom-call(s32[4]{0:T(128)S(1)} %pad_add_fusion.place, bf16[4,384,384]{2,1,0:T(8,128)(2,1)S(1)} %get-tuple-element.63.gated, bf16[384,384]{1,0:T(8,128)(2,1)S(1)} %get-tuple-element.64.attended, ...), custom_call_target="tpu_custom_call" | custom-call | flops 1358954496 | bytes 9437184 | tf_op jit(solution)/shard_map/pallas_call | solution.py:53
  56.8 2.8 %shard_map.104 = (bf16[33,48,384]{2,1,0:T(8,128)(2,1)S(1)}, bf16[32,48,384]{2,1,0:T(8,128)(2,1)S(1)}, bf16[384,384]{1,0:T(8,128)(2,1)S(1)}, bf16[384,384]{1,0:T(8,128)(2,1)S(1)}, f32[8,384]{1,0:T(8,128)S(1)}) custom-call(s32[4]{0:T(128)S(1)} %pad_add_fusion.place, f32[384,768]{1,0:T(8,128)S(1)} %get-tuple-element.59.kv_grad, ...), custom_call_target="tpu_custom_call" | custom-call | flops 1358954496 | bytes 9437184 | tf_op jit(solution)/shard_map/pallas_call | solution.py:53
  59.6 2.8 %collective-permute-start.10 = (bf16[33,48,384]{2,1,0:T(8,128)(2,1)S(1)}, bf16[33,48,384]{2,1,0:T(8,128)(2,1)S(1)}, u32[]{:S(2)}, u32[]{:S(2)}) collective-permute-start(bf16[33,48,384]{2,1,0:T(8,128)(2,1)S(1)} %get-tuple-element.68), channel_id=1, source_target_pairs={{0,4},{4,0},{1,5},{5,1},{2,6},{6,2},{3,7},{7,3},{8,12},{12,8},{9,1... | collective-permute-start | bytes 3649544 | tf_op jit(solution)/shard_map/ppermute | solution.py:24
  62.7 2.2 %collective-permute-done.10.received = bf16[33,48,384]{2,1,0:T(8,128)(2,1)S(1)} collective-permute-done((bf16[33,48,384]{2,1,0:T(8,128)(2,1)S(1)}, bf16[33,48,384]{2,1,0:T(8,128)(2,1)S(1)}, u32[]{:S(2)}, u32[]{:S(2)}) %collective-permute-start.10) | collective-permute-done | bytes 1216544 | tf_op jit(solution)/shard_map/ppermute | solution.py:24
  68.0 3.1 %shard_map.106 = bf16[4,784,384]{2,1,0:T(8,128)(2,1)S(1)} custom-call(f32[8,384]{1,0:T(8,128)S(1)} %get-tuple-element.70.after.gain_part, bf16[384,384]{1,0:T(8,128)(2,1)S(1)} %get-tuple-element.64.attended, bf16[1536,384]{1,0:T(8,128)(2,1)S(1)} %copy-done.7, bf16[384,384]{1,0:T(8,128)(2,1)S(1)} %get-tuple-element.65.q_grad, ...), custom_call_target="tpu_custom_call" | custom-call | flops 1811939328 | bytes 9437184 | tf_op jit(solution)/shard_map/pallas_call | solution.py:53
  72.5 5.4 %all-to-all-start = ((bf16[4,784,384]{2,1,0:T(8,128)(2,1)}), bf16[4,784,384]{2,1,0:T(8,128)(2,1)S(1)}, u32[]{:S(2)}, u32[]{:S(2)}) async-start(bf16[4,784,384]{2,1,0:T(8,128)(2,1)} %copy-done.2), calls=%async_computation | async-start | bytes 4816896 | tf_op jit(solution)/shard_map/all_to_all | solution.py:462
  81.1 4.0 %collective-permute-start.16 = (bf16[9,48,384]{2,1,0:T(8,128)(2,1)S(1)}, bf16[9,48,384]{2,1,0:T(8,128)(2,1)S(1)}, u32[]{:S(2)}, u32[]{:S(2)}) collective-permute-start(bf16[9,48,384]{2,1,0:T(8,128)(2,1)S(1)} %copy-done.12), channel_id=1, source_target_pairs={{0,16},{8,24},{16,0},{24,8},{1,17},{9,25},{17,1},{25,9},{2,18},{10... | collective-permute-start | bytes 995336 | tf_op jit(solution)/shard_map/ppermute | solution.py:19
  85.1 2.2 %collective-permute-start.13 = (bf16[8,48,384]{2,1,0:T(8,128)(2,1)S(1)}, bf16[8,48,384]{2,1,0:T(8,128)(2,1)S(1)}, u32[]{:S(2)}, u32[]{:S(2)}) collective-permute-start(bf16[8,48,384]{2,1,0:T(8,128)(2,1)S(1)} %get-tuple-element.78), channel_id=1, source_target_pairs={{0,16},{8,24},{16,0},{24,8},{1,17},{9,25},{17,1},{25,9},{2,18},{10... | collective-permute-start | bytes 884744 | tf_op jit(solution)/shard_map/ppermute | solution.py:19
  87.2 3.6 %collective-permute-done.12.a1 = bf16[8,48,384]{2,1,0:T(8,128)(2,1)S(1)} collective-permute-done((bf16[8,48,384]{2,1,0:T(8,128)(2,1)S(1)}, bf16[8,48,384]{2,1,0:T(8,128)(2,1)S(1)}, u32[]{:S(2)}, u32[]{:S(2)}) %collective-permute-start.12) | collective-permute-done | bytes 294944 | tf_op jit(solution)/shard_map/ppermute | solution.py:19
  90.8 16.4 %collective-permute-done.13.a2 = bf16[8,48,384]{2,1,0:T(8,128)(2,1)S(1)} collective-permute-done((bf16[8,48,384]{2,1,0:T(8,128)(2,1)S(1)}, bf16[8,48,384]{2,1,0:T(8,128)(2,1)S(1)}, u32[]{:S(2)}, u32[]{:S(2)}) %collective-permute-start.13) | collective-permute-done | bytes 294944 | tf_op jit(solution)/shard_map/ppermute | solution.py:19
  107.2 5.0 %collective-permute-done.14.a3 = bf16[8,48,384]{2,1,0:T(8,128)(2,1)S(1)} collective-permute-done((bf16[8,48,384]{2,1,0:T(8,128)(2,1)S(1)}, bf16[8,48,384]{2,1,0:T(8,128)(2,1)S(1)}, u32[]{:S(2)}, u32[]{:S(2)}) %collective-permute-start.14) | collective-permute-done | bytes 294944 | tf_op jit(solution)/shard_map/ppermute | solution.py:19
  115.1 7.5 %collective-permute-done.18.received = bf16[400,384]{1,0:T(8,128)(2,1)S(1)} collective-permute-done((bf16[400,384]{1,0:T(8,128)(2,1)S(1)}, bf16[400,384]{1,0:T(8,128)(2,1)S(1)}, u32[]{:S(2)}, u32[]{:S(2)}) %collective-permute-start.18) | collective-permute-done | bytes 307232 | tf_op jit(solution)/shard_map/ppermute | solution.py:24
  123.2 7.0 %collective-permute-start.19 = (bf16[112,384]{1,0:T(8,128)(2,1)S(1)}, bf16[112,384]{1,0:T(8,128)(2,1)S(1)}, u32[]{:S(2)}, u32[]{:S(2)}) collective-permute-start(bf16[112,384]{1,0:T(8,128)(2,1)S(1)} %get-tuple-element.88), channel_id=1, source_target_pairs={{0,64},{32,96},{64,128},{96,160},{128,192},{160,224},{192,0},{224,... | collective-permute-start | bytes 258056 | tf_op jit(solution)/shard_map/ppermute | solution.py:19
  132.2 4.0 %collective-permute-start.21 = (bf16[112,384]{1,0:T(8,128)(2,1)S(1)}, bf16[112,384]{1,0:T(8,128)(2,1)S(1)}, u32[]{:S(2)}, u32[]{:S(2)}) collective-permute-start(bf16[112,384]{1,0:T(8,128)(2,1)S(1)} %get-tuple-element.90), channel_id=1, source_target_pairs={{0,192},{32,224},{64,0},{96,32},{128,64},{160,96},{192,128},{224,1... | collective-permute-start | bytes 258056 | tf_op jit(solution)/shard_map/ppermute | solution.py:19
  136.2 2.9 %collective-permute-done.20.r2 = bf16[112,384]{1,0:T(8,128)(2,1)S(1)} collective-permute-done((bf16[112,384]{1,0:T(8,128)(2,1)S(1)}, bf16[112,384]{1,0:T(8,128)(2,1)S(1)}, u32[]{:S(2)}, u32[]{:S(2)}) %collective-permute-start.20) | collective-permute-done | bytes 86048 | tf_op jit(solution)/shard_map/ppermute | solution.py:19
  140.3 3.2 %collective-permute-start.22 = (f32[4,384]{1,0:T(4,128)S(1)}, f32[4,384]{1,0:T(4,128)S(1)}, u32[]{:S(2)}, u32[]{:S(2)}) collective-permute-start(f32[4,384]{1,0:T(4,128)S(1)} %get-tuple-element.92), channel_id=1, source_target_pairs={{0,2},{1,3},{2,0},{3,1},{4,6},{5,7},{6,4},{7,5},{8,10},{9,11},{10,... | collective-permute-start | bytes 18440 | tf_op jit(solution)/shard_map/ppermute | solution.py:19
  144.1 2.7 %collective-permute-start.24 = (f32[4,384]{1,0:T(4,128)S(1)}, f32[4,384]{1,0:T(4,128)S(1)}, u32[]{:S(2)}, u32[]{:S(2)}) collective-permute-start(f32[4,384]{1,0:T(4,128)S(1)} %get-tuple-element.92), channel_id=1, source_target_pairs={{0,3},{1,0},{2,1},{3,2},{4,7},{5,4},{6,5},{7,6},{8,11},{9,8},{10,9... | collective-permute-start | bytes 18440 | tf_op jit(solution)/shard_map/ppermute | solution.py:19
  (75 shorter events, 36.2 us)
Async XLA Ops:
  0.6 16.0 %collective-permute-start = (bf16[384,384]{1,0:T(8,128)(2,1)}, bf16[384,384]{1,0:T(8,128)(2,1)S(1)}, u32[]{:S(2)}, u32[]{:S(2)}) collective-permute-start(bf16[384,384]{1,0:T(8,128)(2,1)} %tokens.3), channel_id=1, source_target_pairs={{0,3},{1,0},{2,1},{3,2},{4,7},{5,4},{6,5},{7,6},{8,11},{9,8},{10,9... | collective-permute-start | bytes 884744 | tf_op jit(solution)/shard_map/ppermute | solution.py:19
  3.7 12.9 %collective-permute-start.1 = (bf16[384,384]{1,0:T(8,128)(2,1)}, bf16[384,384]{1,0:T(8,128)(2,1)S(1)}, u32[]{:S(2)}, u32[]{:S(2)}) collective-permute-start(bf16[384,384]{1,0:T(8,128)(2,1)} %tokens.3), channel_id=1, source_target_pairs={{0,2},{1,3},{2,0},{3,1},{4,6},{5,7},{6,4},{7,5},{8,10},{9,11},{10,... | collective-permute-start | bytes 884744 | tf_op jit(solution)/shard_map/ppermute | solution.py:19
  4.4 15.9 %collective-permute-start.2 = (bf16[384,384]{1,0:T(8,128)(2,1)}, bf16[384,384]{1,0:T(8,128)(2,1)S(1)}, u32[]{:S(2)}, u32[]{:S(2)}) collective-permute-start(bf16[384,384]{1,0:T(8,128)(2,1)} %tokens.3), channel_id=1, source_target_pairs={{0,1},{1,2},{2,3},{3,0},{4,5},{5,6},{6,7},{7,4},{8,9},{9,10},{10,1... | collective-permute-start | bytes 884744 | tf_op jit(solution)/shard_map/ppermute | solution.py:19
  20.2 17.6 %collective-permute-start.5 = (bf16[384,384]{1,0:T(8,128)(2,1)}, bf16[384,384]{1,0:T(8,128)(2,1)S(1)}, u32[]{:S(2)}, u32[]{:S(2)}) collective-permute-start(bf16[384,384]{1,0:T(8,128)(2,1)} %out_grad.1), channel_id=1, source_target_pairs={{0,3},{1,0},{2,1},{3,2},{4,7},{5,4},{6,5},{7,6},{8,11},{9,8},{10,9... | collective-permute-start | bytes 884744 | tf_op jit(solution)/shard_map/ppermute | solution.py:19
  20.8 17.0 %collective-permute-start.6 = (bf16[384,384]{1,0:T(8,128)(2,1)}, bf16[384,384]{1,0:T(8,128)(2,1)S(1)}, u32[]{:S(2)}, u32[]{:S(2)}) collective-permute-start(bf16[384,384]{1,0:T(8,128)(2,1)} %out_grad.1), channel_id=1, source_target_pairs={{0,2},{1,3},{2,0},{3,1},{4,6},{5,7},{6,4},{7,5},{8,10},{9,11},{10,... | collective-permute-start | bytes 884744 | tf_op jit(solution)/shard_map/ppermute | solution.py:19
  21.5 16.4 %collective-permute-start.7 = (bf16[384,384]{1,0:T(8,128)(2,1)}, bf16[384,384]{1,0:T(8,128)(2,1)S(1)}, u32[]{:S(2)}, u32[]{:S(2)}) collective-permute-start(bf16[384,384]{1,0:T(8,128)(2,1)} %out_grad.1), channel_id=1, source_target_pairs={{0,1},{1,2},{2,3},{3,0},{4,5},{5,6},{6,7},{7,4},{8,9},{9,10},{10,1... | collective-permute-start | bytes 884744 | tf_op jit(solution)/shard_map/ppermute | solution.py:19
  28.8 7.3 %collective-permute-start.3 = (bf16[144,768]{1,0:T(8,128)(2,1)S(1)}, bf16[144,768]{1,0:T(8,128)(2,1)S(1)}, u32[]{:S(2)}, u32[]{:S(2)}) collective-permute-start(bf16[144,768]{1,0:T(8,128)(2,1)S(1)} %get-tuple-element.56), channel_id=1, source_target_pairs={{0,4},{4,8},{8,12},{12,16},{16,20},{20,24},{24,28},{28,32},{32,36}... | collective-permute-start | bytes 663560 | tf_op jit(solution)/shard_map/ppermute | solution.py:29
  30.8 7.1 %collective-permute-start.4 = (bf16[144,768]{1,0:T(8,128)(2,1)S(1)}, bf16[144,768]{1,0:T(8,128)(2,1)S(1)}, u32[]{:S(2)}, u32[]{:S(2)}) collective-permute-start(bf16[144,768]{1,0:T(8,128)(2,1)S(1)} %get-tuple-element.57), channel_id=1, source_target_pairs={{4,0},{8,4},{12,8},{16,12},{20,16},{24,20},{28,24},{32,28},{36,32}... | collective-permute-start | bytes 663560 | tf_op jit(solution)/shard_map/ppermute | solution.py:34
  44.3 12.5 %collective-permute-start.8 = (bf16[128,768]{1,0:T(8,128)(2,1)S(1)}, bf16[128,768]{1,0:T(8,128)(2,1)S(1)}, u32[]{:S(2)}, u32[]{:S(2)}) collective-permute-start(bf16[128,768]{1,0:T(8,128)(2,1)S(1)} %get-tuple-element.60), channel_id=1, source_target_pairs={{0,4},{4,8},{8,12},{12,16},{16,20},{20,24},{24,28},{28,32},{32,36}... | collective-permute-start | bytes 589832 | tf_op jit(solution)/shard_map/ppermute | solution.py:29
  50.4 6.4 %collective-permute-start.9 = (bf16[128,768]{1,0:T(8,128)(2,1)S(1)}, bf16[128,768]{1,0:T(8,128)(2,1)S(1)}, u32[]{:S(2)}, u32[]{:S(2)}) collective-permute-start(bf16[128,768]{1,0:T(8,128)(2,1)S(1)} %get-tuple-element.61), channel_id=1, source_target_pairs={{4,0},{8,4},{12,8},{16,12},{20,16},{24,20},{28,24},{32,28},{36,32}... | collective-permute-start | bytes 589832 | tf_op jit(solution)/shard_map/ppermute | solution.py:34
  59.6 5.3 %collective-permute-start.10 = (bf16[33,48,384]{2,1,0:T(8,128)(2,1)S(1)}, bf16[33,48,384]{2,1,0:T(8,128)(2,1)S(1)}, u32[]{:S(2)}, u32[]{:S(2)}) collective-permute-start(bf16[33,48,384]{2,1,0:T(8,128)(2,1)S(1)} %get-tuple-element.68), channel_id=1, source_target_pairs={{0,4},{4,0},{1,5},{5,1},{2,6},{6,2},{3,7},{7,3},{8,12},{12,8},{9,1... | collective-permute-start | bytes 3649544 | tf_op jit(solution)/shard_map/ppermute | solution.py:24
  62.4 15.6 %collective-permute-start.11 = (bf16[32,48,384]{2,1,0:T(8,128)(2,1)}, bf16[32,48,384]{2,1,0:T(8,128)(2,1)}, u32[]{:S(2)}, u32[]{:S(2)}) collective-permute-start(bf16[32,48,384]{2,1,0:T(8,128)(2,1)} %get-tuple-element.75), channel_id=1, source_target_pairs={{0,4},{4,0},{1,5},{5,1},{2,6},{6,2},{3,7},{7,3},{8,12},{12,8},{9,1... | collective-permute-start | bytes 3538952 | tf_op jit(solution)/shard_map/ppermute | solution.py:24
  72.5 76.5 %all-to-all-start = ((bf16[4,784,384]{2,1,0:T(8,128)(2,1)}), bf16[4,784,384]{2,1,0:T(8,128)(2,1)S(1)}, u32[]{:S(2)}, u32[]{:S(2)}) async-start(bf16[4,784,384]{2,1,0:T(8,128)(2,1)} %copy-done.2), calls=%async_computation | async-start | bytes 4816896 | tf_op jit(solution)/shard_map/all_to_all | solution.py:462
  80.9 9.9 %collective-permute-start.12 = (bf16[8,48,384]{2,1,0:T(8,128)(2,1)S(1)}, bf16[8,48,384]{2,1,0:T(8,128)(2,1)S(1)}, u32[]{:S(2)}, u32[]{:S(2)}) collective-permute-start(bf16[8,48,384]{2,1,0:T(8,128)(2,1)S(1)} %get-tuple-element.77), channel_id=1, source_target_pairs={{0,8},{8,16},{16,24},{24,0},{1,9},{9,17},{17,25},{25,1},{2,10},{10... | collective-permute-start | bytes 884744 | tf_op jit(solution)/shard_map/ppermute | solution.py:19
  81.0 31.3 %collective-permute-start.15 = (bf16[9,48,384]{2,1,0:T(8,128)(2,1)S(1)}, bf16[9,48,384]{2,1,0:T(8,128)(2,1)S(1)}, u32[]{:S(2)}, u32[]{:S(2)}) collective-permute-start(bf16[9,48,384]{2,1,0:T(8,128)(2,1)S(1)} %copy-done.14), channel_id=1, source_target_pairs={{0,8},{8,16},{16,24},{24,0},{1,9},{9,17},{17,25},{25,1},{2,10},{10... | collective-permute-start | bytes 995336 | tf_op jit(solution)/shard_map/ppermute | solution.py:19
  81.1 31.2 %collective-permute-start.16 = (bf16[9,48,384]{2,1,0:T(8,128)(2,1)S(1)}, bf16[9,48,384]{2,1,0:T(8,128)(2,1)S(1)}, u32[]{:S(2)}, u32[]{:S(2)}) collective-permute-start(bf16[9,48,384]{2,1,0:T(8,128)(2,1)S(1)} %copy-done.12), channel_id=1, source_target_pairs={{0,16},{8,24},{16,0},{24,8},{1,17},{9,25},{17,1},{25,9},{2,18},{10... | collective-permute-start | bytes 995336 | tf_op jit(solution)/shard_map/ppermute | solution.py:19
  85.1 27.2 %collective-permute-start.17 = (bf16[9,48,384]{2,1,0:T(8,128)(2,1)S(1)}, bf16[9,48,384]{2,1,0:T(8,128)(2,1)S(1)}, u32[]{:S(2)}, u32[]{:S(2)}) collective-permute-start(bf16[9,48,384]{2,1,0:T(8,128)(2,1)S(1)} %copy-done.10), channel_id=1, source_target_pairs={{0,24},{8,0},{16,8},{24,16},{1,25},{9,1},{17,9},{25,17},{2,26},{10... | collective-permute-start | bytes 995336 | tf_op jit(solution)/shard_map/ppermute | solution.py:19
  85.1 22.2 %collective-permute-start.13 = (bf16[8,48,384]{2,1,0:T(8,128)(2,1)S(1)}, bf16[8,48,384]{2,1,0:T(8,128)(2,1)S(1)}, u32[]{:S(2)}, u32[]{:S(2)}) collective-permute-start(bf16[8,48,384]{2,1,0:T(8,128)(2,1)S(1)} %get-tuple-element.78), channel_id=1, source_target_pairs={{0,16},{8,24},{16,0},{24,8},{1,17},{9,25},{17,1},{25,9},{2,18},{10... | collective-permute-start | bytes 884744 | tf_op jit(solution)/shard_map/ppermute | solution.py:19
  90.8 21.5 %collective-permute-start.14 = (bf16[8,48,384]{2,1,0:T(8,128)(2,1)S(1)}, bf16[8,48,384]{2,1,0:T(8,128)(2,1)S(1)}, u32[]{:S(2)}, u32[]{:S(2)}) collective-permute-start(bf16[8,48,384]{2,1,0:T(8,128)(2,1)S(1)} %get-tuple-element.79), channel_id=1, source_target_pairs={{0,24},{8,0},{16,8},{24,16},{1,25},{9,1},{17,9},{25,17},{2,26},{10... | collective-permute-start | bytes 884744 | tf_op jit(solution)/shard_map/ppermute | solution.py:19
  113.2 9.4 %collective-permute-start.18 = (bf16[400,384]{1,0:T(8,128)(2,1)S(1)}, bf16[400,384]{1,0:T(8,128)(2,1)S(1)}, u32[]{:S(2)}, u32[]{:S(2)}) collective-permute-start(bf16[400,384]{1,0:T(8,128)(2,1)S(1)} %get-tuple-element.85), channel_id=1, source_target_pairs={{0,32},{32,0},{64,96},{96,64},{128,160},{160,128},{192,224},{224,1... | collective-permute-start | bytes 921608 | tf_op jit(solution)/shard_map/ppermute | solution.py:24
  123.2 13.0 %collective-permute-start.19 = (bf16[112,384]{1,0:T(8,128)(2,1)S(1)}, bf16[112,384]{1,0:T(8,128)(2,1)S(1)}, u32[]{:S(2)}, u32[]{:S(2)}) collective-permute-start(bf16[112,384]{1,0:T(8,128)(2,1)S(1)} %get-tuple-element.88), channel_id=1, source_target_pairs={{0,64},{32,96},{64,128},{96,160},{128,192},{160,224},{192,0},{224,... | collective-permute-start | bytes 258056 | tf_op jit(solution)/shard_map/ppermute | solution.py:19
  130.2 8.9 %collective-permute-start.20 = (bf16[112,384]{1,0:T(8,128)(2,1)S(1)}, bf16[112,384]{1,0:T(8,128)(2,1)S(1)}, u32[]{:S(2)}, u32[]{:S(2)}) collective-permute-start(bf16[112,384]{1,0:T(8,128)(2,1)S(1)} %get-tuple-element.89), channel_id=1, source_target_pairs={{0,128},{32,160},{64,192},{96,224},{128,0},{160,32},{192,64},{224,... | collective-permute-start | bytes 258056 | tf_op jit(solution)/shard_map/ppermute | solution.py:19
  132.2 7.5 %collective-permute-start.21 = (bf16[112,384]{1,0:T(8,128)(2,1)S(1)}, bf16[112,384]{1,0:T(8,128)(2,1)S(1)}, u32[]{:S(2)}, u32[]{:S(2)}) collective-permute-start(bf16[112,384]{1,0:T(8,128)(2,1)S(1)} %get-tuple-element.90), channel_id=1, source_target_pairs={{0,192},{32,224},{64,0},{96,32},{128,64},{160,96},{192,128},{224,1... | collective-permute-start | bytes 258056 | tf_op jit(solution)/shard_map/ppermute | solution.py:19
  140.3 6.5 %collective-permute-start.22 = (f32[4,384]{1,0:T(4,128)S(1)}, f32[4,384]{1,0:T(4,128)S(1)}, u32[]{:S(2)}, u32[]{:S(2)}) collective-permute-start(f32[4,384]{1,0:T(4,128)S(1)} %get-tuple-element.92), channel_id=1, source_target_pairs={{0,2},{1,3},{2,0},{3,1},{4,6},{5,7},{6,4},{7,5},{8,10},{9,11},{10,... | collective-permute-start | bytes 18440 | tf_op jit(solution)/shard_map/ppermute | solution.py:19
  (17 other events, 103.1 us)
where the time goes:
time: 153 us; the launch traced here: 152 us
  starting transfers between devices  56.8 us (37%)
  waiting for transfers between devices  56.5 us (37%)
  Pallas kernels  26.7 us (17%)
  local copies, waits for them, and re-layouts  10.9 us (7%)
    ppermute x18, waiting for transfers between devices, shifted(): lax.ppermute(value, axis, [(i, (i + by) % size) for i in range(size)])  43.5 us
    ppermute x18, starting transfers between devices, shifted(): lax.ppermute(value, axis, [(i, (i + by) % size) for i in range(size)])  32.5 us
    pallas_call x12, Pallas kernels, call(): pl.pallas_call(body, out_shape=[jax.ShapeDtypeStruct(s, d) for s, d in ou...  26.7 us
    ppermute x3, waiting for transfers between devices, swapped(): return lax.ppermute(value, axis, [(i, i ^ bit) for i in range(size)])  9.66 us
    unnamed x30, local copies, waits for them, and re-layouts  8.89 us
    ppermute x2, starting transfers between devices, to_next(): return lax.ppermute(value, TM, [(i, i + 1) for i in range(size - 1)])  8.05 us
    ppermute x2, starting transfers between devices, to_previous(): return lax.ppermute(value, TM, [(i + 1, i) for i in range(size - 1)])  5.74 us
    all_to_all x1, starting transfers between devices, per_device(): exchanged = lax.all_to_all(exchanged, 'tp', 0, 0, tiled=True)  5.41 us
  transfers between devices with their start and end apart: 26, of which 12 were waited for; matrix products, arithmetic and copies ran while one was open for 1% of the time, Pallas kernels for 10%

commit v1 on v0

--- a/solution.py
+++ b/solution.py
@@ -46,9 +46,12 @@
     return lax.dot_general(a, b, (((0,), (0,)), ((), ())), preferred_element_type=F32)
 
 
-def call(body, outs, args, smem=(), scratch=(), flops=0, moved=0, vmem=24):
+def call(body, outs, args, smem=(), far=(), scratch=(), cost=0, vmem=24):
     in_specs = [
-        pl.BlockSpec(memory_space=pltpu.SMEM if k in smem else pltpu.VMEM) for k in range(len(args))
+        pl.BlockSpec(
+            memory_space=pltpu.SMEM if k in smem else pltpu.HBM if k in far else pltpu.VMEM
+        )
+        for k in range(len(args))
     ]
     return pl.pallas_call(
         body,
@@ -56,13 +59,22 @@
         in_specs=in_specs,
         out_specs=[pl.BlockSpec(memory_space=pltpu.VMEM)] * len(outs),
         scratch_shapes=list(scratch),
-        cost_estimate=pl.CostEstimate(flops=flops, bytes_accessed=moved, transcendentals=0),
+        cost_estimate=pl.CostEstimate(flops=cost, bytes_accessed=0, transcendentals=0),
         compiler_params=pltpu.CompilerParams(vmem_limit_bytes=vmem * 2**20),
     )(*args)
 
 
 def block_of(place, step):
     return lax.rem(place[3] + step, 4)
+
+
+def preload_kernel(weights, tokens, weights_here, tokens_here, arrived):
+    first = pltpu.make_async_copy(weights, weights_here, arrived.at[0])
+    second = pltpu.make_async_copy(tokens, tokens_here, arrived.at[1])
+    first.start()
+    second.start()
+    first.wait()
+    second.wait()
 
 
 def project_kernel(
@@ -223,6 +235,13 @@
         split_rows(place, block, held, send, keep)
 
 
+def branch_kernel(attended, w_out, branches):
+    width = attended.shape[1]
+    for block in range(4):
+        rows = w_out[width * block : width * (block + 1), :]
+        branches[block] = dot_nt(attended[...], rows).astype(BF16)
+
+
 def second_weights_kernel(
     place, kv_grad, from_prev, from_next, normed, weights, gain_sums, gain,
     send, keep, k_grad, v_grad, gain_part, held,
@@ -254,19 +273,20 @@
     send[32, :16, :] = in_two(gain_part[...])
 
 
-def norm_kernel(after, attended, w_out, q_grad, k_grad, v_grad, weights, normed, gain, parts):
-    del after
+def norm_kernel(
+    place, branches, q_grad, k_grad, v_grad, weights, normed, gain, n0, n1, n2, n3
+):
     frames, width = q_grad.shape
     first_sum = second_sum = None
-    for block in range(4):
-        rows = slice(width * block, width * (block + 1))
+    for step, out in enumerate((n0, n1, n2, n3)):
+        block = block_of(place, step)
+        rows = pl.ds(pl.multiple_of(width * block, width), width)
         total = None
         for kind, part in enumerate((q_grad, k_grad, v_grad)):
             term = dot_nt(part[...], weights[kind, rows, :])
             total = term if total is None else total + term
-        parts[block, :frames, :] = total.astype(BF16)
-        branch = dot_nt(attended[...], w_out[rows, :])
-        parts[block, frames + 16 :, :] = branch.astype(BF16)
+        out[:frames, :] = total.astype(BF16)
+        out[frames + 16 :, :] = branches[block]
         first = jnp.sum(total * gain[block], axis=1, keepdims=True)
         second = jnp.sum(total * normed[block].astype(F32), axis=1, keepdims=True)
         first_sum = first if first_sum is None else first_sum + first
@@ -274,18 +294,18 @@
     lane = lax.broadcasted_iota(jnp.int32, (frames, LANES), 1)
     sums = jnp.transpose(jnp.where(lane == 0, first_sum, jnp.where(lane == 1, second_sum, 0.0)))
     tail = in_two(sums[:8, :])
-    for block in range(4):
-        parts[block, frames : frames + 16, :] = tail
-
-
-def tokens_kernel(place, gain, tokens, out_grad, stats, parts, out):
+    for out in (n0, n1, n2, n3):
+        out[frames : frames + 16, :] = tail
+
+
+def tokens_kernel(place, gain, tokens, out_grad, stats, n0, n1, n2, n3, out):
     frames = tokens.shape[0]
     width = 4 * tokens.shape[1]
     average, inverse_std = stats[:, 0:1], stats[:, 1:2]
     total, rows = None, None
-    for block in range(4):
-        part = parts[block, :frames, :].astype(F32)
-        tail = from_two(parts[block, frames : frames + 16, :])
+    for ref in (n0, n1, n2, n3):
+        part = ref[:frames, :].astype(F32)
+        tail = from_two(ref[frames : frames + 16, :])
         total = part if total is None else total + part
         rows = tail if rows is None else rows + tail
     rows = jnp.concatenate([rows, jnp.zeros((LANES - 8, frames), F32)], axis=0) / width
@@ -297,10 +317,10 @@
     out[...] = (out_grad[...].astype(F32) + moved).astype(BF16)
 
 
-def layer_kernel(tokens, mask, parts, out):
+def layer_kernel(tokens, mask, n0, n1, n2, n3, out):
     total = None
-    for block in range(4):
-        term = parts[block, tokens.shape[0] + 16 :, :].astype(F32)
+    for ref in (n0, n1, n2, n3):
+        term = ref[tokens.shape[0] + 16 :, :].astype(F32)
         total = term if total is None else total + term
     for part in range(tokens.shape[0] // WINDOW):
         rows = slice(part * WINDOW, (part + 1) * WINDOW)
@@ -317,8 +337,14 @@
             out[z] = (keep[which].astype(F32) + received[which].astype(F32)).astype(out.dtype)
 
 
-def first_core_kernel(place, keep, received, own, p1, p2, p3):
-    core_sum(place, keep, received, (own, p1, p2, p3))
+def first_core_kernel(place, keep, received, send, own):
+    parity = lax.rem(place[0], 2)
+    for out, whose in ((send, 1 - parity), (own, parity)):
+        for x in range(4):
+            for far in range(4):
+                which = 8 * x + 2 * far + whose
+                total = keep[which].astype(F32) + received[which].astype(F32)
+                out[4 * x + far] = total.astype(out.dtype)
 
 
 def second_core_kernel(place, keep, received, gain_part, own, p1, p2, p3, gain_sum):
@@ -328,30 +354,38 @@
         out[8, :16, :] = in_two(gain_sum[...])
 
 
-def x_sum_kernel(
-    place, own1, a1, a2, a3, own2, b1, b2, b3, gain_part, send, keep, gain_sum
-):
+def first_near_kernel(place, keep, received, own, p1, p2, p3):
+    for step, out in enumerate((own, p1, p2, p3)):
+        for far in range(4):
+            which = lax.rem(place[1] + step, 4) * 4 + far
+            out[far] = (keep[which] + received[which].astype(F32)).astype(out.dtype)
+
+
+def second_x_kernel(place, own, r1, r2, r3, gain_part, send, keep, gain_sum):
     parity = lax.rem(place[0], 2)
     for out, whose in ((send, 1 - parity), (keep, parity)):
         for far in range(4):
-            for at, (own, r1, r2, r3) in enumerate(((own1, a1, a2, a3), (own2, b1, b2, b3))):
-                which = 2 * far + whose
-                total = own[which] + r2[which].astype(F32)
-                total = total + (r1[which].astype(F32) + r3[which].astype(F32))
-                start = 96 * far + 48 * at
-                out[start : start + 48, :] = total.astype(out.dtype)
-    near = from_two(in_two(gain_part[...])) + from_two(b2[8, :16, :])
-    gain_sum[...] = near + (from_two(b1[8, :16, :]) + from_two(b3[8, :16, :]))
-    send[384:, :] = in_two(gain_sum[...])
-
-
-def near_sum_kernel(place, keep, received, gain_part, own, p1, p2, p3, gain_sum):
-    far = lax.div(place[0], 2)
-    gain_sum[...] = from_two(in_two(gain_part[...])) + from_two(received[384:, :])
+            which = 2 * far + whose
+            total = own[which] + r2[which].astype(F32)
+            total = total + (r1[which].astype(F32) + r3[which].astype(F32))
+            out[48 * far : 48 * far + 48, :] = total.astype(out.dtype)
+    near = from_two(in_two(gain_part[...])) + from_two(r2[8, :16, :])
+    gain_sum[...] = near + (from_two(r1[8, :16, :]) + from_two(r3[8, :16, :]))
+    send[192:, :] = in_two(gain_sum[...])
+
+
+def near_sum_kernel(
+    place, own1, r1, r2, r3, keep, received, gain_part, own, p1, p2, p3, gain_sum
+):
+    gain_sum[...] = from_two(in_two(gain_part[...])) + from_two(received[192:, :])
     for step, out in enumerate((own, p1, p2, p3)):
-        rows = pl.ds(pl.multiple_of(96 * lax.rem(far + step, 4), 32), 96)
-        total = keep[rows, :] + received[rows, :].astype(F32)
-        out[:96, :] = total.astype(out.dtype)
+        far = lax.rem(lax.div(place[0], 2) + step, 4)
+        first = own1[far] + r2[far].astype(F32)
+        first = first + (r1[far].astype(F32) + r3[far].astype(F32))
+        rows = pl.ds(pl.multiple_of(48 * far, 16), 48)
+        second = keep[rows, :] + received[rows, :].astype(F32)
+        out[:48, :] = first.astype(out.dtype)
+        out[48:96, :] = second.astype(out.dtype)
         if step:
             out[96:, :] = in_two(gain_sum[...])
 
@@ -370,11 +404,20 @@
     frames, width = tokens.shape
     place = jnp.stack([lax.axis_index(a) for a in ("z", "x", "core", "tp")]).astype(jnp.int32)
     token_parts = [tokens] + [shifted(tokens, "tp", -step) for step in (1, 2, 3)]
-    late, token_parts[1:] = lax.optimization_barrier((out_grad, token_parts[1:]))
+    late, token_parts[3] = lax.optimization_barrier((out_grad, token_parts[3]))
     grad_parts = [out_grad] + [shifted(late, "tp", -step) for step in (1, 2, 3)]
     mask_row = frame_mask[None, :]
     gain = ln_gain.reshape(4, 1, width)
     weights = jnp.transpose(w_qkv, (1, 0, 2))
+    weights_here, token_parts[0] = call(
+        preload_kernel,
+        [(weights.shape, BF16), ((frames, width), BF16)],
+        (weights, tokens),
+        far=(0, 1),
+        scratch=[pltpu.SemaphoreType.DMA((2,))],
+        cost=2**30,
+        vmem=8,
+    )
 
     sheet, wide_sheet = ((frames, width), BF16), ((4, frames, width), BF16)
     edge, halo = ((WINDOW, 2 * width), BF16), ((WINDOW + 16, 2 * width), BF16)
@@ -382,10 +425,9 @@
     normed, q_own, k_own, v_own, kv_low, kv_high, stats = call(
         project_kernel,
         [wide_sheet, sheet, sheet, sheet, halo, halo, ((frames, LANES), F32)],
-        (place, *token_parts, gain, weights, mask_row),
-        smem=(0,),
-        flops=12 * square,
-        moved=8 * 2**20,
+        (place, *token_parts, gain, weights_here, mask_row),
+        smem=(0,),
+        cost=12 * square,
     )
     kv_prev, kv_next = to_next(kv_high), to_previous(kv_low)
     span = frames + 2 * WINDOW
@@ -404,8 +446,6 @@
             pltpu.VMEM((span, width), F32),
             pltpu.VMEM((span, width), F32),
         ],
-        flops=40 * square,
-        moved=8 * 2**20,
     )
     from_next, from_prev = to_previous(edge_low), to_next(edge_high)
     held = pltpu.VMEM((2, frames, width), F32)
@@ -420,80 +460,87 @@
         (place, gated, attended, q_grad, normed, weights),
         smem=(0,),
         scratch=[held],
-        flops=12 * square,
-        moved=9 * 2**20,
+        cost=12 * square,
     )
     received = swapped(send, "core", 1)
+    (branches,) = call(branch_kernel, [wide_sheet], (attended, w_out), cost=4 * square)
+    branches, from_prev, from_next, received = lax.optimization_barrier(
+        (branches, from_prev, from_next, received)
+    )
     send2, keep2, k_grad, v_grad, gain_part = call(
         second_weights_kernel,
         [pieces(33), pieces(32), sheet, sheet, small],
         (place, kv_grad, from_prev, from_next, normed, weights, gain_sums, gain),
         smem=(0,),
         scratch=[held],
-        flops=12 * square,
-        moved=9 * 2**20,
     )
     received2 = swapped(send2, "core", 1)
-    own1, *parts = call(
+    near1, keep1 = call(
         first_core_kernel,
-        [pieces(8, F32)] + [pieces(8)] * 3,
+        [pieces(16), pieces(16, F32)],
         (place, keep, received),
         smem=(0,),
-        moved=6 * 2**20,
-        vmem=16,
-    )
-    received1 = [shifted(part, "x", by + 1) for by, part in enumerate(parts)]
-    own2, *parts, gain_part = call(
+        vmem=16,
+    )
+    k_grad, near1 = lax.optimization_barrier((k_grad, near1))
+    near1 = swapped(near1, "z", 1)
+    exchanged = [None] * 4
+    exchanged[:] = call(
+        norm_kernel,
+        [((2 * frames + 16, width), BF16)] * 4,
+        (place, branches, q_grad, k_grad, v_grad, weights, normed, gain),
+        smem=(0,),
+    )
+    received2, exchanged[0] = lax.optimization_barrier((received2, exchanged[0]))
+    own2, *parts2, gain_part = call(
         second_core_kernel,
         [pieces(8, F32)] + [pieces(9)] * 3 + [small],
         (place, keep2, received2, gain_part),
         smem=(0,),
-        moved=6 * 2**20,
-        vmem=16,
-    )
-    received2 = [shifted(part, "x", by + 1) for by, part in enumerate(parts)]
-    (exchanged,) = call(
-        norm_kernel,
-        [((4, 2 * frames + 16, width), BF16)],
-        (gain_part, attended, w_out, q_grad, k_grad, v_grad, weights, normed, gain),
-        flops=16 * square,
-        moved=9 * 2**20,
-    )
-    exchanged = lax.all_to_all(exchanged, "tp", 0, 0, tiled=True)
+        vmem=16,
+    )
+    received2 = [shifted(part, "x", by + 1) for by, part in enumerate(parts2)]
+    own1, *parts1 = call(
+        first_near_kernel,
+        [pieces(4, F32)] + [pieces(4)] * 3,
+        (place, keep1, near1),
+        smem=(0,),
+        vmem=16,
+    )
+    received1 = [shifted(part, "x", by + 1) for by, part in enumerate(parts1)]
+    exchanged[1:], received2 = lax.optimization_barrier((exchanged[1:], received2))
+    exchanged[1:] = [shifted(part, "tp", by + 1) for by, part in enumerate(exchanged[1:])]
     send, keep, gain_part = call(
-        x_sum_kernel,
-        [((400, width), BF16), ((384, width), F32), small],
-        (place, own1, *received1, own2, *received2, gain_part),
-        smem=(0,),
-        moved=6 * 2**20,
+        second_x_kernel,
+        [((208, width), BF16), ((192, width), F32), small],
+        (place, own2, *received2, gain_part),
+        smem=(0,),
         vmem=16,
     )
     received = swapped(send, "z", 1)
-    (layer_out,) = call(
-        layer_kernel, [sheet], (tokens, mask_row, exchanged), moved=2 * 2**20, vmem=16
-    )
+    own, *parts, gain_part = call(
+        near_sum_kernel,
+        [((96, width), F32)] + [((112, width), BF16)] * 3 + [small],
+        (place, own1, *received1, keep, received, gain_part),
+        smem=(0,),
+        vmem=16,
+    )
+    received = [shifted(part, "z", 2 * (by + 1)) for by, part in enumerate(parts)]
+    (layer_out,) = call(layer_kernel, [sheet], (tokens, mask_row, *exchanged), vmem=16)
     (tokens_grad,) = call(
         tokens_kernel,
         [sheet],
-        (place, gain, tokens, out_grad, stats, exchanged),
-        smem=(0,),
-        moved=4 * 2**20,
-        vmem=16,
-    )
-    own, *parts, gain_part = call(
-        near_sum_kernel,
-        [((96, width), F32)] + [((112, width), BF16)] * 3 + [small],
-        (place, keep, received, gain_part),
-        smem=(0,),
-        moved=2**20,
-        vmem=16,
-    )
-    received = [shifted(part, "z", 2 * (by + 1)) for by, part in enumerate(parts)]
+        (place, gain, tokens, out_grad, stats, *exchanged),
+        smem=(0,),
+        vmem=16,
+    )
+    received[2], layer_out, tokens_grad = lax.optimization_barrier(
+        (received[2], layer_out, tokens_grad)
+    )
     out_weight_grad, qkv_grad, gain_part = call(
         far_sum_kernel,
         [((24, width), F32), ((3, 24, width), F32), ((4, width), F32)],
         (own, *received, gain_part),
-        moved=2**20,
         vmem=16,
     )
     around = [shifted(gain_part, "tp", by) for by in (1, 2, 3)]

time: 153 us -> 135 us (0.88)
  waiting for transfers between devices: 56.5 us -> 36.3 us
  starting transfers between devices: 56.8 us -> 63.5 us
  local copies, waits for them, and re-layouts: 10.9 us -> 5.28 us
    ppermute x18 -> x21, waiting for transfers between devices: 43.5 us -> 30.8 us  [shifted(): lax.ppermute(value, axis, [(i, (i + by) % size) for i in range(size)])]
    ppermute x3 -> x4, waiting for transfers between devices: 9.66 us -> 0.01 us  [swapped(): return lax.ppermute(value, axis, [(i, i ^ bit) for i in range(size)])]
    ppermute x18 -> x21, starting transfers between devices: 32.5 us -> 41.5 us  [shifted(): lax.ppermute(value, axis, [(i, (i + by) % size) for i in range(size)])]
    unnamed x30 -> x12, local copies, waits for them, and re-layouts: 8.89 us -> 3.28 us
    ppermute x3 -> x4, starting transfers between devices: 5.13 us -> 10.7 us  [swapped(): return lax.ppermute(value, axis, [(i, i ^ bit) for i in range(size)])]
    all_to_all x1 -> x0, starting transfers between devices: 5.41 us -> none  [per_device(): exchanged = lax.all_to_all(exchanged, 'tp', 0, 0, tiled=True)]
    ppermute x2, starting transfers between devices: 8.05 us -> 3.84 us  [to_next(): return lax.ppermute(value, TM, [(i, i + 1) for i in range(size - 1)])]
    ppermute x2, waiting for transfers between devices: 1.76 us -> 3.51 us  [to_previous(): return lax.ppermute(value, TM, [(i + 1, i) for i in range(size - 1)])]
  transfers between devices with their start and end apart: 26 -> 29, of which waited for: 12 -> 14; matrix products, arithmetic and copies ran while one was open for 1% -> 1% of each run, Pallas kernels for 10% -> 10%
where the time goes in v1:
time: 135 us; the launch traced here: 133 us
  starting transfers between devices  63.5 us (47%)
  waiting for transfers between devices  36.3 us (27%)
  Pallas kernels  27.1 us (20%)
  local copies, waits for them, and re-layouts  5.28 us (4%)
    ppermute x21, starting transfers between devices, shifted(): lax.ppermute(value, axis, [(i, (i + by) % size) for i in range(size)])  41.5 us
    ppermute x21, waiting for transfers between devices, shifted(): lax.ppermute(value, axis, [(i, (i + by) % size) for i in range(size)])  30.8 us
    pallas_call x15, Pallas kernels, call(): pl.pallas_call(body, out_shape=[jax.ShapeDtypeStruct(s, d) for s, d in ou...  27.1 us
    ppermute x4, starting transfers between devices, swapped(): return lax.ppermute(value, axis, [(i, i ^ bit) for i in range(size)])  10.7 us
    ppermute x2, starting transfers between devices, to_previous(): return lax.ppermute(value, TM, [(i + 1, i) for i in range(size - 1)])  7.45 us
    ppermute x2, starting transfers between devices, to_next(): return lax.ppermute(value, TM, [(i, i + 1) for i in range(size - 1)])  3.84 us
    ppermute x2, waiting for transfers between devices, to_previous(): return lax.ppermute(value, TM, [(i + 1, i) for i in range(size - 1)])  3.51 us
    unnamed x12, local copies, waits for them, and re-layouts  3.28 us
  transfers between devices with their start and end apart: 29, of which 14 were waited for; matrix products, arithmetic and copies ran while one was open for 1% of the time, Pallas kernels for 10%

profile of v1, /device:TPU:6, one launch (start us, length us, event | category | flops | bytes accessed | tf_op | source)
XLA Modules:
  0.0 133.0 jit_solution(12459403822751707384)
XLA Ops:
  3.9 2.0 %collective-permute-start.1 = (bf16[384,384]{1,0:T(8,128)(2,1)}, bf16[384,384]{1,0:T(8,128)(2,1)S(1)}, u32[]{:S(2)}, u32[]{:S(2)}) collective-permute-start(bf16[384,384]{1,0:T(8,128)(2,1)} %tokens.5), channel_id=1, source_target_pairs={{0,2},{1,3},{2,0},{3,1},{4,6},{5,7},{6,4},{7,5},{8,10},{9,11},{10,... | collective-permute-start | bytes 884744 | tf_op jit(solution)/shard_map/ppermute | solution.py:19
  7.3 2.0 %copy-done = bf16[1536,3,384]{2,0,1:T(8,128)(2,1)S(1)} copy-done((bf16[1536,3,384]{2,0,1:T(8,128)(2,1)S(1)}, bf16[1536,3,384]{2,0,1:T(8,128)(2,1)}, u32[]{:S(2)}) %copy-start) | copy-done | bytes 3538968
  11.2 2.6 %collective-permute-start.5 = (bf16[384,384]{1,0:T(8,128)(2,1)S(1)}, bf16[384,384]{1,0:T(8,128)(2,1)S(1)}, u32[]{:S(2)}, u32[]{:S(2)}) collective-permute-start(bf16[384,384]{1,0:T(8,128)(2,1)S(1)} %copy-done.5), channel_id=1, source_target_pairs={{0,3},{1,0},{2,1},{3,2},{4,7},{5,4},{6,5},{7,6},{8,11},{9,8},{10,9... | collective-permute-start | bytes 884744 | tf_op jit(solution)/shard_map/ppermute | solution.py:19
  13.8 8.5 %collective-permute-start.6 = (bf16[384,384]{1,0:T(8,128)(2,1)S(1)}, bf16[384,384]{1,0:T(8,128)(2,1)S(1)}, u32[]{:S(2)}, u32[]{:S(2)}) collective-permute-start(bf16[384,384]{1,0:T(8,128)(2,1)S(1)} %copy-done.5), channel_id=1, source_target_pairs={{0,2},{1,3},{2,0},{3,1},{4,6},{5,7},{6,4},{7,5},{8,10},{9,11},{10,... | collective-permute-start | bytes 884744 | tf_op jit(solution)/shard_map/ppermute | solution.py:19
  23.8 3.6 %shard_map.102 = (bf16[4,384,384]{2,1,0:T(8,128)(2,1)S(1)}, bf16[384,384]{1,0:T(8,128)(2,1)S(1)}, bf16[384,384]{1,0:T(8,128)(2,1)S(1)}, bf16[384,384]{1,0:T(8,12...) custom-call(s32[4]{0:T(128)S(1)} %pad_add_fusion.place, ...), custom_call_target="tpu_custom_call" | custom-call | flops 1358954496 | tf_op jit(solution)/shard_map/pallas_call | solution.py:56
  29.4 3.8 %collective-permute-start.4 = (bf16[144,768]{1,0:T(8,128)(2,1)S(1)}, bf16[144,768]{1,0:T(8,128)(2,1)S(1)}, u32[]{:S(2)}, u32[]{:S(2)}) collective-permute-start(bf16[144,768]{1,0:T(8,128)(2,1)S(1)} %get-tuple-element.80), channel_id=1, source_target_pairs={{4,0},{8,4},{12,8},{16,12},{20,16},{24,20},{28,24},{32,28},{36,32}... | collective-permute-start | bytes 663560 | tf_op jit(solution)/shard_map/ppermute | solution.py:34
  36.5 6.4 %shard_map.103 = (bf16[384,384]{1,0:T(8,128)(2,1)S(1)}, bf16[384,384]{1,0:T(8,128)(2,1)S(1)}, f32[384,768]{1,0:T(8,128)S(1)}, bf16[128,768]{1,0:T(8,128)(2,1)S(1...) custom-call(s32[4]{0:T(128)S(1)} %pad_add_fusion.place, s32[1,384]{1,0:T(1,128)S(1)} %broadcast_in_dim.3.mask, ...), custom_call_target="tpu_custom_call" | custom-call | tf_op jit(solution)/shard_map/pallas_call | solution.py:56
  42.9 2.4 %shard_map.104 = (bf16[32,48,384]{2,1,0:T(8,128)(2,1)S(1)}, bf16[32,48,384]{2,1,0:T(8,128)(2,1)S(1)}, f32[4,384,128]{2,1,0:T(8,128)S(1)}) custom-call(s32[4]{0:T(128)S(1)} %pad_add_fusion.place, bf16[4,384,384]{2,1,0:T(8,128)(2,1)S(1)} %get-tuple-element.82.gated, bf16[384,384]{1,0:T(8,128)(2,1)S(1)} %get-tuple-element.83.attended, ...), custom_call_target="tpu_custom_call" | custom-call | flops 1358954496 | tf_op jit(solution)/shard_map/pallas_call | solution.py:56
  45.3 4.3 %collective-permute-start.10 = (bf16[32,48,384]{2,1,0:T(8,128)(2,1)S(1)}, bf16[32,48,384]{2,1,0:T(8,128)(2,1)S(1)}, u32[]{:S(2)}, u32[]{:S(2)}) collective-permute-start(bf16[32,48,384]{2,1,0:T(8,128)(2,1)S(1)} %get-tuple-element.89), channel_id=1, source_target_pairs={{0,4},{4,0},{1,5},{5,1},{2,6},{6,2},{3,7},{7,3},{8,12},{12,8},{9,1... | collective-permute-start | bytes 3538952 | tf_op jit(solution)/shard_map/ppermute | solution.py:24
  51.5 3.6 %collective-permute-start.9 = (bf16[128,768]{1,0:T(8,128)(2,1)S(1)}, bf16[128,768]{1,0:T(8,128)(2,1)S(1)}, u32[]{:S(2)}, u32[]{:S(2)}) collective-permute-start(bf16[128,768]{1,0:T(8,128)(2,1)S(1)} %get-tuple-element.88), channel_id=1, source_target_pairs={{4,0},{8,4},{12,8},{16,12},{20,16},{24,20},{28,24},{32,28},{36,32}... | collective-permute-start | bytes 589832 | tf_op jit(solution)/shard_map/ppermute | solution.py:34
  58.3 2.9 %shard_map.107 = (bf16[33,48,384]{2,1,0:T(8,128)(2,1)S(1)}, bf16[32,48,384]{2,1,0:T(8,128)(2,1)S(1)}, bf16[384,384]{1,0:T(8,128)(2,1)S(1)}, bf16[384,384]{1,0:T(8,128)(2,1)S(1)}, f32[8,384]{1,0:T(8,128)S(1)}) custom-call(s32[4]{0:T(128)S(1)} %pad_add_fusion.place, f32[384,768]{1,0:T(8,128)S(1)} %get-tuple-element.92.kv_grad, ...), custom_call_target="tpu_custom_call" | custom-call | tf_op jit(solution)/shard_map/pallas_call | solution.py:56
  61.2 2.6 %collective-permute-start.15 = (bf16[33,48,384]{2,1,0:T(8,128)(2,1)S(1)}, bf16[33,48,384]{2,1,0:T(8,128)(2,1)S(1)}, u32[]{:S(2)}, u32[]{:S(2)}) collective-permute-start(bf16[33,48,384]{2,1,0:T(8,128)(2,1)S(1)} %get-tuple-element.104), channel_id=1, source_target_pairs={{0,4},{4,0},{1,5},{5,1},{2,6},{6,2},{3,7},{7,3},{8,12},{12,8},{9,1... | collective-permute-start | bytes 3649544 | tf_op jit(solution)/shard_map/ppermute | solution.py:24
  64.6 3.2 %shard_map.109 = (bf16[784,384]{1,0:T(8,128)(2,1)S(1)}, bf16[784,384]{1,0:T(8,128)(2,1)S(1)}, bf16[784,384]{1,0:T(8,128)(2,1)S(1)}, bf16[784,384]{1,0:T(8,128)(2,1)S(1)}) custom-call(s32[4]{0:T(128)S(1)} %pad_add_fusion.place, bf16[4,384,384]{2,1,0:T(8,128)(2,1)S(1)} %shard_map.105.branches, bf16[384,384]{1,0:T(8,128)(2,1)S(1)} %get-tuple-element.84.q_grad, ...), custom_call_target="tpu_custom_call" | custom-call | tf_op jit(solution)/shard_map/pallas_call | solution.py:56
  68.8 2.1 %collective-permute-start.17 = (bf16[9,48,384]{2,1,0:T(8,128)(2,1)S(1)}, bf16[9,48,384]{2,1,0:T(8,128)(2,1)S(1)}, u32[]{:S(2)}, u32[]{:S(2)}) collective-permute-start(bf16[9,48,384]{2,1,0:T(8,128)(2,1)S(1)} %get-tuple-element.116), channel_id=1, source_target_pairs={{0,16},{8,24},{16,0},{24,8},{1,17},{9,25},{17,1},{25,9},{2,18},{10... | collective-permute-start | bytes 995336 | tf_op jit(solution)/shard_map/ppermute | solution.py:19
  72.7 6.7 %collective-permute-done.16.r1 = bf16[9,48,384]{2,1,0:T(8,128)(2,1)S(1)} collective-permute-done((bf16[9,48,384]{2,1,0:T(8,128)(2,1)S(1)}, bf16[9,48,384]{2,1,0:T(8,128)(2,1)S(1)}, u32[]{:S(2)}, u32[]{:S(2)}) %collective-permute-start.16) | collective-permute-done | bytes 331808 | tf_op jit(solution)/shard_map/ppermute | solution.py:19
  81.1 6.1 %collective-permute-done.18.r3 = bf16[9,48,384]{2,1,0:T(8,128)(2,1)S(1)} collective-permute-done((bf16[9,48,384]{2,1,0:T(8,128)(2,1)S(1)}, bf16[9,48,384]{2,1,0:T(8,128)(2,1)S(1)}, u32[]{:S(2)}, u32[]{:S(2)}) %collective-permute-start.18) | collective-permute-done | bytes 331808 | tf_op jit(solution)/shard_map/ppermute | solution.py:19
  87.2 3.3 %collective-permute-start.22 = (bf16[784,384]{1,0:T(8,128)(2,1)S(1)}, bf16[784,384]{1,0:T(8,128)(2,1)S(1)}, u32[]{:S(2)}, u32[]{:S(2)}) collective-permute-start(bf16[784,384]{1,0:T(8,128)(2,1)S(1)} %get-tuple-element.128), channel_id=1, source_target_pairs={{0,2},{1,3},{2,0},{3,1},{4,6},{5,7},{6,4},{7,5},{8,10},{9,11},{10,... | collective-permute-start | bytes 1806344 | tf_op jit(solution)/shard_map/ppermute | solution.py:19
  94.2 3.8 %collective-permute-done.12.r1 = bf16[4,48,384]{2,1,0:T(8,128)(2,1)S(1)} collective-permute-done((bf16[4,48,384]{2,1,0:T(8,128)(2,1)S(1)}, bf16[4,48,384]{2,1,0:T(8,128)(2,1)S(1)}, u32[]{:S(2)}, u32[]{:S(2)}) %collective-permute-start.12) | collective-permute-done | bytes 147488 | tf_op jit(solution)/shard_map/ppermute | solution.py:19
  100.7 5.6 %collective-permute-done.14.r3 = bf16[4,48,384]{2,1,0:T(8,128)(2,1)S(1)} collective-permute-done((bf16[4,48,384]{2,1,0:T(8,128)(2,1)S(1)}, bf16[4,48,384]{2,1,0:T(8,128)(2,1)S(1)}, u32[]{:S(2)}, u32[]{:S(2)}) %collective-permute-start.14) | collective-permute-done | bytes 147488 | tf_op jit(solution)/shard_map/ppermute | solution.py:19
  107.0 4.6 %collective-permute-start.20 = (bf16[112,384]{1,0:T(8,128)(2,1)S(1)}, bf16[112,384]{1,0:T(8,128)(2,1)S(1)}, u32[]{:S(2)}, u32[]{:S(2)}) collective-permute-start(bf16[112,384]{1,0:T(8,128)(2,1)S(1)} %get-tuple-element.125), channel_id=1, source_target_pairs={{0,192},{32,224},{64,0},{96,32},{128,64},{160,96},{192,128},{224,1... | collective-permute-start | bytes 258056 | tf_op jit(solution)/shard_map/ppermute | solution.py:19
  111.5 2.8 %collective-permute-start.24 = (bf16[112,384]{1,0:T(8,128)(2,1)S(1)}, bf16[112,384]{1,0:T(8,128)(2,1)S(1)}, u32[]{:S(2)}, u32[]{:S(2)}) collective-permute-start(bf16[112,384]{1,0:T(8,128)(2,1)S(1)} %get-tuple-element.134), channel_id=1, source_target_pairs={{0,64},{32,96},{64,128},{96,160},{128,192},{160,224},{192,0},{224,... | collective-permute-start | bytes 258056 | tf_op jit(solution)/shard_map/ppermute | solution.py:19
  114.3 3.2 %collective-permute-start.25 = (bf16[112,384]{1,0:T(8,128)(2,1)S(1)}, bf16[112,384]{1,0:T(8,128)(2,1)S(1)}, u32[]{:S(2)}, u32[]{:S(2)}) collective-permute-start(bf16[112,384]{1,0:T(8,128)(2,1)S(1)} %get-tuple-element.135), channel_id=1, source_target_pairs={{0,128},{32,160},{64,192},{96,224},{128,0},{160,32},{192,64},{224,... | collective-permute-start | bytes 258056 | tf_op jit(solution)/shard_map/ppermute | solution.py:19
  120.3 3.0 %collective-permute-done.25.r2 = bf16[112,384]{1,0:T(8,128)(2,1)S(1)} collective-permute-done((bf16[112,384]{1,0:T(8,128)(2,1)S(1)}, bf16[112,384]{1,0:T(8,128)(2,1)S(1)}, u32[]{:S(2)}, u32[]{:S(2)}) %collective-permute-start.25) | collective-permute-done | bytes 86048 | tf_op jit(solution)/shard_map/ppermute | solution.py:19
  129.1 3.3 %collective-permute-done.26 = f32[4,384]{1,0:T(4,128)S(1)} collective-permute-done((f32[4,384]{1,0:T(4,128)S(1)}, f32[4,384]{1,0:T(4,128)S(1)}, u32[]{:S(2)}, u32[]{:S(2)}) %collective-permute-start.26) | collective-permute-done | bytes 6176 | tf_op jit(solution)/shard_map/ppermute | solution.py:19
  (66 shorter events, 39.9 us)
Async XLA Ops:
  0.6 10.3 %collective-permute-start.2 = (bf16[384,384]{1,0:T(8,128)(2,1)}, bf16[384,384]{1,0:T(8,128)(2,1)S(1)}, u32[]{:S(2)}, u32[]{:S(2)}) collective-permute-start(bf16[384,384]{1,0:T(8,128)(2,1)} %tokens.5), channel_id=1, source_target_pairs={{0,1},{1,2},{2,3},{3,0},{4,5},{5,6},{6,7},{7,4},{8,9},{9,10},{10,1... | collective-permute-start | bytes 884744 | tf_op jit(solution)/shard_map/ppermute | solution.py:19
  2.3 21.5 %collective-permute-start = (bf16[384,384]{1,0:T(8,128)(2,1)}, bf16[384,384]{1,0:T(8,128)(2,1)S(1)}, u32[]{:S(2)}, u32[]{:S(2)}) collective-permute-start(bf16[384,384]{1,0:T(8,128)(2,1)} %tokens.5), channel_id=1, source_target_pairs={{0,3},{1,0},{2,1},{3,2},{4,7},{5,4},{6,5},{7,6},{8,11},{9,8},{10,9... | collective-permute-start | bytes 884744 | tf_op jit(solution)/shard_map/ppermute | solution.py:19
  3.9 19.8 %collective-permute-start.1 = (bf16[384,384]{1,0:T(8,128)(2,1)}, bf16[384,384]{1,0:T(8,128)(2,1)S(1)}, u32[]{:S(2)}, u32[]{:S(2)}) collective-permute-start(bf16[384,384]{1,0:T(8,128)(2,1)} %tokens.5), channel_id=1, source_target_pairs={{0,2},{1,3},{2,0},{3,1},{4,6},{5,7},{6,4},{7,5},{8,10},{9,11},{10,... | collective-permute-start | bytes 884744 | tf_op jit(solution)/shard_map/ppermute | solution.py:19
  11.2 25.2 %collective-permute-start.5 = (bf16[384,384]{1,0:T(8,128)(2,1)S(1)}, bf16[384,384]{1,0:T(8,128)(2,1)S(1)}, u32[]{:S(2)}, u32[]{:S(2)}) collective-permute-start(bf16[384,384]{1,0:T(8,128)(2,1)S(1)} %copy-done.5), channel_id=1, source_target_pairs={{0,3},{1,0},{2,1},{3,2},{4,7},{5,4},{6,5},{7,6},{8,11},{9,8},{10,9... | collective-permute-start | bytes 884744 | tf_op jit(solution)/shard_map/ppermute | solution.py:19
  13.8 22.6 %collective-permute-start.6 = (bf16[384,384]{1,0:T(8,128)(2,1)S(1)}, bf16[384,384]{1,0:T(8,128)(2,1)S(1)}, u32[]{:S(2)}, u32[]{:S(2)}) collective-permute-start(bf16[384,384]{1,0:T(8,128)(2,1)S(1)} %copy-done.5), channel_id=1, source_target_pairs={{0,2},{1,3},{2,0},{3,1},{4,6},{5,7},{6,4},{7,5},{8,10},{9,11},{10,... | collective-permute-start | bytes 884744 | tf_op jit(solution)/shard_map/ppermute | solution.py:19
  22.3 14.1 %collective-permute-start.7 = (bf16[384,384]{1,0:T(8,128)(2,1)S(1)}, bf16[384,384]{1,0:T(8,128)(2,1)S(1)}, u32[]{:S(2)}, u32[]{:S(2)}) collective-permute-start(bf16[384,384]{1,0:T(8,128)(2,1)S(1)} %copy-done.5), channel_id=1, source_target_pairs={{0,1},{1,2},{2,3},{3,0},{4,5},{5,6},{6,7},{7,4},{8,9},{9,10},{10,1... | collective-permute-start | bytes 884744 | tf_op jit(solution)/shard_map/ppermute | solution.py:19
  27.4 7.3 %collective-permute-start.3 = (bf16[144,768]{1,0:T(8,128)(2,1)S(1)}, bf16[144,768]{1,0:T(8,128)(2,1)S(1)}, u32[]{:S(2)}, u32[]{:S(2)}) collective-permute-start(bf16[144,768]{1,0:T(8,128)(2,1)S(1)} %get-tuple-element.79), channel_id=1, source_target_pairs={{0,4},{4,8},{8,12},{12,16},{16,20},{20,24},{24,28},{28,32},{32,36}... | collective-permute-start | bytes 663560 | tf_op jit(solution)/shard_map/ppermute | solution.py:29
  29.4 7.1 %collective-permute-start.4 = (bf16[144,768]{1,0:T(8,128)(2,1)S(1)}, bf16[144,768]{1,0:T(8,128)(2,1)S(1)}, u32[]{:S(2)}, u32[]{:S(2)}) collective-permute-start(bf16[144,768]{1,0:T(8,128)(2,1)S(1)} %get-tuple-element.80), channel_id=1, source_target_pairs={{4,0},{8,4},{12,8},{16,12},{20,16},{24,20},{28,24},{32,28},{36,32}... | collective-permute-start | bytes 663560 | tf_op jit(solution)/shard_map/ppermute | solution.py:34
  45.3 13.0 %collective-permute-start.10 = (bf16[32,48,384]{2,1,0:T(8,128)(2,1)S(1)}, bf16[32,48,384]{2,1,0:T(8,128)(2,1)S(1)}, u32[]{:S(2)}, u32[]{:S(2)}) collective-permute-start(bf16[32,48,384]{2,1,0:T(8,128)(2,1)S(1)} %get-tuple-element.89), channel_id=1, source_target_pairs={{0,4},{4,0},{1,5},{5,1},{2,6},{6,2},{3,7},{7,3},{8,12},{12,8},{9,1... | collective-permute-start | bytes 3538952 | tf_op jit(solution)/shard_map/ppermute | solution.py:24
  49.6 7.0 %collective-permute-start.8 = (bf16[128,768]{1,0:T(8,128)(2,1)S(1)}, bf16[128,768]{1,0:T(8,128)(2,1)S(1)}, u32[]{:S(2)}, u32[]{:S(2)}) collective-permute-start(bf16[128,768]{1,0:T(8,128)(2,1)S(1)} %get-tuple-element.87), channel_id=1, source_target_pairs={{0,4},{4,8},{8,12},{12,16},{16,20},{20,24},{24,28},{28,32},{32,36}... | collective-permute-start | bytes 589832 | tf_op jit(solution)/shard_map/ppermute | solution.py:29
  51.5 6.8 %collective-permute-start.9 = (bf16[128,768]{1,0:T(8,128)(2,1)S(1)}, bf16[128,768]{1,0:T(8,128)(2,1)S(1)}, u32[]{:S(2)}, u32[]{:S(2)}) collective-permute-start(bf16[128,768]{1,0:T(8,128)(2,1)S(1)} %get-tuple-element.88), channel_id=1, source_target_pairs={{4,0},{8,4},{12,8},{16,12},{20,16},{24,20},{28,24},{32,28},{36,32}... | collective-permute-start | bytes 589832 | tf_op jit(solution)/shard_map/ppermute | solution.py:34
  68.7 10.7 %collective-permute-start.16 = (bf16[9,48,384]{2,1,0:T(8,128)(2,1)S(1)}, bf16[9,48,384]{2,1,0:T(8,128)(2,1)S(1)}, u32[]{:S(2)}, u32[]{:S(2)}) collective-permute-start(bf16[9,48,384]{2,1,0:T(8,128)(2,1)S(1)} %get-tuple-element.115), channel_id=1, source_target_pairs={{0,8},{8,16},{16,24},{24,0},{1,9},{9,17},{17,25},{25,1},{2,10},{10... | collective-permute-start | bytes 995336 | tf_op jit(solution)/shard_map/ppermute | solution.py:19
  68.8 12.3 %collective-permute-start.17 = (bf16[9,48,384]{2,1,0:T(8,128)(2,1)S(1)}, bf16[9,48,384]{2,1,0:T(8,128)(2,1)S(1)}, u32[]{:S(2)}, u32[]{:S(2)}) collective-permute-start(bf16[9,48,384]{2,1,0:T(8,128)(2,1)S(1)} %get-tuple-element.116), channel_id=1, source_target_pairs={{0,16},{8,24},{16,0},{24,8},{1,17},{9,25},{17,1},{25,9},{2,18},{10... | collective-permute-start | bytes 995336 | tf_op jit(solution)/shard_map/ppermute | solution.py:19
  70.8 16.4 %collective-permute-start.18 = (bf16[9,48,384]{2,1,0:T(8,128)(2,1)S(1)}, bf16[9,48,384]{2,1,0:T(8,128)(2,1)S(1)}, u32[]{:S(2)}, u32[]{:S(2)}) collective-permute-start(bf16[9,48,384]{2,1,0:T(8,128)(2,1)S(1)} %get-tuple-element.117), channel_id=1, source_target_pairs={{0,24},{8,0},{16,8},{24,16},{1,25},{9,1},{17,9},{25,17},{2,26},{10... | collective-permute-start | bytes 995336 | tf_op jit(solution)/shard_map/ppermute | solution.py:19
  70.8 19.6 %collective-permute-start.11 = (bf16[16,48,384]{2,1,0:T(8,128)(2,1)S(1)}, bf16[16,48,384]{2,1,0:T(8,128)(2,1)S(1)}, u32[]{:S(2)}, u32[]{:S(2)}) collective-permute-start(bf16[16,48,384]{2,1,0:T(8,128)(2,1)S(1)} %get-tuple-element.98), channel_id=1, source_target_pairs={{0,32},{32,0},{64,96},{96,64},{128,160},{160,128},{192,224},{224,1... | collective-permute-start | bytes 1769480 | tf_op jit(solution)/shard_map/ppermute | solution.py:24
  87.2 27.1 %collective-permute-start.21 = (bf16[784,384]{1,0:T(8,128)(2,1)S(1)}, bf16[784,384]{1,0:T(8,128)(2,1)S(1)}, u32[]{:S(2)}, u32[]{:S(2)}) collective-permute-start(bf16[784,384]{1,0:T(8,128)(2,1)S(1)} %get-tuple-element.127), channel_id=1, source_target_pairs={{0,1},{1,2},{2,3},{3,0},{4,5},{5,6},{6,7},{7,4},{8,9},{9,10},{10,1... | collective-permute-start | bytes 1806344 | tf_op jit(solution)/shard_map/ppermute | solution.py:19
  87.2 30.3 %collective-permute-start.22 = (bf16[784,384]{1,0:T(8,128)(2,1)S(1)}, bf16[784,384]{1,0:T(8,128)(2,1)S(1)}, u32[]{:S(2)}, u32[]{:S(2)}) collective-permute-start(bf16[784,384]{1,0:T(8,128)(2,1)S(1)} %get-tuple-element.128), channel_id=1, source_target_pairs={{0,2},{1,3},{2,0},{3,1},{4,6},{5,7},{6,4},{7,5},{8,10},{9,11},{10,... | collective-permute-start | bytes 1806344 | tf_op jit(solution)/shard_map/ppermute | solution.py:19
  90.5 27.1 %collective-permute-start.23 = (bf16[784,384]{1,0:T(8,128)(2,1)S(1)}, bf16[784,384]{1,0:T(8,128)(2,1)S(1)}, u32[]{:S(2)}, u32[]{:S(2)}) collective-permute-start(bf16[784,384]{1,0:T(8,128)(2,1)S(1)} %get-tuple-element.129), channel_id=1, source_target_pairs={{0,3},{1,0},{2,1},{3,2},{4,7},{5,4},{6,5},{7,6},{8,11},{9,8},{10,9... | collective-permute-start | bytes 1806344 | tf_op jit(solution)/shard_map/ppermute | solution.py:19
  91.2 6.9 %collective-permute-start.12 = (bf16[4,48,384]{2,1,0:T(8,128)(2,1)S(1)}, bf16[4,48,384]{2,1,0:T(8,128)(2,1)S(1)}, u32[]{:S(2)}, u32[]{:S(2)}) collective-permute-start(bf16[4,48,384]{2,1,0:T(8,128)(2,1)S(1)} %get-tuple-element.100), channel_id=1, source_target_pairs={{0,8},{8,16},{16,24},{24,0},{1,9},{9,17},{17,25},{25,1},{2,10},{10... | collective-permute-start | bytes 442376 | tf_op jit(solution)/shard_map/ppermute | solution.py:19
  92.3 7.6 %collective-permute-start.13 = (bf16[4,48,384]{2,1,0:T(8,128)(2,1)S(1)}, bf16[4,48,384]{2,1,0:T(8,128)(2,1)S(1)}, u32[]{:S(2)}, u32[]{:S(2)}) collective-permute-start(bf16[4,48,384]{2,1,0:T(8,128)(2,1)S(1)} %get-tuple-element.101), channel_id=1, source_target_pairs={{0,16},{8,24},{16,0},{24,8},{1,17},{9,25},{17,1},{25,9},{2,18},{10... | collective-permute-start | bytes 442376 | tf_op jit(solution)/shard_map/ppermute | solution.py:19
  98.0 8.3 %collective-permute-start.19 = (bf16[208,384]{1,0:T(8,128)(2,1)S(1)}, bf16[208,384]{1,0:T(8,128)(2,1)S(1)}, u32[]{:S(2)}, u32[]{:S(2)}) collective-permute-start(bf16[208,384]{1,0:T(8,128)(2,1)S(1)} %get-tuple-element.123), channel_id=1, source_target_pairs={{0,32},{32,0},{64,96},{96,64},{128,160},{160,128},{192,224},{224,1... | collective-permute-start | bytes 479240 | tf_op jit(solution)/shard_map/ppermute | solution.py:24
  107.0 13.4 %collective-permute-start.20 = (bf16[112,384]{1,0:T(8,128)(2,1)S(1)}, bf16[112,384]{1,0:T(8,128)(2,1)S(1)}, u32[]{:S(2)}, u32[]{:S(2)}) collective-permute-start(bf16[112,384]{1,0:T(8,128)(2,1)S(1)} %get-tuple-element.125), channel_id=1, source_target_pairs={{0,192},{32,224},{64,0},{96,32},{128,64},{160,96},{192,128},{224,1... | collective-permute-start | bytes 258056 | tf_op jit(solution)/shard_map/ppermute | solution.py:19
  111.5 8.8 %collective-permute-start.24 = (bf16[112,384]{1,0:T(8,128)(2,1)S(1)}, bf16[112,384]{1,0:T(8,128)(2,1)S(1)}, u32[]{:S(2)}, u32[]{:S(2)}) collective-permute-start(bf16[112,384]{1,0:T(8,128)(2,1)S(1)} %get-tuple-element.134), channel_id=1, source_target_pairs={{0,64},{32,96},{64,128},{96,160},{128,192},{160,224},{192,0},{224,... | collective-permute-start | bytes 258056 | tf_op jit(solution)/shard_map/ppermute | solution.py:19
  114.3 9.0 %collective-permute-start.25 = (bf16[112,384]{1,0:T(8,128)(2,1)S(1)}, bf16[112,384]{1,0:T(8,128)(2,1)S(1)}, u32[]{:S(2)}, u32[]{:S(2)}) collective-permute-start(bf16[112,384]{1,0:T(8,128)(2,1)S(1)} %get-tuple-element.135), channel_id=1, source_target_pairs={{0,128},{32,160},{64,192},{96,224},{128,0},{160,32},{192,64},{224,... | collective-permute-start | bytes 258056 | tf_op jit(solution)/shard_map/ppermute | solution.py:19
  (11 other events, 73.6 us)

commit v2 on v1

--- a/solution.py
+++ b/solution.py
@@ -22,6 +22,11 @@
 def swapped(value, axis, bit):
     size = lax.axis_size(axis)
     return lax.ppermute(value, axis, [(i, i ^ bit) for i in range(size)])
+
+
+def across(value, axis):
+    size = lax.axis_size(axis)
+    return lax.ppermute(value, axis, [(i, (i + 2 * (i % 2) - 1) % size) for i in range(size)])
 
 
 def to_next(value):
@@ -330,14 +335,7 @@
         out[rows, :] = (tokens[rows, :].astype(F32) + keep * total[rows, :]).astype(BF16)
 
 
-def core_sum(place, keep, received, outs):
-    for step, out in enumerate(outs):
-        for z in range(8):
-            which = lax.rem(place[1] + step, 4) * 8 + z
-            out[z] = (keep[which].astype(F32) + received[which].astype(F32)).astype(out.dtype)
-
-
-def first_core_kernel(place, keep, received, send, own):
+def core_sum(place, keep, received, send, own):
     parity = lax.rem(place[0], 2)
     for out, whose in ((send, 1 - parity), (own, parity)):
         for x in range(4):
@@ -347,45 +345,46 @@
                 out[4 * x + far] = total.astype(out.dtype)
 
 
-def second_core_kernel(place, keep, received, gain_part, own, p1, p2, p3, gain_sum):
-    core_sum(place, keep, received, (own, p1, p2, p3))
+def first_core_kernel(place, keep, received, send, own):
+    core_sum(place, keep, received, send, own)
+
+
+def gain_kernel(received, gain_part, gain_sum):
     gain_sum[...] = from_two(in_two(gain_part[...])) + from_two(received[32, :16, :])
-    for out in (p1, p2, p3):
-        out[8, :16, :] = in_two(gain_sum[...])
-
-
-def first_near_kernel(place, keep, received, own, p1, p2, p3):
+
+
+def second_core_kernel(place, keep, received, g0, g1, g2, g3, send, own, gain_sum):
+    core_sum(place, keep, received, send, own)
+    gain_sum[...] = (g0[...] + g2[...]) + (g1[...] + g3[...])
+    send[16, :16, :] = in_two(gain_sum[...])
+
+
+def first_near_kernel(keep, received, total):
+    for which in range(16):
+        total[which] = keep[which] + received[which].astype(F32)
+
+
+def near_kernel(place, sum1, keep, received, gain_part, own, p1, p2, p3, gain_sum):
+    gain_sum[...] = from_two(in_two(gain_part[...])) + from_two(received[16, :16, :])
     for step, out in enumerate((own, p1, p2, p3)):
         for far in range(4):
             which = lax.rem(place[1] + step, 4) * 4 + far
-            out[far] = (keep[which] + received[which].astype(F32)).astype(out.dtype)
-
-
-def second_x_kernel(place, own, r1, r2, r3, gain_part, send, keep, gain_sum):
-    parity = lax.rem(place[0], 2)
-    for out, whose in ((send, 1 - parity), (keep, parity)):
-        for far in range(4):
-            which = 2 * far + whose
-            total = own[which] + r2[which].astype(F32)
-            total = total + (r1[which].astype(F32) + r3[which].astype(F32))
-            out[48 * far : 48 * far + 48, :] = total.astype(out.dtype)
-    near = from_two(in_two(gain_part[...])) + from_two(r2[8, :16, :])
-    gain_sum[...] = near + (from_two(r1[8, :16, :]) + from_two(r3[8, :16, :]))
-    send[192:, :] = in_two(gain_sum[...])
-
-
-def near_sum_kernel(
-    place, own1, r1, r2, r3, keep, received, gain_part, own, p1, p2, p3, gain_sum
-):
-    gain_sum[...] = from_two(in_two(gain_part[...])) + from_two(received[192:, :])
+            out[96 * far : 96 * far + 48, :] = sum1[which].astype(out.dtype)
+            total = keep[which] + received[which].astype(F32)
+            out[96 * far + 48 : 96 * far + 96, :] = total.astype(out.dtype)
+        if step:
+            out[384:, :] = in_two(gain_sum[...])
+
+
+def x_sum_kernel(place, kept, r1, r2, r3, gain_part, own, p1, p2, p3, gain_sum):
+    near = from_two(in_two(gain_part[...])) + from_two(r2[384:, :])
+    gain_sum[...] = near + (from_two(r1[384:, :]) + from_two(r3[384:, :]))
     for step, out in enumerate((own, p1, p2, p3)):
         far = lax.rem(lax.div(place[0], 2) + step, 4)
-        first = own1[far] + r2[far].astype(F32)
-        first = first + (r1[far].astype(F32) + r3[far].astype(F32))
-        rows = pl.ds(pl.multiple_of(48 * far, 16), 48)
-        second = keep[rows, :] + received[rows, :].astype(F32)
-        out[:48, :] = first.astype(out.dtype)
-        out[48:96, :] = second.astype(out.dtype)
+        rows = pl.ds(pl.multiple_of(96 * far, 32), 96)
+        total = kept[rows, :] + r2[rows, :].astype(F32)
+        total = total + (r1[rows, :].astype(F32) + r3[rows, :].astype(F32))
+        out[:96, :] = total.astype(out.dtype)
         if step:
             out[96:, :] = in_two(gain_sum[...])
 
@@ -484,44 +483,40 @@
     )
     k_grad, near1 = lax.optimization_barrier((k_grad, near1))
     near1 = swapped(near1, "z", 1)
-    exchanged = [None] * 4
-    exchanged[:] = call(
+    exchanged = call(
         norm_kernel,
         [((2 * frames + 16, width), BF16)] * 4,
         (place, branches, q_grad, k_grad, v_grad, weights, normed, gain),
         smem=(0,),
     )
+    exchanged = list(exchanged)
     received2, exchanged[0] = lax.optimization_barrier((received2, exchanged[0]))
-    own2, *parts2, gain_part = call(
+    (gain_part,) = call(gain_kernel, [small], (received2, gain_part), vmem=8)
+    gains = [gain_part] + [shifted(gain_part, "tp", by) for by in (1, 2, 3)]
+    near2, keep2, gain_part = call(
         second_core_kernel,
-        [pieces(8, F32)] + [pieces(9)] * 3 + [small],
-        (place, keep2, received2, gain_part),
+        [pieces(17), pieces(16, F32), small],
+        (place, keep2, received2, *gains),
         smem=(0,),
         vmem=16,
     )
-    received2 = [shifted(part, "x", by + 1) for by, part in enumerate(parts2)]
-    own1, *parts1 = call(
-        first_near_kernel,
-        [pieces(4, F32)] + [pieces(4)] * 3,
-        (place, keep1, near1),
+    near2 = across(near2, "z")
+    (sum1,) = call(first_near_kernel, [pieces(16, F32)], (keep1, near1), vmem=16)
+    exchanged, gain_part = lax.optimization_barrier((exchanged, gain_part))
+    exchanged = list(exchanged)
+    exchanged[1:] = [shifted(part, "tp", by + 1) for by, part in enumerate(exchanged[1:])]
+    own, *parts, gain_part = call(
+        near_kernel,
+        [((384, width), F32)] + [((400, width), BF16)] * 3 + [small],
+        (place, sum1, keep2, near2, gain_part),
         smem=(0,),
         vmem=16,
     )
-    received1 = [shifted(part, "x", by + 1) for by, part in enumerate(parts1)]
-    exchanged[1:], received2 = lax.optimization_barrier((exchanged[1:], received2))
-    exchanged[1:] = [shifted(part, "tp", by + 1) for by, part in enumerate(exchanged[1:])]
-    send, keep, gain_part = call(
-        second_x_kernel,
-        [((208, width), BF16), ((192, width), F32), small],
-        (place, own2, *received2, gain_part),
-        smem=(0,),
-        vmem=16,
-    )
-    received = swapped(send, "z", 1)
+    received = [shifted(part, "x", by + 1) for by, part in enumerate(parts)]
     own, *parts, gain_part = call(
-        near_sum_kernel,
+        x_sum_kernel,
         [((96, width), F32)] + [((112, width), BF16)] * 3 + [small],
-        (place, own1, *received1, keep, received, gain_part),
+        (place, own, *received, gain_part),
         smem=(0,),
         vmem=16,
     )
@@ -537,14 +532,12 @@
     received[2], layer_out, tokens_grad = lax.optimization_barrier(
         (received[2], layer_out, tokens_grad)
     )
-    out_weight_grad, qkv_grad, gain_part = call(
+    out_weight_grad, qkv_grad, gain_grad = call(
         far_sum_kernel,
         [((24, width), F32), ((3, 24, width), F32), ((4, width), F32)],
         (own, *received, gain_part),
         vmem=16,
     )
-    around = [shifted(gain_part, "tp", by) for by in (1, 2, 3)]
-    gain_grad = (gain_part + around[1]) + (around[0] + around[2])
     return (
         layer_out,
         tokens_grad,

time: 135 us -> 131 us (0.970)
  starting transfers between devices: 63.5 us -> 58.4 us
    ppermute x4 -> x3, waiting for transfers between devices: 0.01 us -> 11.7 us  [swapped(): return lax.ppermute(value, axis, [(i, i ^ bit) for i in range(size)])]
    ppermute x21 -> x18, waiting for transfers between devices: 30.8 us -> 20 us  [shifted(): lax.ppermute(value, axis, [(i, (i + by) % size) for i in range(size)])]
    ppermute x21 -> x18, starting transfers between devices: 41.5 us -> 36.3 us  [shifted(): lax.ppermute(value, axis, [(i, (i + by) % size) for i in range(size)])]
    pallas_call x15 -> x16, Pallas kernels: 27.1 us -> 26.5 us  [call(): pl.pallas_call(body, out_shape=[jax.ShapeDtypeStruct(s, d) for s, d in ou...]
    ppermute x4 -> x3, starting transfers between devices: 10.7 us -> 10.7 us  [swapped(): return lax.ppermute(value, axis, [(i, i ^ bit) for i in range(size)])]
  transfers between devices with their start and end apart: 29 -> 26, of which waited for: 14 -> 14; matrix products, arithmetic and copies ran while one was open for 1% -> 1% of each run, Pallas kernels for 10% -> 10%
where the time goes in v2:
time: 131 us; the launch traced here: 128 us
  starting transfers between devices  58.4 us (45%)
  waiting for transfers between devices  37.1 us (28%)
  Pallas kernels  26.5 us (20%)
  local copies, waits for them, and re-layouts  5.28 us (4%)
    ppermute x18, starting transfers between devices, shifted(): lax.ppermute(value, axis, [(i, (i + by) % size) for i in range(size)])  36.3 us
    pallas_call x16, Pallas kernels, call(): pl.pallas_call(body, out_shape=[jax.ShapeDtypeStruct(s, d) for s, d in ou...  26.5 us
    ppermute x18, waiting for transfers between devices, shifted(): lax.ppermute(value, axis, [(i, (i + by) % size) for i in range(size)])  20 us
    ppermute x3, waiting for transfers between devices, swapped(): return lax.ppermute(value, axis, [(i, i ^ bit) for i in range(size)])  11.7 us
    ppermute x3, starting transfers between devices, swapped(): return lax.ppermute(value, axis, [(i, i ^ bit) for i in range(size)])  10.7 us
    ppermute x2, starting transfers between devices, to_previous(): return lax.ppermute(value, TM, [(i + 1, i) for i in range(size - 1)])  7.45 us
    ppermute x2, starting transfers between devices, to_next(): return lax.ppermute(value, TM, [(i, i + 1) for i in range(size - 1)])  3.84 us
    ppermute x2, waiting for transfers between devices, to_previous(): return lax.ppermute(value, TM, [(i + 1, i) for i in range(size - 1)])  3.51 us
  transfers between devices with their start and end apart: 26, of which 14 were waited for; matrix products, arithmetic and copies ran while one was open for 1% of the time, Pallas kernels for 10%

profile of v2, /device:TPU:6, one launch (start us, length us, event | category | flops | bytes accessed | tf_op | source)
XLA Modules:
  0.0 128.2 jit_solution(465525864226251797)
XLA Ops:
  3.9 2.0 %collective-permute-start.1 = (bf16[384,384]{1,0:T(8,128)(2,1)}, bf16[384,384]{1,0:T(8,128)(2,1)S(1)}, u32[]{:S(2)}, u32[]{:S(2)}) collective-permute-start(bf16[384,384]{1,0:T(8,128)(2,1)} %tokens.5), channel_id=1, source_target_pairs={{0,2},{1,3},{2,0},{3,1},{4,6},{5,7},{6,4},{7,5},{8,10},{9,11},{10,... | collective-permute-start | bytes 884744 | tf_op jit(solution)/shard_map/ppermute | solution.py:19
  7.3 2.0 %copy-done = bf16[1536,3,384]{2,0,1:T(8,128)(2,1)S(1)} copy-done((bf16[1536,3,384]{2,0,1:T(8,128)(2,1)S(1)}, bf16[1536,3,384]{2,0,1:T(8,128)(2,1)}, u32[]{:S(2)}) %copy-start) | copy-done | bytes 3538968
  11.2 2.6 %collective-permute-start.5 = (bf16[384,384]{1,0:T(8,128)(2,1)S(1)}, bf16[384,384]{1,0:T(8,128)(2,1)S(1)}, u32[]{:S(2)}, u32[]{:S(2)}) collective-permute-start(bf16[384,384]{1,0:T(8,128)(2,1)S(1)} %copy-done.5), channel_id=1, source_target_pairs={{0,3},{1,0},{2,1},{3,2},{4,7},{5,4},{6,5},{7,6},{8,11},{9,8},{10,9... | collective-permute-start | bytes 884744 | tf_op jit(solution)/shard_map/ppermute | solution.py:19
  13.8 8.5 %collective-permute-start.6 = (bf16[384,384]{1,0:T(8,128)(2,1)S(1)}, bf16[384,384]{1,0:T(8,128)(2,1)S(1)}, u32[]{:S(2)}, u32[]{:S(2)}) collective-permute-start(bf16[384,384]{1,0:T(8,128)(2,1)S(1)} %copy-done.5), channel_id=1, source_target_pairs={{0,2},{1,3},{2,0},{3,1},{4,6},{5,7},{6,4},{7,5},{8,10},{9,11},{10,... | collective-permute-start | bytes 884744 | tf_op jit(solution)/shard_map/ppermute | solution.py:19
  23.8 3.6 %shard_map.102 = (bf16[4,384,384]{2,1,0:T(8,128)(2,1)S(1)}, bf16[384,384]{1,0:T(8,128)(2,1)S(1)}, bf16[384,384]{1,0:T(8,128)(2,1)S(1)}, bf16[384,384]{1,0:T(8,12...) custom-call(s32[4]{0:T(128)S(1)} %pad_add_fusion.place, ...), custom_call_target="tpu_custom_call" | custom-call | flops 1358954496 | tf_op jit(solution)/shard_map/pallas_call | solution.py:61
  29.4 3.8 %collective-permute-start.4 = (bf16[144,768]{1,0:T(8,128)(2,1)S(1)}, bf16[144,768]{1,0:T(8,128)(2,1)S(1)}, u32[]{:S(2)}, u32[]{:S(2)}) collective-permute-start(bf16[144,768]{1,0:T(8,128)(2,1)S(1)} %get-tuple-element.75), channel_id=1, source_target_pairs={{4,0},{8,4},{12,8},{16,12},{20,16},{24,20},{28,24},{32,28},{36,32}... | collective-permute-start | bytes 663560 | tf_op jit(solution)/shard_map/ppermute | solution.py:39
  36.5 6.4 %shard_map.103 = (bf16[384,384]{1,0:T(8,128)(2,1)S(1)}, bf16[384,384]{1,0:T(8,128)(2,1)S(1)}, f32[384,768]{1,0:T(8,128)S(1)}, bf16[128,768]{1,0:T(8,128)(2,1)S(1...) custom-call(s32[4]{0:T(128)S(1)} %pad_add_fusion.place, s32[1,384]{1,0:T(1,128)S(1)} %broadcast_in_dim.3.mask, ...), custom_call_target="tpu_custom_call" | custom-call | tf_op jit(solution)/shard_map/pallas_call | solution.py:61
  42.9 2.4 %shard_map.104 = (bf16[32,48,384]{2,1,0:T(8,128)(2,1)S(1)}, bf16[32,48,384]{2,1,0:T(8,128)(2,1)S(1)}, f32[4,384,128]{2,1,0:T(8,128)S(1)}) custom-call(s32[4]{0:T(128)S(1)} %pad_add_fusion.place, bf16[4,384,384]{2,1,0:T(8,128)(2,1)S(1)} %get-tuple-element.77.gated, bf16[384,384]{1,0:T(8,128)(2,1)S(1)} %get-tuple-element.78.attended, ...), custom_call_target="tpu_custom_call" | custom-call | flops 1358954496 | tf_op jit(solution)/shard_map/pallas_call | solution.py:61
  45.3 4.3 %collective-permute-start.10 = (bf16[32,48,384]{2,1,0:T(8,128)(2,1)S(1)}, bf16[32,48,384]{2,1,0:T(8,128)(2,1)S(1)}, u32[]{:S(2)}, u32[]{:S(2)}) collective-permute-start(bf16[32,48,384]{2,1,0:T(8,128)(2,1)S(1)} %get-tuple-element.84), channel_id=1, source_target_pairs={{0,4},{4,0},{1,5},{5,1},{2,6},{6,2},{3,7},{7,3},{8,12},{12,8},{9,1... | collective-permute-start | bytes 3538952 | tf_op jit(solution)/shard_map/ppermute | solution.py:24
  49.6 1.9 %collective-permute-start.8 = (bf16[128,768]{1,0:T(8,128)(2,1)S(1)}, bf16[128,768]{1,0:T(8,128)(2,1)S(1)}, u32[]{:S(2)}, u32[]{:S(2)}) collective-permute-start(bf16[128,768]{1,0:T(8,128)(2,1)S(1)} %get-tuple-element.82), channel_id=1, source_target_pairs={{0,4},{4,8},{8,12},{12,16},{16,20},{20,24},{24,28},{28,32},{32,36}... | collective-permute-start | bytes 589832 | tf_op jit(solution)/shard_map/ppermute | solution.py:34
  51.5 3.6 %collective-permute-start.9 = (bf16[128,768]{1,0:T(8,128)(2,1)S(1)}, bf16[128,768]{1,0:T(8,128)(2,1)S(1)}, u32[]{:S(2)}, u32[]{:S(2)}) collective-permute-start(bf16[128,768]{1,0:T(8,128)(2,1)S(1)} %get-tuple-element.83), channel_id=1, source_target_pairs={{4,0},{8,4},{12,8},{16,12},{20,16},{24,20},{28,24},{32,28},{36,32}... | collective-permute-start | bytes 589832 | tf_op jit(solution)/shard_map/ppermute | solution.py:39
  58.3 2.8 %shard_map.107 = (bf16[33,48,384]{2,1,0:T(8,128)(2,1)S(1)}, bf16[32,48,384]{2,1,0:T(8,128)(2,1)S(1)}, bf16[384,384]{1,0:T(8,128)(2,1)S(1)}, bf16[384,384]{1,0:T(8,128)(2,1)S(1)}, f32[8,384]{1,0:T(8,128)S(1)}) custom-call(s32[4]{0:T(128)S(1)} %pad_add_fusion.place, f32[384,768]{1,0:T(8,128)S(1)} %get-tuple-element.87.kv_grad, ...), custom_call_target="tpu_custom_call" | custom-call | tf_op jit(solution)/shard_map/pallas_call | solution.py:61
  61.1 2.6 %collective-permute-start.12 = (bf16[33,48,384]{2,1,0:T(8,128)(2,1)S(1)}, bf16[33,48,384]{2,1,0:T(8,128)(2,1)S(1)}, u32[]{:S(2)}, u32[]{:S(2)}) collective-permute-start(bf16[33,48,384]{2,1,0:T(8,128)(2,1)S(1)} %get-tuple-element.95), channel_id=1, source_target_pairs={{0,4},{4,0},{1,5},{5,1},{2,6},{6,2},{3,7},{7,3},{8,12},{12,8},{9,1... | collective-permute-start | bytes 3649544 | tf_op jit(solution)/shard_map/ppermute | solution.py:24
  64.6 3.2 %shard_map.109 = (bf16[784,384]{1,0:T(8,128)(2,1)S(1)}, bf16[784,384]{1,0:T(8,128)(2,1)S(1)}, bf16[784,384]{1,0:T(8,128)(2,1)S(1)}, bf16[784,384]{1,0:T(8,128)(2,1)S(1)}) custom-call(s32[4]{0:T(128)S(1)} %pad_add_fusion.place, bf16[4,384,384]{2,1,0:T(8,128)(2,1)S(1)} %shard_map.105.branches, bf16[384,384]{1,0:T(8,128)(2,1)S(1)} %get-tuple-element.79.q_grad, ...), custom_call_target="tpu_custom_call" | custom-call | tf_op jit(solution)/shard_map/pallas_call | solution.py:61
  67.9 3.3 %collective-permute-start.14 = (f32[8,384]{1,0:T(8,128)S(1)}, f32[8,384]{1,0:T(8,128)S(1)}, u32[]{:S(2)}, u32[]{:S(2)}) collective-permute-start(f32[8,384]{1,0:T(8,128)S(1)} %shard_map.110.g0), channel_id=1, source_target_pairs={{0,2},{1,3},{2,0},{3,1},{4,6},{5,7},{6,4},{7,5},{8,10},{9,11},{10,... | collective-permute-start | bytes 36872 | tf_op jit(solution)/shard_map/ppermute | solution.py:19
  75.8 3.8 %collective-permute-start.11 = (bf16[16,48,384]{2,1,0:T(8,128)(2,1)S(1)}, bf16[16,48,384]{2,1,0:T(8,128)(2,1)S(1)}, u32[]{:S(2)}, u32[]{:S(2)}) collective-permute-start(bf16[16,48,384]{2,1,0:T(8,128)(2,1)S(1)} %get-tuple-element.93), channel_id=1, source_target_pairs={{0,32},{32,0},{64,96},{96,64},{128,160},{160,128},{192,224},{224,1... | collective-permute-start | bytes 1769480 | tf_op jit(solution)/shard_map/ppermute | solution.py:24
  79.6 11.6 %collective-permute-done.11.received = bf16[16,48,384]{2,1,0:T(8,128)(2,1)S(1)} collective-permute-done((bf16[16,48,384]{2,1,0:T(8,128)(2,1)S(1)}, bf16[16,48,384]{2,1,0:T(8,128)(2,1)S(1)}, u32[]{:S(2)}, u32[]{:S(2)}) %collective-permute-start.11) | collective-permute-done | bytes 589856 | tf_op jit(solution)/shard_map/ppermute | solution.py:24
  92.2 2.5 %collective-permute-start.17 = (bf16[400,384]{1,0:T(8,128)(2,1)S(1)}, bf16[400,384]{1,0:T(8,128)(2,1)S(1)}, u32[]{:S(2)}, u32[]{:S(2)}) collective-permute-start(bf16[400,384]{1,0:T(8,128)(2,1)S(1)} %get-tuple-element.111), channel_id=1, source_target_pairs={{0,8},{8,16},{16,24},{24,0},{1,9},{9,17},{17,25},{25,1},{2,10},{10... | collective-permute-start | bytes 921608 | tf_op jit(solution)/shard_map/ppermute | solution.py:19
  95.5 2.4 %collective-permute-start.22 = (bf16[784,384]{1,0:T(8,128)(2,1)S(1)}, bf16[784,384]{1,0:T(8,128)(2,1)S(1)}, u32[]{:S(2)}, u32[]{:S(2)}) collective-permute-start(bf16[784,384]{1,0:T(8,128)(2,1)S(1)} %get-tuple-element.118), channel_id=1, source_target_pairs={{0,2},{1,3},{2,0},{3,1},{4,6},{5,7},{6,4},{7,5},{8,10},{9,11},{10,... | collective-permute-start | bytes 1806344 | tf_op jit(solution)/shard_map/ppermute | solution.py:19
  99.1 6.6 %collective-permute-done.17.r1 = bf16[400,384]{1,0:T(8,128)(2,1)S(1)} collective-permute-done((bf16[400,384]{1,0:T(8,128)(2,1)S(1)}, bf16[400,384]{1,0:T(8,128)(2,1)S(1)}, u32[]{:S(2)}, u32[]{:S(2)}) %collective-permute-start.17) | collective-permute-done | bytes 307232 | tf_op jit(solution)/shard_map/ppermute | solution.py:19
  105.7 4.2 %collective-permute-done.18.r2 = bf16[400,384]{1,0:T(8,128)(2,1)S(1)} collective-permute-done((bf16[400,384]{1,0:T(8,128)(2,1)S(1)}, bf16[400,384]{1,0:T(8,128)(2,1)S(1)}, u32[]{:S(2)}, u32[]{:S(2)}) %collective-permute-start.18) | collective-permute-done | bytes 307232 | tf_op jit(solution)/shard_map/ppermute | solution.py:19
  109.9 4.3 %collective-permute-done.19.r3 = bf16[400,384]{1,0:T(8,128)(2,1)S(1)} collective-permute-done((bf16[400,384]{1,0:T(8,128)(2,1)S(1)}, bf16[400,384]{1,0:T(8,128)(2,1)S(1)}, u32[]{:S(2)}, u32[]{:S(2)}) %collective-permute-start.19) | collective-permute-done | bytes 307232 | tf_op jit(solution)/shard_map/ppermute | solution.py:19
  115.7 2.2 %collective-permute-start.24 = (bf16[112,384]{1,0:T(8,128)(2,1)S(1)}, bf16[112,384]{1,0:T(8,128)(2,1)S(1)}, u32[]{:S(2)}, u32[]{:S(2)}) collective-permute-start(bf16[112,384]{1,0:T(8,128)(2,1)S(1)} %get-tuple-element.124), channel_id=1, source_target_pairs={{0,64},{32,96},{64,128},{96,160},{128,192},{160,224},{192,0},{224,... | collective-permute-start | bytes 258056 | tf_op jit(solution)/shard_map/ppermute | solution.py:19
  117.9 5.1 %collective-permute-start.25 = (bf16[112,384]{1,0:T(8,128)(2,1)S(1)}, bf16[112,384]{1,0:T(8,128)(2,1)S(1)}, u32[]{:S(2)}, u32[]{:S(2)}) collective-permute-start(bf16[112,384]{1,0:T(8,128)(2,1)S(1)} %get-tuple-element.125), channel_id=1, source_target_pairs={{0,128},{32,160},{64,192},{96,224},{128,0},{160,32},{192,64},{224,... | collective-permute-start | bytes 258056 | tf_op jit(solution)/shard_map/ppermute | solution.py:19
  (60 shorter events, 31.6 us)
Async XLA Ops:
  0.6 10.3 %collective-permute-start.2 = (bf16[384,384]{1,0:T(8,128)(2,1)}, bf16[384,384]{1,0:T(8,128)(2,1)S(1)}, u32[]{:S(2)}, u32[]{:S(2)}) collective-permute-start(bf16[384,384]{1,0:T(8,128)(2,1)} %tokens.5), channel_id=1, source_target_pairs={{0,1},{1,2},{2,3},{3,0},{4,5},{5,6},{6,7},{7,4},{8,9},{9,10},{10,1... | collective-permute-start | bytes 884744 | tf_op jit(solution)/shard_map/ppermute | solution.py:19
  2.3 21.5 %collective-permute-start = (bf16[384,384]{1,0:T(8,128)(2,1)}, bf16[384,384]{1,0:T(8,128)(2,1)S(1)}, u32[]{:S(2)}, u32[]{:S(2)}) collective-permute-start(bf16[384,384]{1,0:T(8,128)(2,1)} %tokens.5), channel_id=1, source_target_pairs={{0,3},{1,0},{2,1},{3,2},{4,7},{5,4},{6,5},{7,6},{8,11},{9,8},{10,9... | collective-permute-start | bytes 884744 | tf_op jit(solution)/shard_map/ppermute | solution.py:19
  3.9 19.8 %collective-permute-start.1 = (bf16[384,384]{1,0:T(8,128)(2,1)}, bf16[384,384]{1,0:T(8,128)(2,1)S(1)}, u32[]{:S(2)}, u32[]{:S(2)}) collective-permute-start(bf16[384,384]{1,0:T(8,128)(2,1)} %tokens.5), channel_id=1, source_target_pairs={{0,2},{1,3},{2,0},{3,1},{4,6},{5,7},{6,4},{7,5},{8,10},{9,11},{10,... | collective-permute-start | bytes 884744 | tf_op jit(solution)/shard_map/ppermute | solution.py:19
  11.2 25.2 %collective-permute-start.5 = (bf16[384,384]{1,0:T(8,128)(2,1)S(1)}, bf16[384,384]{1,0:T(8,128)(2,1)S(1)}, u32[]{:S(2)}, u32[]{:S(2)}) collective-permute-start(bf16[384,384]{1,0:T(8,128)(2,1)S(1)} %copy-done.5), channel_id=1, source_target_pairs={{0,3},{1,0},{2,1},{3,2},{4,7},{5,4},{6,5},{7,6},{8,11},{9,8},{10,9... | collective-permute-start | bytes 884744 | tf_op jit(solution)/shard_map/ppermute | solution.py:19
  13.8 22.6 %collective-permute-start.6 = (bf16[384,384]{1,0:T(8,128)(2,1)S(1)}, bf16[384,384]{1,0:T(8,128)(2,1)S(1)}, u32[]{:S(2)}, u32[]{:S(2)}) collective-permute-start(bf16[384,384]{1,0:T(8,128)(2,1)S(1)} %copy-done.5), channel_id=1, source_target_pairs={{0,2},{1,3},{2,0},{3,1},{4,6},{5,7},{6,4},{7,5},{8,10},{9,11},{10,... | collective-permute-start | bytes 884744 | tf_op jit(solution)/shard_map/ppermute | solution.py:19
  22.3 14.1 %collective-permute-start.7 = (bf16[384,384]{1,0:T(8,128)(2,1)S(1)}, bf16[384,384]{1,0:T(8,128)(2,1)S(1)}, u32[]{:S(2)}, u32[]{:S(2)}) collective-permute-start(bf16[384,384]{1,0:T(8,128)(2,1)S(1)} %copy-done.5), channel_id=1, source_target_pairs={{0,1},{1,2},{2,3},{3,0},{4,5},{5,6},{6,7},{7,4},{8,9},{9,10},{10,1... | collective-permute-start | bytes 884744 | tf_op jit(solution)/shard_map/ppermute | solution.py:19
  27.4 7.3 %collective-permute-start.3 = (bf16[144,768]{1,0:T(8,128)(2,1)S(1)}, bf16[144,768]{1,0:T(8,128)(2,1)S(1)}, u32[]{:S(2)}, u32[]{:S(2)}) collective-permute-start(bf16[144,768]{1,0:T(8,128)(2,1)S(1)} %get-tuple-element.74), channel_id=1, source_target_pairs={{0,4},{4,8},{8,12},{12,16},{16,20},{20,24},{24,28},{28,32},{32,36}... | collective-permute-start | bytes 663560 | tf_op jit(solution)/shard_map/ppermute | solution.py:34
  29.4 7.1 %collective-permute-start.4 = (bf16[144,768]{1,0:T(8,128)(2,1)S(1)}, bf16[144,768]{1,0:T(8,128)(2,1)S(1)}, u32[]{:S(2)}, u32[]{:S(2)}) collective-permute-start(bf16[144,768]{1,0:T(8,128)(2,1)S(1)} %get-tuple-element.75), channel_id=1, source_target_pairs={{4,0},{8,4},{12,8},{16,12},{20,16},{24,20},{28,24},{32,28},{36,32}... | collective-permute-start | bytes 663560 | tf_op jit(solution)/shard_map/ppermute | solution.py:39
  45.3 13.0 %collective-permute-start.10 = (bf16[32,48,384]{2,1,0:T(8,128)(2,1)S(1)}, bf16[32,48,384]{2,1,0:T(8,128)(2,1)S(1)}, u32[]{:S(2)}, u32[]{:S(2)}) collective-permute-start(bf16[32,48,384]{2,1,0:T(8,128)(2,1)S(1)} %get-tuple-element.84), channel_id=1, source_target_pairs={{0,4},{4,0},{1,5},{5,1},{2,6},{6,2},{3,7},{7,3},{8,12},{12,8},{9,1... | collective-permute-start | bytes 3538952 | tf_op jit(solution)/shard_map/ppermute | solution.py:24
  49.6 7.0 %collective-permute-start.8 = (bf16[128,768]{1,0:T(8,128)(2,1)S(1)}, bf16[128,768]{1,0:T(8,128)(2,1)S(1)}, u32[]{:S(2)}, u32[]{:S(2)}) collective-permute-start(bf16[128,768]{1,0:T(8,128)(2,1)S(1)} %get-tuple-element.82), channel_id=1, source_target_pairs={{0,4},{4,8},{8,12},{12,16},{16,20},{20,24},{24,28},{28,32},{32,36}... | collective-permute-start | bytes 589832 | tf_op jit(solution)/shard_map/ppermute | solution.py:34
  51.5 6.8 %collective-permute-start.9 = (bf16[128,768]{1,0:T(8,128)(2,1)S(1)}, bf16[128,768]{1,0:T(8,128)(2,1)S(1)}, u32[]{:S(2)}, u32[]{:S(2)}) collective-permute-start(bf16[128,768]{1,0:T(8,128)(2,1)S(1)} %get-tuple-element.83), channel_id=1, source_target_pairs={{4,0},{8,4},{12,8},{16,12},{20,16},{24,20},{28,24},{32,28},{36,32}... | collective-permute-start | bytes 589832 | tf_op jit(solution)/shard_map/ppermute | solution.py:39
  61.1 6.6 %collective-permute-start.12 = (bf16[33,48,384]{2,1,0:T(8,128)(2,1)S(1)}, bf16[33,48,384]{2,1,0:T(8,128)(2,1)S(1)}, u32[]{:S(2)}, u32[]{:S(2)}) collective-permute-start(bf16[33,48,384]{2,1,0:T(8,128)(2,1)S(1)} %get-tuple-element.95), channel_id=1, source_target_pairs={{0,4},{4,0},{1,5},{5,1},{2,6},{6,2},{3,7},{7,3},{8,12},{12,8},{9,1... | collective-permute-start | bytes 3649544 | tf_op jit(solution)/shard_map/ppermute | solution.py:24
  67.9 5.3 %collective-permute-start.14 = (f32[8,384]{1,0:T(8,128)S(1)}, f32[8,384]{1,0:T(8,128)S(1)}, u32[]{:S(2)}, u32[]{:S(2)}) collective-permute-start(f32[8,384]{1,0:T(8,128)S(1)} %shard_map.110.g0), channel_id=1, source_target_pairs={{0,2},{1,3},{2,0},{3,1},{4,6},{5,7},{6,4},{7,5},{8,10},{9,11},{10,... | collective-permute-start | bytes 36872 | tf_op jit(solution)/shard_map/ppermute | solution.py:19
  75.7 15.8 %collective-permute-start.16 = (bf16[17,48,384]{2,1,0:T(8,128)(2,1)S(1)}, bf16[17,48,384]{2,1,0:T(8,128)(2,1)S(1)}, u32[]{:S(2)}, u32[]{:S(2)}) collective-permute-start(bf16[17,48,384]{2,1,0:T(8,128)(2,1)S(1)} %get-tuple-element.103), channel_id=1, source_target_pairs={{0,224},{32,64},{64,32},{96,128},{128,96},{160,192},{192,160},{224... | collective-permute-start | bytes 1880072 | tf_op jit(solution)/shard_map/ppermute | solution.py:29
  75.8 15.5 %collective-permute-start.11 = (bf16[16,48,384]{2,1,0:T(8,128)(2,1)S(1)}, bf16[16,48,384]{2,1,0:T(8,128)(2,1)S(1)}, u32[]{:S(2)}, u32[]{:S(2)}) collective-permute-start(bf16[16,48,384]{2,1,0:T(8,128)(2,1)S(1)} %get-tuple-element.93), channel_id=1, source_target_pairs={{0,32},{32,0},{64,96},{96,64},{128,160},{160,128},{192,224},{224,1... | collective-permute-start | bytes 1769480 | tf_op jit(solution)/shard_map/ppermute | solution.py:24
  92.2 13.5 %collective-permute-start.17 = (bf16[400,384]{1,0:T(8,128)(2,1)S(1)}, bf16[400,384]{1,0:T(8,128)(2,1)S(1)}, u32[]{:S(2)}, u32[]{:S(2)}) collective-permute-start(bf16[400,384]{1,0:T(8,128)(2,1)S(1)} %get-tuple-element.111), channel_id=1, source_target_pairs={{0,8},{8,16},{16,24},{24,0},{1,9},{9,17},{17,25},{25,1},{2,10},{10... | collective-permute-start | bytes 921608 | tf_op jit(solution)/shard_map/ppermute | solution.py:19
  94.7 23.2 %collective-permute-start.21 = (bf16[784,384]{1,0:T(8,128)(2,1)S(1)}, bf16[784,384]{1,0:T(8,128)(2,1)S(1)}, u32[]{:S(2)}, u32[]{:S(2)}) collective-permute-start(bf16[784,384]{1,0:T(8,128)(2,1)S(1)} %get-tuple-element.117), channel_id=1, source_target_pairs={{0,1},{1,2},{2,3},{3,0},{4,5},{5,6},{6,7},{7,4},{8,9},{9,10},{10,1... | collective-permute-start | bytes 1806344 | tf_op jit(solution)/shard_map/ppermute | solution.py:19
  95.5 27.5 %collective-permute-start.22 = (bf16[784,384]{1,0:T(8,128)(2,1)S(1)}, bf16[784,384]{1,0:T(8,128)(2,1)S(1)}, u32[]{:S(2)}, u32[]{:S(2)}) collective-permute-start(bf16[784,384]{1,0:T(8,128)(2,1)S(1)} %get-tuple-element.118), channel_id=1, source_target_pairs={{0,2},{1,3},{2,0},{3,1},{4,6},{5,7},{6,4},{7,5},{8,10},{9,11},{10,... | collective-permute-start | bytes 1806344 | tf_op jit(solution)/shard_map/ppermute | solution.py:19
  97.9 25.1 %collective-permute-start.23 = (bf16[784,384]{1,0:T(8,128)(2,1)S(1)}, bf16[784,384]{1,0:T(8,128)(2,1)S(1)}, u32[]{:S(2)}, u32[]{:S(2)}) collective-permute-start(bf16[784,384]{1,0:T(8,128)(2,1)S(1)} %get-tuple-element.119), channel_id=1, source_target_pairs={{0,3},{1,0},{2,1},{3,2},{4,7},{5,4},{6,5},{7,6},{8,11},{9,8},{10,9... | collective-permute-start | bytes 1806344 | tf_op jit(solution)/shard_map/ppermute | solution.py:19
  99.1 10.8 %collective-permute-start.18 = (bf16[400,384]{1,0:T(8,128)(2,1)S(1)}, bf16[400,384]{1,0:T(8,128)(2,1)S(1)}, u32[]{:S(2)}, u32[]{:S(2)}) collective-permute-start(bf16[400,384]{1,0:T(8,128)(2,1)S(1)} %get-tuple-element.112), channel_id=1, source_target_pairs={{0,16},{8,24},{16,0},{24,8},{1,17},{9,25},{17,1},{25,9},{2,18},{10... | collective-permute-start | bytes 921608 | tf_op jit(solution)/shard_map/ppermute | solution.py:19
  105.7 8.5 %collective-permute-start.19 = (bf16[400,384]{1,0:T(8,128)(2,1)S(1)}, bf16[400,384]{1,0:T(8,128)(2,1)S(1)}, u32[]{:S(2)}, u32[]{:S(2)}) collective-permute-start(bf16[400,384]{1,0:T(8,128)(2,1)S(1)} %get-tuple-element.113), channel_id=1, source_target_pairs={{0,24},{8,0},{16,8},{24,16},{1,25},{9,1},{17,9},{25,17},{2,26},{10... | collective-permute-start | bytes 921608 | tf_op jit(solution)/shard_map/ppermute | solution.py:19
  114.9 10.9 %collective-permute-start.20 = (bf16[112,384]{1,0:T(8,128)(2,1)S(1)}, bf16[112,384]{1,0:T(8,128)(2,1)S(1)}, u32[]{:S(2)}, u32[]{:S(2)}) collective-permute-start(bf16[112,384]{1,0:T(8,128)(2,1)S(1)} %get-tuple-element.115), channel_id=1, source_target_pairs={{0,192},{32,224},{64,0},{96,32},{128,64},{160,96},{192,128},{224,1... | collective-permute-start | bytes 258056 | tf_op jit(solution)/shard_map/ppermute | solution.py:19
  115.7 10.1 %collective-permute-start.24 = (bf16[112,384]{1,0:T(8,128)(2,1)S(1)}, bf16[112,384]{1,0:T(8,128)(2,1)S(1)}, u32[]{:S(2)}, u32[]{:S(2)}) collective-permute-start(bf16[112,384]{1,0:T(8,128)(2,1)S(1)} %get-tuple-element.124), channel_id=1, source_target_pairs={{0,64},{32,96},{64,128},{96,160},{128,192},{160,224},{192,0},{224,... | collective-permute-start | bytes 258056 | tf_op jit(solution)/shard_map/ppermute | solution.py:19
  117.9 9.0 %collective-permute-start.25 = (bf16[112,384]{1,0:T(8,128)(2,1)S(1)}, bf16[112,384]{1,0:T(8,128)(2,1)S(1)}, u32[]{:S(2)}, u32[]{:S(2)}) collective-permute-start(bf16[112,384]{1,0:T(8,128)(2,1)S(1)} %get-tuple-element.125), channel_id=1, source_target_pairs={{0,128},{32,160},{64,192},{96,224},{128,0},{160,32},{192,64},{224,... | collective-permute-start | bytes 258056 | tf_op jit(solution)/shard_map/ppermute | solution.py:19
  (8 other events, 62.6 us)

commit v3 on v2

--- a/solution.py
+++ b/solution.py
@@ -513,6 +513,7 @@
         vmem=16,
     )
     received = [shifted(part, "x", by + 1) for by, part in enumerate(parts)]
+    received[2], exchanged[2] = lax.optimization_barrier((received[2], exchanged[2]))
     own, *parts, gain_part = call(
         x_sum_kernel,
         [((96, width), F32)] + [((112, width), BF16)] * 3 + [small],

time: 131 us -> 129 us (0.985)
  the two profiles are of different devices: /device:TPU:6 before, /device:TPU:96 now
where the time goes in v3:
time: 129 us; the launch traced here: 128 us
  starting transfers between devices  57 us (44%)
  waiting for transfers between devices  38.7 us (30%)
  Pallas kernels  26.5 us (21%)
  local copies, waits for them, and re-layouts  5.28 us (4%)
    ppermute x18, starting transfers between devices, shifted(): lax.ppermute(value, axis, [(i, (i + by) % size) for i in range(size)])  35.3 us
    pallas_call x16, Pallas kernels, call(): pl.pallas_call(body, out_shape=[jax.ShapeDtypeStruct(s, d) for s, d in ou...  26.5 us
    ppermute x18, waiting for transfers between devices, shifted(): lax.ppermute(value, axis, [(i, (i + by) % size) for i in range(size)])  22.7 us
    ppermute x2, starting transfers between devices, to_previous(): return lax.ppermute(value, TM, [(i + 1, i) for i in range(size - 1)])  11.4 us
    ppermute x3, waiting for transfers between devices, swapped(): return lax.ppermute(value, axis, [(i, i ^ bit) for i in range(size)])  10.5 us
    ppermute x1, starting transfers between devices, across(): lax.ppermute(value, axis, [(i, (i + 2 * (i % 2) - 1) % size) for i in ran...  5.63 us
    ppermute x2, starting transfers between devices, to_next(): return lax.ppermute(value, TM, [(i, i + 1) for i in range(size - 1)])  4.31 us
    ppermute x2, waiting for transfers between devices, to_previous(): return lax.ppermute(value, TM, [(i + 1, i) for i in range(size - 1)])  3.51 us
  transfers between devices with their start and end apart: 26, of which 13 were waited for; matrix products, arithmetic and copies ran while one was open for 1% of the time, Pallas kernels for 10%

profile of v3, /device:TPU:96, one launch (start us, length us, event | category | flops | bytes accessed | tf_op | source)
XLA Modules:
  0.0 128.4 jit_solution(3061060950158027353)
XLA Ops:
  3.9 2.0 %collective-permute-start.1 = (bf16[384,384]{1,0:T(8,128)(2,1)}, bf16[384,384]{1,0:T(8,128)(2,1)S(1)}, u32[]{:S(2)}, u32[]{:S(2)}) collective-permute-start(bf16[384,384]{1,0:T(8,128)(2,1)} %tokens.5), channel_id=1, source_target_pairs={{0,2},{1,3},{2,0},{3,1},{4,6},{5,7},{6,4},{7,5},{8,10},{9,11},{10,... | collective-permute-start | bytes 884744 | tf_op jit(solution)/shard_map/ppermute | solution.py:19
  7.3 2.0 %copy-done = bf16[1536,3,384]{2,0,1:T(8,128)(2,1)S(1)} copy-done((bf16[1536,3,384]{2,0,1:T(8,128)(2,1)S(1)}, bf16[1536,3,384]{2,0,1:T(8,128)(2,1)}, u32[]{:S(2)}) %copy-start) | copy-done | bytes 3538968
  11.2 2.6 %collective-permute-start.5 = (bf16[384,384]{1,0:T(8,128)(2,1)S(1)}, bf16[384,384]{1,0:T(8,128)(2,1)S(1)}, u32[]{:S(2)}, u32[]{:S(2)}) collective-permute-start(bf16[384,384]{1,0:T(8,128)(2,1)S(1)} %copy-done.5), channel_id=1, source_target_pairs={{0,3},{1,0},{2,1},{3,2},{4,7},{5,4},{6,5},{7,6},{8,11},{9,8},{10,9... | collective-permute-start | bytes 884744 | tf_op jit(solution)/shard_map/ppermute | solution.py:19
  13.8 8.5 %collective-permute-start.6 = (bf16[384,384]{1,0:T(8,128)(2,1)S(1)}, bf16[384,384]{1,0:T(8,128)(2,1)S(1)}, u32[]{:S(2)}, u32[]{:S(2)}) collective-permute-start(bf16[384,384]{1,0:T(8,128)(2,1)S(1)} %copy-done.5), channel_id=1, source_target_pairs={{0,2},{1,3},{2,0},{3,1},{4,6},{5,7},{6,4},{7,5},{8,10},{9,11},{10,... | collective-permute-start | bytes 884744 | tf_op jit(solution)/shard_map/ppermute | solution.py:19
  23.8 3.6 %shard_map.102 = (bf16[4,384,384]{2,1,0:T(8,128)(2,1)S(1)}, bf16[384,384]{1,0:T(8,128)(2,1)S(1)}, bf16[384,384]{1,0:T(8,128)(2,1)S(1)}, bf16[384,384]{1,0:T(8,12...) custom-call(s32[4]{0:T(128)S(1)} %pad_add_fusion.place, ...), custom_call_target="tpu_custom_call" | custom-call | flops 1358954496 | tf_op jit(solution)/shard_map/pallas_call | solution.py:61
  27.4 1.9 %collective-permute-start.3 = (bf16[144,768]{1,0:T(8,128)(2,1)S(1)}, bf16[144,768]{1,0:T(8,128)(2,1)S(1)}, u32[]{:S(2)}, u32[]{:S(2)}) collective-permute-start(bf16[144,768]{1,0:T(8,128)(2,1)S(1)} %get-tuple-element.76), channel_id=1, source_target_pairs={{0,4},{4,8},{8,12},{12,16},{16,20},{20,24},{24,28},{28,32},{32,36}... | collective-permute-start | bytes 663560 | tf_op jit(solution)/shard_map/ppermute | solution.py:34
  29.4 5.9 %collective-permute-start.4 = (bf16[144,768]{1,0:T(8,128)(2,1)S(1)}, bf16[144,768]{1,0:T(8,128)(2,1)S(1)}, u32[]{:S(2)}, u32[]{:S(2)}) collective-permute-start(bf16[144,768]{1,0:T(8,128)(2,1)S(1)} %get-tuple-element.77), channel_id=1, source_target_pairs={{4,0},{8,4},{12,8},{16,12},{20,16},{24,20},{28,24},{32,28},{36,32}... | collective-permute-start | bytes 663560 | tf_op jit(solution)/shard_map/ppermute | solution.py:39
  36.8 1.8 %collective-permute-done.4.kv_next = bf16[144,768]{1,0:T(8,128)(2,1)S(1)} collective-permute-done((bf16[144,768]{1,0:T(8,128)(2,1)S(1)}, bf16[144,768]{1,0:T(8,128)(2,1)S(1)}, u32[]{:S(2)}, u32[]{:S(2)}) %collective-permute-start.4) | collective-permute-done | bytes 221216 | tf_op jit(solution)/shard_map/ppermute | solution.py:39
  38.6 6.4 %shard_map.103 = (bf16[384,384]{1,0:T(8,128)(2,1)S(1)}, bf16[384,384]{1,0:T(8,128)(2,1)S(1)}, f32[384,768]{1,0:T(8,128)S(1)}, bf16[128,768]{1,0:T(8,128)(2,1)S(1...) custom-call(s32[4]{0:T(128)S(1)} %pad_add_fusion.place, s32[1,384]{1,0:T(1,128)S(1)} %broadcast_in_dim.3.mask, ...), custom_call_target="tpu_custom_call" | custom-call | tf_op jit(solution)/shard_map/pallas_call | solution.py:61
  45.0 2.4 %shard_map.104 = (bf16[32,48,384]{2,1,0:T(8,128)(2,1)S(1)}, bf16[32,48,384]{2,1,0:T(8,128)(2,1)S(1)}, f32[4,384,128]{2,1,0:T(8,128)S(1)}) custom-call(s32[4]{0:T(128)S(1)} %pad_add_fusion.place, bf16[4,384,384]{2,1,0:T(8,128)(2,1)S(1)} %get-tuple-element.79.gated, bf16[384,384]{1,0:T(8,128)(2,1)S(1)} %get-tuple-element.80.attended, ...), custom_call_target="tpu_custom_call" | custom-call | flops 1358954496 | tf_op jit(solution)/shard_map/pallas_call | solution.py:61
  47.5 2.4 %collective-permute-start.8 = (bf16[128,768]{1,0:T(8,128)(2,1)S(1)}, bf16[128,768]{1,0:T(8,128)(2,1)S(1)}, u32[]{:S(2)}, u32[]{:S(2)}) collective-permute-start(bf16[128,768]{1,0:T(8,128)(2,1)S(1)} %get-tuple-element.84), channel_id=1, source_target_pairs={{0,4},{4,8},{8,12},{12,16},{16,20},{20,24},{24,28},{28,32},{32,36}... | collective-permute-start | bytes 589832 | tf_op jit(solution)/shard_map/ppermute | solution.py:34
  49.9 5.4 %collective-permute-start.9 = (bf16[128,768]{1,0:T(8,128)(2,1)S(1)}, bf16[128,768]{1,0:T(8,128)(2,1)S(1)}, u32[]{:S(2)}, u32[]{:S(2)}) collective-permute-start(bf16[128,768]{1,0:T(8,128)(2,1)S(1)} %get-tuple-element.85), channel_id=1, source_target_pairs={{4,0},{8,4},{12,8},{16,12},{20,16},{24,20},{28,24},{32,28},{36,32}... | collective-permute-start | bytes 589832 | tf_op jit(solution)/shard_map/ppermute | solution.py:39
  58.5 2.8 %shard_map.107 = (bf16[33,48,384]{2,1,0:T(8,128)(2,1)S(1)}, bf16[32,48,384]{2,1,0:T(8,128)(2,1)S(1)}, bf16[384,384]{1,0:T(8,128)(2,1)S(1)}, bf16[384,384]{1,0:T(8,128)(2,1)S(1)}, f32[8,384]{1,0:T(8,128)S(1)}) custom-call(s32[4]{0:T(128)S(1)} %pad_add_fusion.place, f32[384,768]{1,0:T(8,128)S(1)} %get-tuple-element.89.kv_grad, ...), custom_call_target="tpu_custom_call" | custom-call | tf_op jit(solution)/shard_map/pallas_call | solution.py:61
  62.5 3.2 %shard_map.109 = (bf16[784,384]{1,0:T(8,128)(2,1)S(1)}, bf16[784,384]{1,0:T(8,128)(2,1)S(1)}, bf16[784,384]{1,0:T(8,128)(2,1)S(1)}, bf16[784,384]{1,0:T(8,128)(2,1)S(1)}) custom-call(s32[4]{0:T(128)S(1)} %pad_add_fusion.place, bf16[4,384,384]{2,1,0:T(8,128)(2,1)S(1)} %shard_map.105.branches, bf16[384,384]{1,0:T(8,128)(2,1)S(1)} %get-tuple-element.81.q_grad, ...), custom_call_target="tpu_custom_call" | custom-call | tf_op jit(solution)/shard_map/pallas_call | solution.py:61
  65.8 3.3 %collective-permute-start.14 = (f32[8,384]{1,0:T(8,128)S(1)}, f32[8,384]{1,0:T(8,128)S(1)}, u32[]{:S(2)}, u32[]{:S(2)}) collective-permute-start(f32[8,384]{1,0:T(8,128)S(1)} %shard_map.110.g0), channel_id=1, source_target_pairs={{0,2},{1,3},{2,0},{3,1},{4,6},{5,7},{6,4},{7,5},{8,10},{9,11},{10,... | collective-permute-start | bytes 36872 | tf_op jit(solution)/shard_map/ppermute | solution.py:19
  73.6 5.6 %collective-permute-start.16 = (bf16[17,48,384]{2,1,0:T(8,128)(2,1)S(1)}, bf16[17,48,384]{2,1,0:T(8,128)(2,1)S(1)}, u32[]{:S(2)}, u32[]{:S(2)}) collective-permute-start(bf16[17,48,384]{2,1,0:T(8,128)(2,1)S(1)} %get-tuple-element.105), channel_id=1, source_target_pairs={{0,224},{32,64},{64,32},{96,128},{128,96},{160,192},{192,160},{224... | collective-permute-start | bytes 1880072 | tf_op jit(solution)/shard_map/ppermute | solution.py:29
  81.6 2.4 %collective-permute-start.23 = (bf16[784,384]{1,0:T(8,128)(2,1)S(1)}, bf16[784,384]{1,0:T(8,128)(2,1)S(1)}, u32[]{:S(2)}, u32[]{:S(2)}) collective-permute-start(bf16[784,384]{1,0:T(8,128)(2,1)S(1)} %get-tuple-element.123), channel_id=1, source_target_pairs={{0,3},{1,0},{2,1},{3,2},{4,7},{5,4},{6,5},{7,6},{8,11},{9,8},{10,9... | collective-permute-start | bytes 1806344 | tf_op jit(solution)/shard_map/ppermute | solution.py:19
  84.0 10.5 %collective-permute-done.11.received = bf16[16,48,384]{2,1,0:T(8,128)(2,1)S(1)} collective-permute-done((bf16[16,48,384]{2,1,0:T(8,128)(2,1)S(1)}, bf16[16,48,384]{2,1,0:T(8,128)(2,1)S(1)}, u32[]{:S(2)}, u32[]{:S(2)}) %collective-permute-start.11) | collective-permute-done | bytes 589856 | tf_op jit(solution)/shard_map/ppermute | solution.py:24
  95.4 3.3 %collective-permute-start.19 = (bf16[400,384]{1,0:T(8,128)(2,1)S(1)}, bf16[400,384]{1,0:T(8,128)(2,1)S(1)}, u32[]{:S(2)}, u32[]{:S(2)}) collective-permute-start(bf16[400,384]{1,0:T(8,128)(2,1)S(1)} %get-tuple-element.115), channel_id=1, source_target_pairs={{0,24},{8,0},{16,8},{24,16},{1,25},{9,1},{17,9},{25,17},{2,26},{10... | collective-permute-start | bytes 921608 | tf_op jit(solution)/shard_map/ppermute | solution.py:19
  100.2 9.2 %collective-permute-done.19.r3 = bf16[400,384]{1,0:T(8,128)(2,1)S(1)} collective-permute-done((bf16[400,384]{1,0:T(8,128)(2,1)S(1)}, bf16[400,384]{1,0:T(8,128)(2,1)S(1)}, u32[]{:S(2)}, u32[]{:S(2)}) %collective-permute-start.19) | collective-permute-done | bytes 307232 | tf_op jit(solution)/shard_map/ppermute | solution.py:19
  109.4 3.4 %collective-permute-done.17.r1 = bf16[400,384]{1,0:T(8,128)(2,1)S(1)} collective-permute-done((bf16[400,384]{1,0:T(8,128)(2,1)S(1)}, bf16[400,384]{1,0:T(8,128)(2,1)S(1)}, u32[]{:S(2)}, u32[]{:S(2)}) %collective-permute-start.17) | collective-permute-done | bytes 307232 | tf_op jit(solution)/shard_map/ppermute | solution.py:19
  113.7 4.1 %collective-permute-start.24 = (bf16[112,384]{1,0:T(8,128)(2,1)S(1)}, bf16[112,384]{1,0:T(8,128)(2,1)S(1)}, u32[]{:S(2)}, u32[]{:S(2)}) collective-permute-start(bf16[112,384]{1,0:T(8,128)(2,1)S(1)} %get-tuple-element.128), channel_id=1, source_target_pairs={{0,64},{32,96},{64,128},{96,160},{128,192},{160,224},{192,0},{224,... | collective-permute-start | bytes 258056 | tf_op jit(solution)/shard_map/ppermute | solution.py:19
  119.0 1.8 %shard_map.115 = bf16[384,384]{1,0:T(8,128)(2,1)} custom-call(s32[4]{0:T(128)S(1)} %pad_add_fusion.place, f32[4,1,384]{2,1,0:T(1,128)S(1)} %reshape.16.gain, bf16[384,384]{1,0:T(8,128)(2,1)S(1)} %copy-done.4, bf16[384,384]{1,0:T(8,128)(2,1)S(1)} %copy-done.5, f32[384,128]{1,0:T(8,128)S(1)} %get-tuple-element.124.stats, ...), custom_call_target="tpu_custom_call" | custom-call | tf_op jit(solution)/shard_map/pallas_call | solution.py:61
  121.4 5.7 %collective-permute-done.25.r2 = bf16[112,384]{1,0:T(8,128)(2,1)S(1)} collective-permute-done((bf16[112,384]{1,0:T(8,128)(2,1)S(1)}, bf16[112,384]{1,0:T(8,128)(2,1)S(1)}, u32[]{:S(2)}, u32[]{:S(2)}) %collective-permute-start.25) | collective-permute-done | bytes 86048 | tf_op jit(solution)/shard_map/ppermute | solution.py:19
  (60 shorter events, 27.2 us)
Async XLA Ops:
  0.6 10.3 %collective-permute-start.2 = (bf16[384,384]{1,0:T(8,128)(2,1)}, bf16[384,384]{1,0:T(8,128)(2,1)S(1)}, u32[]{:S(2)}, u32[]{:S(2)}) collective-permute-start(bf16[384,384]{1,0:T(8,128)(2,1)} %tokens.5), channel_id=1, source_target_pairs={{0,1},{1,2},{2,3},{3,0},{4,5},{5,6},{6,7},{7,4},{8,9},{9,10},{10,1... | collective-permute-start | bytes 884744 | tf_op jit(solution)/shard_map/ppermute | solution.py:19
  2.3 21.5 %collective-permute-start = (bf16[384,384]{1,0:T(8,128)(2,1)}, bf16[384,384]{1,0:T(8,128)(2,1)S(1)}, u32[]{:S(2)}, u32[]{:S(2)}) collective-permute-start(bf16[384,384]{1,0:T(8,128)(2,1)} %tokens.5), channel_id=1, source_target_pairs={{0,3},{1,0},{2,1},{3,2},{4,7},{5,4},{6,5},{7,6},{8,11},{9,8},{10,9... | collective-permute-start | bytes 884744 | tf_op jit(solution)/shard_map/ppermute | solution.py:19
  3.9 19.8 %collective-permute-start.1 = (bf16[384,384]{1,0:T(8,128)(2,1)}, bf16[384,384]{1,0:T(8,128)(2,1)S(1)}, u32[]{:S(2)}, u32[]{:S(2)}) collective-permute-start(bf16[384,384]{1,0:T(8,128)(2,1)} %tokens.5), channel_id=1, source_target_pairs={{0,2},{1,3},{2,0},{3,1},{4,6},{5,7},{6,4},{7,5},{8,10},{9,11},{10,... | collective-permute-start | bytes 884744 | tf_op jit(solution)/shard_map/ppermute | solution.py:19
  11.2 27.3 %collective-permute-start.5 = (bf16[384,384]{1,0:T(8,128)(2,1)S(1)}, bf16[384,384]{1,0:T(8,128)(2,1)S(1)}, u32[]{:S(2)}, u32[]{:S(2)}) collective-permute-start(bf16[384,384]{1,0:T(8,128)(2,1)S(1)} %copy-done.5), channel_id=1, source_target_pairs={{0,3},{1,0},{2,1},{3,2},{4,7},{5,4},{6,5},{7,6},{8,11},{9,8},{10,9... | collective-permute-start | bytes 884744 | tf_op jit(solution)/shard_map/ppermute | solution.py:19
  13.8 24.7 %collective-permute-start.6 = (bf16[384,384]{1,0:T(8,128)(2,1)S(1)}, bf16[384,384]{1,0:T(8,128)(2,1)S(1)}, u32[]{:S(2)}, u32[]{:S(2)}) collective-permute-start(bf16[384,384]{1,0:T(8,128)(2,1)S(1)} %copy-done.5), channel_id=1, source_target_pairs={{0,2},{1,3},{2,0},{3,1},{4,6},{5,7},{6,4},{7,5},{8,10},{9,11},{10,... | collective-permute-start | bytes 884744 | tf_op jit(solution)/shard_map/ppermute | solution.py:19
  22.3 16.2 %collective-permute-start.7 = (bf16[384,384]{1,0:T(8,128)(2,1)S(1)}, bf16[384,384]{1,0:T(8,128)(2,1)S(1)}, u32[]{:S(2)}, u32[]{:S(2)}) collective-permute-start(bf16[384,384]{1,0:T(8,128)(2,1)S(1)} %copy-done.5), channel_id=1, source_target_pairs={{0,1},{1,2},{2,3},{3,0},{4,5},{5,6},{6,7},{7,4},{8,9},{9,10},{10,1... | collective-permute-start | bytes 884744 | tf_op jit(solution)/shard_map/ppermute | solution.py:19
  27.4 9.4 %collective-permute-start.3 = (bf16[144,768]{1,0:T(8,128)(2,1)S(1)}, bf16[144,768]{1,0:T(8,128)(2,1)S(1)}, u32[]{:S(2)}, u32[]{:S(2)}) collective-permute-start(bf16[144,768]{1,0:T(8,128)(2,1)S(1)} %get-tuple-element.76), channel_id=1, source_target_pairs={{0,4},{4,8},{8,12},{12,16},{16,20},{20,24},{24,28},{28,32},{32,36}... | collective-permute-start | bytes 663560 | tf_op jit(solution)/shard_map/ppermute | solution.py:34
  29.4 9.2 %collective-permute-start.4 = (bf16[144,768]{1,0:T(8,128)(2,1)S(1)}, bf16[144,768]{1,0:T(8,128)(2,1)S(1)}, u32[]{:S(2)}, u32[]{:S(2)}) collective-permute-start(bf16[144,768]{1,0:T(8,128)(2,1)S(1)} %get-tuple-element.77), channel_id=1, source_target_pairs={{4,0},{8,4},{12,8},{16,12},{20,16},{24,20},{28,24},{32,28},{36,32}... | collective-permute-start | bytes 663560 | tf_op jit(solution)/shard_map/ppermute | solution.py:39
  47.4 11.1 %collective-permute-start.10 = (bf16[32,48,384]{2,1,0:T(8,128)(2,1)S(1)}, bf16[32,48,384]{2,1,0:T(8,128)(2,1)S(1)}, u32[]{:S(2)}, u32[]{:S(2)}) collective-permute-start(bf16[32,48,384]{2,1,0:T(8,128)(2,1)S(1)} %get-tuple-element.86), channel_id=1, source_target_pairs={{0,4},{4,0},{1,5},{5,1},{2,6},{6,2},{3,7},{7,3},{8,12},{12,8},{9,1... | collective-permute-start | bytes 3538952 | tf_op jit(solution)/shard_map/ppermute | solution.py:24
  47.5 9.3 %collective-permute-start.8 = (bf16[128,768]{1,0:T(8,128)(2,1)S(1)}, bf16[128,768]{1,0:T(8,128)(2,1)S(1)}, u32[]{:S(2)}, u32[]{:S(2)}) collective-permute-start(bf16[128,768]{1,0:T(8,128)(2,1)S(1)} %get-tuple-element.84), channel_id=1, source_target_pairs={{0,4},{4,8},{8,12},{12,16},{16,20},{20,24},{24,28},{28,32},{32,36}... | collective-permute-start | bytes 589832 | tf_op jit(solution)/shard_map/ppermute | solution.py:34
  49.9 8.6 %collective-permute-start.9 = (bf16[128,768]{1,0:T(8,128)(2,1)S(1)}, bf16[128,768]{1,0:T(8,128)(2,1)S(1)}, u32[]{:S(2)}, u32[]{:S(2)}) collective-permute-start(bf16[128,768]{1,0:T(8,128)(2,1)S(1)} %get-tuple-element.85), channel_id=1, source_target_pairs={{4,0},{8,4},{12,8},{16,12},{20,16},{24,20},{28,24},{32,28},{36,32}... | collective-permute-start | bytes 589832 | tf_op jit(solution)/shard_map/ppermute | solution.py:39
  65.7 5.0 %collective-permute-start.13 = (f32[8,384]{1,0:T(8,128)S(1)}, f32[8,384]{1,0:T(8,128)S(1)}, u32[]{:S(2)}, u32[]{:S(2)}) collective-permute-start(f32[8,384]{1,0:T(8,128)S(1)} %shard_map.110.g0), channel_id=1, source_target_pairs={{0,1},{1,2},{2,3},{3,0},{4,5},{5,6},{6,7},{7,4},{8,9},{9,10},{10,1... | collective-permute-start | bytes 36872 | tf_op jit(solution)/shard_map/ppermute | solution.py:19
  65.8 5.3 %collective-permute-start.14 = (f32[8,384]{1,0:T(8,128)S(1)}, f32[8,384]{1,0:T(8,128)S(1)}, u32[]{:S(2)}, u32[]{:S(2)}) collective-permute-start(f32[8,384]{1,0:T(8,128)S(1)} %shard_map.110.g0), channel_id=1, source_target_pairs={{0,2},{1,3},{2,0},{3,1},{4,6},{5,7},{6,4},{7,5},{8,10},{9,11},{10,... | collective-permute-start | bytes 36872 | tf_op jit(solution)/shard_map/ppermute | solution.py:19
  73.6 21.0 %collective-permute-start.16 = (bf16[17,48,384]{2,1,0:T(8,128)(2,1)S(1)}, bf16[17,48,384]{2,1,0:T(8,128)(2,1)S(1)}, u32[]{:S(2)}, u32[]{:S(2)}) collective-permute-start(bf16[17,48,384]{2,1,0:T(8,128)(2,1)S(1)} %get-tuple-element.105), channel_id=1, source_target_pairs={{0,224},{32,64},{64,32},{96,128},{128,96},{160,192},{192,160},{224... | collective-permute-start | bytes 1880072 | tf_op jit(solution)/shard_map/ppermute | solution.py:29
  79.2 19.4 %collective-permute-start.20 = (bf16[784,384]{1,0:T(8,128)(2,1)S(1)}, bf16[784,384]{1,0:T(8,128)(2,1)S(1)}, u32[]{:S(2)}, u32[]{:S(2)}) collective-permute-start(bf16[784,384]{1,0:T(8,128)(2,1)S(1)} %get-tuple-element.116), channel_id=1, source_target_pairs={{0,2},{1,3},{2,0},{3,1},{4,6},{5,7},{6,4},{7,5},{8,10},{9,11},{10,... | collective-permute-start | bytes 1806344 | tf_op jit(solution)/shard_map/ppermute | solution.py:19
  80.7 13.7 %collective-permute-start.11 = (bf16[16,48,384]{2,1,0:T(8,128)(2,1)S(1)}, bf16[16,48,384]{2,1,0:T(8,128)(2,1)S(1)}, u32[]{:S(2)}, u32[]{:S(2)}) collective-permute-start(bf16[16,48,384]{2,1,0:T(8,128)(2,1)S(1)} %get-tuple-element.95), channel_id=1, source_target_pairs={{0,32},{32,0},{64,96},{96,64},{128,160},{160,128},{192,224},{224,1... | collective-permute-start | bytes 1769480 | tf_op jit(solution)/shard_map/ppermute | solution.py:24
  80.7 37.3 %collective-permute-start.22 = (bf16[784,384]{1,0:T(8,128)(2,1)S(1)}, bf16[784,384]{1,0:T(8,128)(2,1)S(1)}, u32[]{:S(2)}, u32[]{:S(2)}) collective-permute-start(bf16[784,384]{1,0:T(8,128)(2,1)S(1)} %get-tuple-element.121), channel_id=1, source_target_pairs={{0,1},{1,2},{2,3},{3,0},{4,5},{5,6},{6,7},{7,4},{8,9},{9,10},{10,1... | collective-permute-start | bytes 1806344 | tf_op jit(solution)/shard_map/ppermute | solution.py:19
  81.6 36.5 %collective-permute-start.23 = (bf16[784,384]{1,0:T(8,128)(2,1)S(1)}, bf16[784,384]{1,0:T(8,128)(2,1)S(1)}, u32[]{:S(2)}, u32[]{:S(2)}) collective-permute-start(bf16[784,384]{1,0:T(8,128)(2,1)S(1)} %get-tuple-element.123), channel_id=1, source_target_pairs={{0,3},{1,0},{2,1},{3,2},{4,7},{5,4},{6,5},{7,6},{8,11},{9,8},{10,9... | collective-permute-start | bytes 1806344 | tf_op jit(solution)/shard_map/ppermute | solution.py:19
  95.4 14.1 %collective-permute-start.19 = (bf16[400,384]{1,0:T(8,128)(2,1)S(1)}, bf16[400,384]{1,0:T(8,128)(2,1)S(1)}, u32[]{:S(2)}, u32[]{:S(2)}) collective-permute-start(bf16[400,384]{1,0:T(8,128)(2,1)S(1)} %get-tuple-element.115), channel_id=1, source_target_pairs={{0,24},{8,0},{16,8},{24,16},{1,25},{9,1},{17,9},{25,17},{2,26},{10... | collective-permute-start | bytes 921608 | tf_op jit(solution)/shard_map/ppermute | solution.py:19
  98.7 14.2 %collective-permute-start.17 = (bf16[400,384]{1,0:T(8,128)(2,1)S(1)}, bf16[400,384]{1,0:T(8,128)(2,1)S(1)}, u32[]{:S(2)}, u32[]{:S(2)}) collective-permute-start(bf16[400,384]{1,0:T(8,128)(2,1)S(1)} %get-tuple-element.113), channel_id=1, source_target_pairs={{0,8},{8,16},{16,24},{24,0},{1,9},{9,17},{17,25},{25,1},{2,10},{10... | collective-permute-start | bytes 921608 | tf_op jit(solution)/shard_map/ppermute | solution.py:19
  98.7 14.2 %collective-permute-start.18 = (bf16[400,384]{1,0:T(8,128)(2,1)S(1)}, bf16[400,384]{1,0:T(8,128)(2,1)S(1)}, u32[]{:S(2)}, u32[]{:S(2)}) collective-permute-start(bf16[400,384]{1,0:T(8,128)(2,1)S(1)} %get-tuple-element.114), channel_id=1, source_target_pairs={{0,16},{8,24},{16,0},{24,8},{1,17},{9,25},{17,1},{25,9},{2,18},{10... | collective-permute-start | bytes 921608 | tf_op jit(solution)/shard_map/ppermute | solution.py:19
  113.6 7.8 %collective-permute-start.21 = (bf16[112,384]{1,0:T(8,128)(2,1)S(1)}, bf16[112,384]{1,0:T(8,128)(2,1)S(1)}, u32[]{:S(2)}, u32[]{:S(2)}) collective-permute-start(bf16[112,384]{1,0:T(8,128)(2,1)S(1)} %get-tuple-element.119), channel_id=1, source_target_pairs={{0,192},{32,224},{64,0},{96,32},{128,64},{160,96},{192,128},{224,1... | collective-permute-start | bytes 258056 | tf_op jit(solution)/shard_map/ppermute | solution.py:19
  113.7 7.7 %collective-permute-start.24 = (bf16[112,384]{1,0:T(8,128)(2,1)S(1)}, bf16[112,384]{1,0:T(8,128)(2,1)S(1)}, u32[]{:S(2)}, u32[]{:S(2)}) collective-permute-start(bf16[112,384]{1,0:T(8,128)(2,1)S(1)} %get-tuple-element.128), channel_id=1, source_target_pairs={{0,64},{32,96},{64,128},{96,160},{128,192},{160,224},{192,0},{224,... | collective-permute-start | bytes 258056 | tf_op jit(solution)/shard_map/ppermute | solution.py:19
  117.8 9.3 %collective-permute-start.25 = (bf16[112,384]{1,0:T(8,128)(2,1)S(1)}, bf16[112,384]{1,0:T(8,128)(2,1)S(1)}, u32[]{:S(2)}, u32[]{:S(2)}) collective-permute-start(bf16[112,384]{1,0:T(8,128)(2,1)S(1)} %get-tuple-element.129), channel_id=1, source_target_pairs={{0,128},{32,160},{64,192},{96,224},{128,0},{160,32},{192,64},{224,... | collective-permute-start | bytes 258056 | tf_op jit(solution)/shard_map/ppermute | solution.py:19
  (8 other events, 55.9 us)

commit v4 on v2

--- a/solution.py
+++ b/solution.py
@@ -396,7 +396,10 @@
     for kind in range(3):
         qkv_weight[kind] = total[24 * (kind + 1) : 24 * (kind + 2)]
     near = from_two(in_two(gain_part[...])) + from_two(r2[96:, :])
-    gain_sum[...] = (near + (from_two(r1[96:, :]) + from_two(r3[96:, :])))[:4]
+    total = near + (from_two(r1[96:, :]) + from_two(r3[96:, :]))
+    width = total.shape[1]
+    for block in range(4):
+        gain_sum[:, width * block : width * (block + 1)] = total[block : block + 1, :]
 
 
 def per_device(tokens, ln_gain, w_qkv, w_out, frame_mask, out_grad):
@@ -513,6 +516,7 @@
         vmem=16,
     )
     received = [shifted(part, "x", by + 1) for by, part in enumerate(parts)]
+    received[2], exchanged[1] = lax.optimization_barrier((received[2], exchanged[1]))
     own, *parts, gain_part = call(
         x_sum_kernel,
         [((96, width), F32)] + [((112, width), BF16)] * 3 + [small],
@@ -534,7 +538,7 @@
     )
     out_weight_grad, qkv_grad, gain_grad = call(
         far_sum_kernel,
-        [((24, width), F32), ((3, 24, width), F32), ((4, width), F32)],
+        [((24, width), F32), ((3, 24, width), F32), ((1, 4 * width), F32)],
         (own, *received, gain_part),
         vmem=16,
     )

time: 131 us -> 133 us (1.015); the launches traced: 128 us -> 132 us
  starting transfers between devices: 58.4 us -> 67.8 us
  waiting for transfers between devices: 37.1 us -> 31.6 us
    ppermute x18, starting transfers between devices: 36.3 us -> 45.8 us  [shifted(): lax.ppermute(value, axis, [(i, (i + by) % size) for i in range(size)])]
    ppermute x3, waiting for transfers between devices: 11.7 us -> 7.91 us  [swapped(): return lax.ppermute(value, axis, [(i, i ^ bit) for i in range(size)])]
    ppermute x18, waiting for transfers between devices: 20 us -> 18.3 us  [shifted(): lax.ppermute(value, axis, [(i, (i + by) % size) for i in range(size)])]
  transfers between devices with their start and end apart: 26 -> 26, of which waited for: 14 -> 12; matrix products, arithmetic and copies ran while one was open for 1% -> 1% of each run, Pallas kernels for 10% -> 10%
where the time goes in v4:
time: 133 us; the launch traced here: 132 us
  starting transfers between devices  67.8 us (51%)
  waiting for transfers between devices  31.6 us (24%)
  Pallas kernels  26.5 us (20%)
  local copies, waits for them, and re-layouts  4.67 us (4%)
    ppermute x18, starting transfers between devices, shifted(): lax.ppermute(value, axis, [(i, (i + by) % size) for i in range(size)])  45.8 us
    pallas_call x16, Pallas kernels, call(): pl.pallas_call(body, out_shape=[jax.ShapeDtypeStruct(s, d) for s, d in ou...  26.5 us
    ppermute x18, waiting for transfers between devices, shifted(): lax.ppermute(value, axis, [(i, (i + by) % size) for i in range(size)])  18.3 us
    ppermute x3, starting transfers between devices, swapped(): return lax.ppermute(value, axis, [(i, i ^ bit) for i in range(size)])  10.7 us
    ppermute x3, waiting for transfers between devices, swapped(): return lax.ppermute(value, axis, [(i, i ^ bit) for i in range(size)])  7.91 us
    ppermute x2, starting transfers between devices, to_previous(): return lax.ppermute(value, TM, [(i + 1, i) for i in range(size - 1)])  7.45 us
    ppermute x2, starting transfers between devices, to_next(): return lax.ppermute(value, TM, [(i, i + 1) for i in range(size - 1)])  3.84 us
    ppermute x2, waiting for transfers between devices, to_previous(): return lax.ppermute(value, TM, [(i + 1, i) for i in range(size - 1)])  3.51 us
  transfers between devices with their start and end apart: 26, of which 12 were waited for; matrix products, arithmetic and copies ran while one was open for 1% of the time, Pallas kernels for 10%

profile of v4, /device:TPU:6, one launch (start us, length us, event | category | flops | bytes accessed | tf_op | source)
XLA Modules:
  0.0 132.2 jit_solution(17442205111319437716)
XLA Ops:
  3.9 2.0 %collective-permute-start.1 = (bf16[384,384]{1,0:T(8,128)(2,1)}, bf16[384,384]{1,0:T(8,128)(2,1)S(1)}, u32[]{:S(2)}, u32[]{:S(2)}) collective-permute-start(bf16[384,384]{1,0:T(8,128)(2,1)} %tokens.5), channel_id=1, source_target_pairs={{0,2},{1,3},{2,0},{3,1},{4,6},{5,7},{6,4},{7,5},{8,10},{9,11},{10,... | collective-permute-start | bytes 884744 | tf_op jit(solution)/shard_map/ppermute | solution.py:19
  7.3 2.0 %copy-done = bf16[1536,3,384]{2,0,1:T(8,128)(2,1)S(1)} copy-done((bf16[1536,3,384]{2,0,1:T(8,128)(2,1)S(1)}, bf16[1536,3,384]{2,0,1:T(8,128)(2,1)}, u32[]{:S(2)}) %copy-start) | copy-done | bytes 3538968
  11.2 2.6 %collective-permute-start.5 = (bf16[384,384]{1,0:T(8,128)(2,1)S(1)}, bf16[384,384]{1,0:T(8,128)(2,1)S(1)}, u32[]{:S(2)}, u32[]{:S(2)}) collective-permute-start(bf16[384,384]{1,0:T(8,128)(2,1)S(1)} %copy-done.5), channel_id=1, source_target_pairs={{0,3},{1,0},{2,1},{3,2},{4,7},{5,4},{6,5},{7,6},{8,11},{9,8},{10,9... | collective-permute-start | bytes 884744 | tf_op jit(solution)/shard_map/ppermute | solution.py:19
  13.8 8.5 %collective-permute-start.6 = (bf16[384,384]{1,0:T(8,128)(2,1)S(1)}, bf16[384,384]{1,0:T(8,128)(2,1)S(1)}, u32[]{:S(2)}, u32[]{:S(2)}) collective-permute-start(bf16[384,384]{1,0:T(8,128)(2,1)S(1)} %copy-done.5), channel_id=1, source_target_pairs={{0,2},{1,3},{2,0},{3,1},{4,6},{5,7},{6,4},{7,5},{8,10},{9,11},{10,... | collective-permute-start | bytes 884744 | tf_op jit(solution)/shard_map/ppermute | solution.py:19
  23.8 3.6 %shard_map.102 = (bf16[4,384,384]{2,1,0:T(8,128)(2,1)S(1)}, bf16[384,384]{1,0:T(8,128)(2,1)S(1)}, bf16[384,384]{1,0:T(8,128)(2,1)S(1)}, bf16[384,384]{1,0:T(8,12...) custom-call(s32[4]{0:T(128)S(1)} %pad_add_fusion.place, ...), custom_call_target="tpu_custom_call" | custom-call | flops 1358954496 | tf_op jit(solution)/shard_map/pallas_call | solution.py:61
  29.4 3.8 %collective-permute-start.4 = (bf16[144,768]{1,0:T(8,128)(2,1)S(1)}, bf16[144,768]{1,0:T(8,128)(2,1)S(1)}, u32[]{:S(2)}, u32[]{:S(2)}) collective-permute-start(bf16[144,768]{1,0:T(8,128)(2,1)S(1)} %get-tuple-element.77), channel_id=1, source_target_pairs={{4,0},{8,4},{12,8},{16,12},{20,16},{24,20},{28,24},{32,28},{36,32}... | collective-permute-start | bytes 663560 | tf_op jit(solution)/shard_map/ppermute | solution.py:39
  36.5 6.4 %shard_map.103 = (bf16[384,384]{1,0:T(8,128)(2,1)S(1)}, bf16[384,384]{1,0:T(8,128)(2,1)S(1)}, f32[384,768]{1,0:T(8,128)S(1)}, bf16[128,768]{1,0:T(8,128)(2,1)S(1...) custom-call(s32[4]{0:T(128)S(1)} %pad_add_fusion.place, s32[1,384]{1,0:T(1,128)S(1)} %broadcast_in_dim.3.mask, ...), custom_call_target="tpu_custom_call" | custom-call | tf_op jit(solution)/shard_map/pallas_call | solution.py:61
  42.9 2.4 %shard_map.104 = (bf16[32,48,384]{2,1,0:T(8,128)(2,1)S(1)}, bf16[32,48,384]{2,1,0:T(8,128)(2,1)S(1)}, f32[4,384,128]{2,1,0:T(8,128)S(1)}) custom-call(s32[4]{0:T(128)S(1)} %pad_add_fusion.place, bf16[4,384,384]{2,1,0:T(8,128)(2,1)S(1)} %get-tuple-element.79.gated, bf16[384,384]{1,0:T(8,128)(2,1)S(1)} %get-tuple-element.80.attended, ...), custom_call_target="tpu_custom_call" | custom-call | flops 1358954496 | tf_op jit(solution)/shard_map/pallas_call | solution.py:61
  45.3 4.3 %collective-permute-start.10 = (bf16[32,48,384]{2,1,0:T(8,128)(2,1)S(1)}, bf16[32,48,384]{2,1,0:T(8,128)(2,1)S(1)}, u32[]{:S(2)}, u32[]{:S(2)}) collective-permute-start(bf16[32,48,384]{2,1,0:T(8,128)(2,1)S(1)} %get-tuple-element.86), channel_id=1, source_target_pairs={{0,4},{4,0},{1,5},{5,1},{2,6},{6,2},{3,7},{7,3},{8,12},{12,8},{9,1... | collective-permute-start | bytes 3538952 | tf_op jit(solution)/shard_map/ppermute | solution.py:24
  49.6 1.9 %collective-permute-start.8 = (bf16[128,768]{1,0:T(8,128)(2,1)S(1)}, bf16[128,768]{1,0:T(8,128)(2,1)S(1)}, u32[]{:S(2)}, u32[]{:S(2)}) collective-permute-start(bf16[128,768]{1,0:T(8,128)(2,1)S(1)} %get-tuple-element.84), channel_id=1, source_target_pairs={{0,4},{4,8},{8,12},{12,16},{16,20},{20,24},{24,28},{28,32},{32,36}... | collective-permute-start | bytes 589832 | tf_op jit(solution)/shard_map/ppermute | solution.py:34
  51.5 3.6 %collective-permute-start.9 = (bf16[128,768]{1,0:T(8,128)(2,1)S(1)}, bf16[128,768]{1,0:T(8,128)(2,1)S(1)}, u32[]{:S(2)}, u32[]{:S(2)}) collective-permute-start(bf16[128,768]{1,0:T(8,128)(2,1)S(1)} %get-tuple-element.85), channel_id=1, source_target_pairs={{4,0},{8,4},{12,8},{16,12},{20,16},{24,20},{28,24},{32,28},{36,32}... | collective-permute-start | bytes 589832 | tf_op jit(solution)/shard_map/ppermute | solution.py:39
  58.3 2.8 %shard_map.107 = (bf16[33,48,384]{2,1,0:T(8,128)(2,1)S(1)}, bf16[32,48,384]{2,1,0:T(8,128)(2,1)S(1)}, bf16[384,384]{1,0:T(8,128)(2,1)S(1)}, bf16[384,384]{1,0:T(8,128)(2,1)S(1)}, f32[8,384]{1,0:T(8,128)S(1)}) custom-call(s32[4]{0:T(128)S(1)} %pad_add_fusion.place, f32[384,768]{1,0:T(8,128)S(1)} %get-tuple-element.89.kv_grad, ...), custom_call_target="tpu_custom_call" | custom-call | tf_op jit(solution)/shard_map/pallas_call | solution.py:61
  61.1 2.6 %collective-permute-start.12 = (bf16[33,48,384]{2,1,0:T(8,128)(2,1)S(1)}, bf16[33,48,384]{2,1,0:T(8,128)(2,1)S(1)}, u32[]{:S(2)}, u32[]{:S(2)}) collective-permute-start(bf16[33,48,384]{2,1,0:T(8,128)(2,1)S(1)} %get-tuple-element.97), channel_id=1, source_target_pairs={{0,4},{4,0},{1,5},{5,1},{2,6},{6,2},{3,7},{7,3},{8,12},{12,8},{9,1... | collective-permute-start | bytes 3649544 | tf_op jit(solution)/shard_map/ppermute | solution.py:24
  64.6 3.2 %shard_map.109 = (bf16[784,384]{1,0:T(8,128)(2,1)S(1)}, bf16[784,384]{1,0:T(8,128)(2,1)S(1)}, bf16[784,384]{1,0:T(8,128)(2,1)S(1)}, bf16[784,384]{1,0:T(8,128)(2,1)S(1)}) custom-call(s32[4]{0:T(128)S(1)} %pad_add_fusion.place, bf16[4,384,384]{2,1,0:T(8,128)(2,1)S(1)} %shard_map.105.branches, bf16[384,384]{1,0:T(8,128)(2,1)S(1)} %get-tuple-element.81.q_grad, ...), custom_call_target="tpu_custom_call" | custom-call | tf_op jit(solution)/shard_map/pallas_call | solution.py:61
  67.9 3.3 %collective-permute-start.14 = (f32[8,384]{1,0:T(8,128)S(1)}, f32[8,384]{1,0:T(8,128)S(1)}, u32[]{:S(2)}, u32[]{:S(2)}) collective-permute-start(f32[8,384]{1,0:T(8,128)S(1)} %shard_map.110.g0), channel_id=1, source_target_pairs={{0,2},{1,3},{2,0},{3,1},{4,6},{5,7},{6,4},{7,5},{8,10},{9,11},{10,... | collective-permute-start | bytes 36872 | tf_op jit(solution)/shard_map/ppermute | solution.py:19
  76.7 3.7 %collective-permute-start.11 = (bf16[16,48,384]{2,1,0:T(8,128)(2,1)S(1)}, bf16[16,48,384]{2,1,0:T(8,128)(2,1)S(1)}, u32[]{:S(2)}, u32[]{:S(2)}) collective-permute-start(bf16[16,48,384]{2,1,0:T(8,128)(2,1)S(1)} %get-tuple-element.95), channel_id=1, source_target_pairs={{0,32},{32,0},{64,96},{96,64},{128,160},{160,128},{192,224},{224,1... | collective-permute-start | bytes 1769480 | tf_op jit(solution)/shard_map/ppermute | solution.py:24
  80.4 2.1 %collective-permute-start.22 = (bf16[784,384]{1,0:T(8,128)(2,1)S(1)}, bf16[784,384]{1,0:T(8,128)(2,1)S(1)}, u32[]{:S(2)}, u32[]{:S(2)}) collective-permute-start(bf16[784,384]{1,0:T(8,128)(2,1)S(1)} %get-tuple-element.122), channel_id=1, source_target_pairs={{0,2},{1,3},{2,0},{3,1},{4,6},{5,7},{6,4},{7,5},{8,10},{9,11},{10,... | collective-permute-start | bytes 1806344 | tf_op jit(solution)/shard_map/ppermute | solution.py:19
  83.7 7.9 %collective-permute-done.11.received = bf16[16,48,384]{2,1,0:T(8,128)(2,1)S(1)} collective-permute-done((bf16[16,48,384]{2,1,0:T(8,128)(2,1)S(1)}, bf16[16,48,384]{2,1,0:T(8,128)(2,1)S(1)}, u32[]{:S(2)}, u32[]{:S(2)}) %collective-permute-start.11) | collective-permute-done | bytes 589856 | tf_op jit(solution)/shard_map/ppermute | solution.py:24
  92.7 3.2 %collective-permute-start.17 = (bf16[400,384]{1,0:T(8,128)(2,1)S(1)}, bf16[400,384]{1,0:T(8,128)(2,1)S(1)}, u32[]{:S(2)}, u32[]{:S(2)}) collective-permute-start(bf16[400,384]{1,0:T(8,128)(2,1)S(1)} %get-tuple-element.113), channel_id=1, source_target_pairs={{0,8},{8,16},{16,24},{24,0},{1,9},{9,17},{17,25},{25,1},{2,10},{10... | collective-permute-start | bytes 921608 | tf_op jit(solution)/shard_map/ppermute | solution.py:19
  95.8 8.1 %collective-permute-done.20.n1 = bf16[784,384]{1,0:T(8,128)(2,1)S(1)} collective-permute-done((bf16[784,384]{1,0:T(8,128)(2,1)S(1)}, bf16[784,384]{1,0:T(8,128)(2,1)S(1)}, u32[]{:S(2)}, u32[]{:S(2)}) %collective-permute-start.20) | collective-permute-done | bytes 602144 | tf_op jit(solution)/shard_map/ppermute | solution.py:19
  103.9 3.6 %collective-permute-start.18 = (bf16[400,384]{1,0:T(8,128)(2,1)S(1)}, bf16[400,384]{1,0:T(8,128)(2,1)S(1)}, u32[]{:S(2)}, u32[]{:S(2)}) collective-permute-start(bf16[400,384]{1,0:T(8,128)(2,1)S(1)} %get-tuple-element.114), channel_id=1, source_target_pairs={{0,16},{8,24},{16,0},{24,8},{1,17},{9,25},{17,1},{25,9},{2,18},{10... | collective-permute-start | bytes 921608 | tf_op jit(solution)/shard_map/ppermute | solution.py:19
  107.5 4.8 %collective-permute-done.18.r2 = bf16[400,384]{1,0:T(8,128)(2,1)S(1)} collective-permute-done((bf16[400,384]{1,0:T(8,128)(2,1)S(1)}, bf16[400,384]{1,0:T(8,128)(2,1)S(1)}, u32[]{:S(2)}, u32[]{:S(2)}) %collective-permute-start.18) | collective-permute-done | bytes 307232 | tf_op jit(solution)/shard_map/ppermute | solution.py:19
  113.1 6.0 %collective-permute-start.21 = (bf16[112,384]{1,0:T(8,128)(2,1)S(1)}, bf16[112,384]{1,0:T(8,128)(2,1)S(1)}, u32[]{:S(2)}, u32[]{:S(2)}) collective-permute-start(bf16[112,384]{1,0:T(8,128)(2,1)S(1)} %get-tuple-element.119), channel_id=1, source_target_pairs={{0,192},{32,224},{64,0},{96,32},{128,64},{160,96},{192,128},{224,1... | collective-permute-start | bytes 258056 | tf_op jit(solution)/shard_map/ppermute | solution.py:19
  119.1 7.5 %collective-permute-start.25 = (bf16[112,384]{1,0:T(8,128)(2,1)S(1)}, bf16[112,384]{1,0:T(8,128)(2,1)S(1)}, u32[]{:S(2)}, u32[]{:S(2)}) collective-permute-start(bf16[112,384]{1,0:T(8,128)(2,1)S(1)} %get-tuple-element.129), channel_id=1, source_target_pairs={{0,128},{32,160},{64,192},{96,224},{128,0},{160,32},{192,64},{224,... | collective-permute-start | bytes 258056 | tf_op jit(solution)/shard_map/ppermute | solution.py:19
  (60 shorter events, 31.4 us)
Async XLA Ops:
  0.6 10.3 %collective-permute-start.2 = (bf16[384,384]{1,0:T(8,128)(2,1)}, bf16[384,384]{1,0:T(8,128)(2,1)S(1)}, u32[]{:S(2)}, u32[]{:S(2)}) collective-permute-start(bf16[384,384]{1,0:T(8,128)(2,1)} %tokens.5), channel_id=1, source_target_pairs={{0,1},{1,2},{2,3},{3,0},{4,5},{5,6},{6,7},{7,4},{8,9},{9,10},{10,1... | collective-permute-start | bytes 884744 | tf_op jit(solution)/shard_map/ppermute | solution.py:19
  2.3 21.5 %collective-permute-start = (bf16[384,384]{1,0:T(8,128)(2,1)}, bf16[384,384]{1,0:T(8,128)(2,1)S(1)}, u32[]{:S(2)}, u32[]{:S(2)}) collective-permute-start(bf16[384,384]{1,0:T(8,128)(2,1)} %tokens.5), channel_id=1, source_target_pairs={{0,3},{1,0},{2,1},{3,2},{4,7},{5,4},{6,5},{7,6},{8,11},{9,8},{10,9... | collective-permute-start | bytes 884744 | tf_op jit(solution)/shard_map/ppermute | solution.py:19
  3.9 19.8 %collective-permute-start.1 = (bf16[384,384]{1,0:T(8,128)(2,1)}, bf16[384,384]{1,0:T(8,128)(2,1)S(1)}, u32[]{:S(2)}, u32[]{:S(2)}) collective-permute-start(bf16[384,384]{1,0:T(8,128)(2,1)} %tokens.5), channel_id=1, source_target_pairs={{0,2},{1,3},{2,0},{3,1},{4,6},{5,7},{6,4},{7,5},{8,10},{9,11},{10,... | collective-permute-start | bytes 884744 | tf_op jit(solution)/shard_map/ppermute | solution.py:19
  11.2 25.2 %collective-permute-start.5 = (bf16[384,384]{1,0:T(8,128)(2,1)S(1)}, bf16[384,384]{1,0:T(8,128)(2,1)S(1)}, u32[]{:S(2)}, u32[]{:S(2)}) collective-permute-start(bf16[384,384]{1,0:T(8,128)(2,1)S(1)} %copy-done.5), channel_id=1, source_target_pairs={{0,3},{1,0},{2,1},{3,2},{4,7},{5,4},{6,5},{7,6},{8,11},{9,8},{10,9... | collective-permute-start | bytes 884744 | tf_op jit(solution)/shard_map/ppermute | solution.py:19
  13.8 22.6 %collective-permute-start.6 = (bf16[384,384]{1,0:T(8,128)(2,1)S(1)}, bf16[384,384]{1,0:T(8,128)(2,1)S(1)}, u32[]{:S(2)}, u32[]{:S(2)}) collective-permute-start(bf16[384,384]{1,0:T(8,128)(2,1)S(1)} %copy-done.5), channel_id=1, source_target_pairs={{0,2},{1,3},{2,0},{3,1},{4,6},{5,7},{6,4},{7,5},{8,10},{9,11},{10,... | collective-permute-start | bytes 884744 | tf_op jit(solution)/shard_map/ppermute | solution.py:19
  22.3 14.1 %collective-permute-start.7 = (bf16[384,384]{1,0:T(8,128)(2,1)S(1)}, bf16[384,384]{1,0:T(8,128)(2,1)S(1)}, u32[]{:S(2)}, u32[]{:S(2)}) collective-permute-start(bf16[384,384]{1,0:T(8,128)(2,1)S(1)} %copy-done.5), channel_id=1, source_target_pairs={{0,1},{1,2},{2,3},{3,0},{4,5},{5,6},{6,7},{7,4},{8,9},{9,10},{10,1... | collective-permute-start | bytes 884744 | tf_op jit(solution)/shard_map/ppermute | solution.py:19
  27.4 7.3 %collective-permute-start.3 = (bf16[144,768]{1,0:T(8,128)(2,1)S(1)}, bf16[144,768]{1,0:T(8,128)(2,1)S(1)}, u32[]{:S(2)}, u32[]{:S(2)}) collective-permute-start(bf16[144,768]{1,0:T(8,128)(2,1)S(1)} %get-tuple-element.76), channel_id=1, source_target_pairs={{0,4},{4,8},{8,12},{12,16},{16,20},{20,24},{24,28},{28,32},{32,36}... | collective-permute-start | bytes 663560 | tf_op jit(solution)/shard_map/ppermute | solution.py:34
  29.4 7.1 %collective-permute-start.4 = (bf16[144,768]{1,0:T(8,128)(2,1)S(1)}, bf16[144,768]{1,0:T(8,128)(2,1)S(1)}, u32[]{:S(2)}, u32[]{:S(2)}) collective-permute-start(bf16[144,768]{1,0:T(8,128)(2,1)S(1)} %get-tuple-element.77), channel_id=1, source_target_pairs={{4,0},{8,4},{12,8},{16,12},{20,16},{24,20},{28,24},{32,28},{36,32}... | collective-permute-start | bytes 663560 | tf_op jit(solution)/shard_map/ppermute | solution.py:39
  45.3 13.0 %collective-permute-start.10 = (bf16[32,48,384]{2,1,0:T(8,128)(2,1)S(1)}, bf16[32,48,384]{2,1,0:T(8,128)(2,1)S(1)}, u32[]{:S(2)}, u32[]{:S(2)}) collective-permute-start(bf16[32,48,384]{2,1,0:T(8,128)(2,1)S(1)} %get-tuple-element.86), channel_id=1, source_target_pairs={{0,4},{4,0},{1,5},{5,1},{2,6},{6,2},{3,7},{7,3},{8,12},{12,8},{9,1... | collective-permute-start | bytes 3538952 | tf_op jit(solution)/shard_map/ppermute | solution.py:24
  49.6 7.0 %collective-permute-start.8 = (bf16[128,768]{1,0:T(8,128)(2,1)S(1)}, bf16[128,768]{1,0:T(8,128)(2,1)S(1)}, u32[]{:S(2)}, u32[]{:S(2)}) collective-permute-start(bf16[128,768]{1,0:T(8,128)(2,1)S(1)} %get-tuple-element.84), channel_id=1, source_target_pairs={{0,4},{4,8},{8,12},{12,16},{16,20},{20,24},{24,28},{28,32},{32,36}... | collective-permute-start | bytes 589832 | tf_op jit(solution)/shard_map/ppermute | solution.py:34
  51.5 6.8 %collective-permute-start.9 = (bf16[128,768]{1,0:T(8,128)(2,1)S(1)}, bf16[128,768]{1,0:T(8,128)(2,1)S(1)}, u32[]{:S(2)}, u32[]{:S(2)}) collective-permute-start(bf16[128,768]{1,0:T(8,128)(2,1)S(1)} %get-tuple-element.85), channel_id=1, source_target_pairs={{4,0},{8,4},{12,8},{16,12},{20,16},{24,20},{28,24},{32,28},{36,32}... | collective-permute-start | bytes 589832 | tf_op jit(solution)/shard_map/ppermute | solution.py:39
  61.1 6.6 %collective-permute-start.12 = (bf16[33,48,384]{2,1,0:T(8,128)(2,1)S(1)}, bf16[33,48,384]{2,1,0:T(8,128)(2,1)S(1)}, u32[]{:S(2)}, u32[]{:S(2)}) collective-permute-start(bf16[33,48,384]{2,1,0:T(8,128)(2,1)S(1)} %get-tuple-element.97), channel_id=1, source_target_pairs={{0,4},{4,0},{1,5},{5,1},{2,6},{6,2},{3,7},{7,3},{8,12},{12,8},{9,1... | collective-permute-start | bytes 3649544 | tf_op jit(solution)/shard_map/ppermute | solution.py:24
  67.9 5.3 %collective-permute-start.14 = (f32[8,384]{1,0:T(8,128)S(1)}, f32[8,384]{1,0:T(8,128)S(1)}, u32[]{:S(2)}, u32[]{:S(2)}) collective-permute-start(f32[8,384]{1,0:T(8,128)S(1)} %shard_map.110.g0), channel_id=1, source_target_pairs={{0,2},{1,3},{2,0},{3,1},{4,6},{5,7},{6,4},{7,5},{8,10},{9,11},{10,... | collective-permute-start | bytes 36872 | tf_op jit(solution)/shard_map/ppermute | solution.py:19
  75.7 16.1 %collective-permute-start.16 = (bf16[17,48,384]{2,1,0:T(8,128)(2,1)S(1)}, bf16[17,48,384]{2,1,0:T(8,128)(2,1)S(1)}, u32[]{:S(2)}, u32[]{:S(2)}) collective-permute-start(bf16[17,48,384]{2,1,0:T(8,128)(2,1)S(1)} %get-tuple-element.105), channel_id=1, source_target_pairs={{0,224},{32,64},{64,32},{96,128},{128,96},{160,192},{192,160},{224... | collective-permute-start | bytes 1880072 | tf_op jit(solution)/shard_map/ppermute | solution.py:29
  75.8 28.1 %collective-permute-start.20 = (bf16[784,384]{1,0:T(8,128)(2,1)S(1)}, bf16[784,384]{1,0:T(8,128)(2,1)S(1)}, u32[]{:S(2)}, u32[]{:S(2)}) collective-permute-start(bf16[784,384]{1,0:T(8,128)(2,1)S(1)} %get-tuple-element.116), channel_id=1, source_target_pairs={{0,1},{1,2},{2,3},{3,0},{4,5},{5,6},{6,7},{7,4},{8,9},{9,10},{10,1... | collective-permute-start | bytes 1806344 | tf_op jit(solution)/shard_map/ppermute | solution.py:19
  76.7 15.0 %collective-permute-start.11 = (bf16[16,48,384]{2,1,0:T(8,128)(2,1)S(1)}, bf16[16,48,384]{2,1,0:T(8,128)(2,1)S(1)}, u32[]{:S(2)}, u32[]{:S(2)}) collective-permute-start(bf16[16,48,384]{2,1,0:T(8,128)(2,1)S(1)} %get-tuple-element.95), channel_id=1, source_target_pairs={{0,32},{32,0},{64,96},{96,64},{128,160},{160,128},{192,224},{224,1... | collective-permute-start | bytes 1769480 | tf_op jit(solution)/shard_map/ppermute | solution.py:24
  80.4 46.1 %collective-permute-start.22 = (bf16[784,384]{1,0:T(8,128)(2,1)S(1)}, bf16[784,384]{1,0:T(8,128)(2,1)S(1)}, u32[]{:S(2)}, u32[]{:S(2)}) collective-permute-start(bf16[784,384]{1,0:T(8,128)(2,1)S(1)} %get-tuple-element.122), channel_id=1, source_target_pairs={{0,2},{1,3},{2,0},{3,1},{4,6},{5,7},{6,4},{7,5},{8,10},{9,11},{10,... | collective-permute-start | bytes 1806344 | tf_op jit(solution)/shard_map/ppermute | solution.py:19
  82.5 44.0 %collective-permute-start.23 = (bf16[784,384]{1,0:T(8,128)(2,1)S(1)}, bf16[784,384]{1,0:T(8,128)(2,1)S(1)}, u32[]{:S(2)}, u32[]{:S(2)}) collective-permute-start(bf16[784,384]{1,0:T(8,128)(2,1)S(1)} %get-tuple-element.123), channel_id=1, source_target_pairs={{0,3},{1,0},{2,1},{3,2},{4,7},{5,4},{6,5},{7,6},{8,11},{9,8},{10,9... | collective-permute-start | bytes 1806344 | tf_op jit(solution)/shard_map/ppermute | solution.py:19
  92.5 15.0 %collective-permute-start.19 = (bf16[400,384]{1,0:T(8,128)(2,1)S(1)}, bf16[400,384]{1,0:T(8,128)(2,1)S(1)}, u32[]{:S(2)}, u32[]{:S(2)}) collective-permute-start(bf16[400,384]{1,0:T(8,128)(2,1)S(1)} %get-tuple-element.115), channel_id=1, source_target_pairs={{0,24},{8,0},{16,8},{24,16},{1,25},{9,1},{17,9},{25,17},{2,26},{10... | collective-permute-start | bytes 921608 | tf_op jit(solution)/shard_map/ppermute | solution.py:19
  92.7 14.9 %collective-permute-start.17 = (bf16[400,384]{1,0:T(8,128)(2,1)S(1)}, bf16[400,384]{1,0:T(8,128)(2,1)S(1)}, u32[]{:S(2)}, u32[]{:S(2)}) collective-permute-start(bf16[400,384]{1,0:T(8,128)(2,1)S(1)} %get-tuple-element.113), channel_id=1, source_target_pairs={{0,8},{8,16},{16,24},{24,0},{1,9},{9,17},{17,25},{25,1},{2,10},{10... | collective-permute-start | bytes 921608 | tf_op jit(solution)/shard_map/ppermute | solution.py:19
  103.9 8.4 %collective-permute-start.18 = (bf16[400,384]{1,0:T(8,128)(2,1)S(1)}, bf16[400,384]{1,0:T(8,128)(2,1)S(1)}, u32[]{:S(2)}, u32[]{:S(2)}) collective-permute-start(bf16[400,384]{1,0:T(8,128)(2,1)S(1)} %get-tuple-element.114), channel_id=1, source_target_pairs={{0,16},{8,24},{16,0},{24,8},{1,17},{9,25},{17,1},{25,9},{2,18},{10... | collective-permute-start | bytes 921608 | tf_op jit(solution)/shard_map/ppermute | solution.py:19
  113.1 16.2 %collective-permute-start.21 = (bf16[112,384]{1,0:T(8,128)(2,1)S(1)}, bf16[112,384]{1,0:T(8,128)(2,1)S(1)}, u32[]{:S(2)}, u32[]{:S(2)}) collective-permute-start(bf16[112,384]{1,0:T(8,128)(2,1)S(1)} %get-tuple-element.119), channel_id=1, source_target_pairs={{0,192},{32,224},{64,0},{96,32},{128,64},{160,96},{192,128},{224,1... | collective-permute-start | bytes 258056 | tf_op jit(solution)/shard_map/ppermute | solution.py:19
  119.1 10.2 %collective-permute-start.24 = (bf16[112,384]{1,0:T(8,128)(2,1)S(1)}, bf16[112,384]{1,0:T(8,128)(2,1)S(1)}, u32[]{:S(2)}, u32[]{:S(2)}) collective-permute-start(bf16[112,384]{1,0:T(8,128)(2,1)S(1)} %get-tuple-element.128), channel_id=1, source_target_pairs={{0,64},{32,96},{64,128},{96,160},{128,192},{160,224},{192,0},{224,... | collective-permute-start | bytes 258056 | tf_op jit(solution)/shard_map/ppermute | solution.py:19
  119.1 11.8 %collective-permute-start.25 = (bf16[112,384]{1,0:T(8,128)(2,1)S(1)}, bf16[112,384]{1,0:T(8,128)(2,1)S(1)}, u32[]{:S(2)}, u32[]{:S(2)}) collective-permute-start(bf16[112,384]{1,0:T(8,128)(2,1)S(1)} %get-tuple-element.129), channel_id=1, source_target_pairs={{0,128},{32,160},{64,192},{96,224},{128,0},{160,32},{192,64},{224,... | collective-permute-start | bytes 258056 | tf_op jit(solution)/shard_map/ppermute | solution.py:19
  (8 other events, 65.8 us)
